TPU v7x, 32 devices: a whole 2x2x4 slice. The times are simulated.
32 devices in a mesh: mpo: 2 (over x), sector: 16 (over z, y, core).
Axes of the slice: x: 2, y: 2, z: 4, core: 2. Of those that a mesh axis runs over, the one named last changes fastest.
Arguments:
- wavefunction: bfloat16 [64, 512, 512], P('sector'), may hold values from -6 to 6
- left_env: bfloat16 [2, 64, 512, 512], P('mpo', 'sector'), may hold values from -0.375 to 0.375
- right_env: bfloat16 [2, 64, 512, 512], P('mpo', 'sector'), may hold values from -0.1875 to 0.1875
- mpo_mask: int32 [2, 64], P('mpo', 'sector'), may hold values 0 or 1
- block_size: int32 [64], P('sector'), may hold values from 64 to 512, as said below
- route_owner: int32 [2, 64, 8], P('mpo', 'sector'), may hold values from 0 to 15, all different within a row; in each aligned block of 4 rows (0 to 3, 4 to 7, ..., all dimensions but the last counted through in order) at most 4 rows name the same one
- route_block: int32 [2, 64, 8], P('mpo', 'sector'), may hold values from 0 to 3
Outputs:
- sigma_right: bfloat16 [64, 512, 512], P('sector', 'mpo')
Inputs may be any that keep to these rules, and one draw needn't show every extreme that they name: `block_size`: some block in every draw has all 512 states live. `route_owner`: each row (m, b) names 8 different owners. Among the 4 rows of one device (one m and the blocks of one sector owner) no owner is named more than 4 times, and in some device's rows some owner is named exactly 4 times; every owner is named somewhere.
All inputs are finite; a program needn't handle non-finite values. No bound on the sum of `mpo_mask` on one device may be relied on, other than what follows from the above.
Results may differ from a plain program's by a relative error of at most 0.014.
Values may be sent and summed in bfloat16 or wider, within the bound.
No kernel may reach another device: no remote copies, remote signals or barrier semaphores. Data moves between devices by JAX's collectives and lax.ppermute only.
A program may use at most 64 MiB of HBM per device.

v0:
```python
import jax
import jax.numpy as jnp
from jax import lax
from jax.sharding import PartitionSpec as P

ROW_GROUPS = 4
COL_PARTS = 2
PIECES = 8


def per_device(wavefunction, left_env, right_env, mpo_mask, block_size, route_owner, route_block):
    block_count = wavefunction.shape[0]
    states = wavefunction.shape[1]
    row_count = states // lax.axis_size("mpo")
    positions = jnp.arange(states, dtype=jnp.int32)
    live_cols = positions[None, :] < block_size[:, None]
    live_mask = live_cols[:, :, None] & live_cols[:, None, :]
    masked = jnp.where(live_mask, wavefunction, jnp.zeros_like(wavefunction))
    right_part = jnp.einsum(
        "bij,bkj->bik", masked, right_env[0], preferred_element_type=jnp.float32
    ).astype(jnp.bfloat16)
    factor = mpo_mask[0].astype(jnp.float32)
    left_rows = left_env[0]
    product = jnp.einsum("bij,bjk->ibk", left_rows, right_part, preferred_element_type=jnp.float32)
    row_share = lax.psum_scatter(
        (product * factor[None, :, None]).astype(jnp.bfloat16),
        "mpo",
        scatter_dimension=0,
        tiled=True,
    ).astype(jnp.float32)
    global_rows = lax.axis_index("mpo") * row_count + jnp.arange(row_count, dtype=jnp.int32)
    live_rows = global_rows[:, None] < block_size[None, :]
    share_mask = live_rows[:, :, None] & live_cols[None, :, :]
    sigma_share = jnp.where(share_mask, row_share, jnp.zeros_like(row_share)).astype(jnp.bfloat16)
    group_rows = row_count // ROW_GROUPS
    width_part = states // COL_PARTS
    pieces = sigma_share.reshape(ROW_GROUPS, group_rows, block_count, COL_PARTS, width_part)
    pieces = pieces.transpose(2, 0, 3, 1, 4).reshape(block_count * PIECES, group_rows * width_part)
    owners = route_owner[0].reshape(-1)
    target_code = (route_block[0] * PIECES + jnp.arange(PIECES, dtype=jnp.int32)[None, :]).reshape(
        -1
    )
    peer_count = lax.axis_size("sector")
    capacity = min(block_count, max(2, (2 * block_count * PIECES + peer_count - 1) // peer_count))
    is_owner = (owners[:, None] == jnp.arange(peer_count, dtype=jnp.int32)[None, :]).astype(
        jnp.int32
    )
    before = jnp.cumsum(is_owner, axis=0) - is_owner
    position = jnp.sum(before * is_owner, axis=1)
    destination = owners * capacity + position
    slot_ids = jnp.arange(peer_count * capacity, dtype=jnp.int32)
    placing = slot_ids[:, None] == destination[None, :]
    send_data = jnp.dot(
        placing.astype(jnp.bfloat16), pieces, preferred_element_type=jnp.float32
    ).astype(jnp.bfloat16)
    send_data = send_data.reshape(peer_count, capacity, group_rows * width_part)
    send_code = (
        jnp.sum(placing.astype(jnp.int32) * (target_code + 1)[None, :], axis=1) - 1
    ).reshape(peer_count, capacity)
    arrived_data, arrived_code = (
        lax.all_to_all(send_data, "sector", split_axis=0, concat_axis=0, tiled=True),
        lax.all_to_all(send_code, "sector", split_axis=0, concat_axis=0, tiled=True),
    )
    arrived_data = arrived_data.reshape(peer_count * capacity, group_rows * width_part)
    arrived_code = arrived_code.reshape(-1)
    targets = jnp.arange(block_count * PIECES, dtype=jnp.int32)
    collect = (arrived_code[None, :] == targets[:, None]).astype(jnp.bfloat16)
    landed = jnp.dot(collect, arrived_data, preferred_element_type=jnp.float32).astype(jnp.bfloat16)
    landed = landed.reshape(block_count, ROW_GROUPS, COL_PARTS, group_rows, width_part)
    return landed.transpose(0, 1, 3, 2, 4).reshape(block_count, row_count, states)


def solution(mesh):
    placed = (
        P("sector", None, None),
        P("mpo", "sector", None, None),
        P("mpo", "sector", None, None),
        P("mpo", "sector"),
        P("sector"),
        P("mpo", "sector", None),
        P("mpo", "sector", None),
    )
    return jax.shard_map(
        per_device, mesh=mesh, in_specs=placed, out_specs=P("sector", "mpo", None), check_vma=False
    )
```

profile of v0, /device:TPU:9, one launch (start us, length us, event | category | flops | bytes accessed | tf_op | source)
XLA Modules:
  0.0 126.7 jit_solution(2985728828479238715)
XLA Ops:
  6.5 0.0 copy-start
  6.5 0.0 reduce-scatter.2.cloned.1.call-start
  6.5 0.8 convert_bitcast_fusion
  7.3 0.7 iota_compare_fusion.5
  8.1 0.1 copy-done
  8.1 6.0 %fusion.6 = bf16[512,4,512]{0,2,1:T(8,128)(2,1)} fusion(f32[4]{0:T(128)S(1)} %convert_bitcast_fusion, bf16[1,4,512,512]{3,2,1,0:T(8,128)(2,1)S(1)} %copy-done, bf16[4,512,512]{2,1,0:T(8,128)(2,1)} %param.7, bf16[1,4,512,512]{3,2,1,0:T(8,128)(2,1)} %param.9, pred[4,512]{1,0:T(4,128)(4,1)S(1)} %iota_compare_fusion.5), kind=kOutput, calls=%fused_computation.11 | convolution fusion | flops 2152726528 | bytes 8390672 | tf_op jit(solution)/shard_map/bij,bjk->ibk/dot_general | solution.py:24
  14.1 0.0 copy-start.2
  14.1 0.0 copy-start.3
  14.1 0.0 copy-start.1
  14.1 0.0 reduce-scatter.2.cloned.1.call-update
  14.1 0.7 copy-done.2
  14.8 0.1 reshape_squeeze.3
  14.9 0.0 copy-done.3
  14.9 0.1 mul.52
  15.0 0.1 add.56
  15.1 0.1 fusion.17
  15.1 0.1 reduce_window_sum.11
  15.2 0.2 select_reduce_fusion.1
  15.4 0.1 select_reduce_fusion
  15.5 0.7 sub.11
  16.2 6.6 %all-to-all-start = ((s32[16,1,4]{2,1,0:T(1,128)}), s32[16,1,4]{2,1,0:T(1,128)S(1)}, u32[]{:S(2)}, u32[]{:S(2)}) async-start(s32[16,1,4]{2,1,0:T(1,128)} %bitcast), calls=%async_computation | async-start | bytes 16384 | tf_op jit(solution)/shard_map/all_to_all | solution.py:62
  22.8 0.0 copy-done.1
  22.8 0.1 broadcast_compare_fusion
  22.9 24.5 %reduce-scatter.2.cloned.1.call-done = bf16[256,4,512]{0,2,1:T(8,128)(2,1)} async-done(((bf16[512,4,512]{0,2,1:T(8,128)(2,1)}), bf16[256,4,512]{0,2,1:T(8,128)(2,1)}) %reduce-scatter.2.cloned.1.call-update) | async-done | bytes 1048592 | tf_op jit(solution)/shard_map/reduce_scatter | solution.py:25
  47.4 1.6 %select_convert_fusion = bf16[256,4,512]{0,2,1:T(8,128)(2,1)S(1)} fusion(bf16[256,4,512]{0,2,1:T(8,128)(2,1)} %reduce-scatter.2.cloned.1.call-done, pred[4,512]{1,0:T(4,128)(4,1)S(1)} %iota_compare_fusion.5, pred[256,4]{0,1:T(4,128)(4,1)S(1)} %broadcast_compare_fusion), kind=kLoop, calls=%fused_computation.7 | loop fusion | flops 2097152 | bytes 2100224 | tf_op jit(solution)/shard_map/convert_element_type | solution.py:34
  48.9 1.3 %copy.19 = bf16[256,4,512]{2,0,1:T(8,128)(2,1)} copy(bf16[256,4,512]{0,2,1:T(8,128)(2,1)S(1)} %select_convert_fusion) | data formatting | bytes 2097152 | tf_op jit(solution)/shard_map/convert_element_type | solution.py:34
  50.3 1.3 %reshape.149 = bf16[4,64,4,2,256]{4,3,1,0,2:T(2,128)(2,1)S(1)} reshape(bf16[256,4,512]{2,0,1:T(8,128)(2,1)} %copy.19) | data formatting | bytes 2097152 | tf_op jit(solution)/shard_map/reshape | solution.py:37
  51.6 0.2 copy.20
  51.8 0.6 copy.23
  52.4 2.1 %convolution_convert_fusion = bf16[64,16384]{1,0:T(8,128)(2,1)} fusion(bf16[32,16384]{1,0:T(8,128)(2,1)S(1)} %bitcast.30, s32[32]{0:T(128)S(1)} %get-tuple-element.6), kind=kOutput, calls=%fused_computation | convolution fusion | flops 68159488 | bytes 3145856 | tf_op jit(solution)/shard_map/dot_general | solution.py:53
  54.5 4.1 %reshape.151 = bf16[16,4,16384]{2,1,0:T(4,128)(2,1)} reshape(bf16[64,16384]{1,0:T(8,128)(2,1)} %convolution_convert_fusion) | data formatting | bytes 4194304 | tf_op jit(solution)/shard_map/reshape | solution.py:56
  58.6 0.0 all-to-all-done
  58.6 6.4 %all-to-all-start.1 = ((bf16[16,4,16384]{2,1,0:T(4,128)(2,1)}), bf16[16,4,16384]{2,1,0:T(4,128)(2,1)}, u32[]{:S(2)}, u32[]{:S(2)}) async-start(bf16[16,4,16384]{2,1,0:T(4,128)(2,1)} %reshape.151), calls=%async_computation.2 | async-start | bytes 4194304 | tf_op jit(solution)/shard_map/all_to_all | solution.py:61
  65.0 0.5 broadcast.100
  65.5 0.7 reduce.3
  66.2 0.1 eq.47
  66.3 44.8 %all-to-all-done.1 = bf16[16,4,16384]{2,1,0:T(4,128)(2,1)} async-done(((bf16[16,4,16384]{2,1,0:T(4,128)(2,1)}), bf16[16,4,16384]{2,1,0:T(4,128)(2,1)}, u32[]{:S(2)}, u32[]{:S(2)}) %all-to-all-start.1) | async-done | bytes 2097184 | tf_op jit(solution)/shard_map/all_to_all | solution.py:61
  111.1 4.0 %reshape.152 = bf16[64,16384]{1,0:T(8,128)(2,1)} reshape(bf16[16,4,16384]{2,1,0:T(4,128)(2,1)} %all-to-all-done.1) | data formatting | bytes 4194304 | tf_op jit(solution)/shard_map/reshape | solution.py:64
  115.0 2.0 %convolution_convert_fusion.1 = bf16[32,16384]{1,0:T(8,128)(2,1)S(1)} fusion(bf16[64,16384]{1,0:T(8,128)(2,1)} %reshape.152, s32[64]{0:T(128)S(1)} %eq.47), kind=kOutput, calls=%fused_computation.1 | convolution fusion | flops 67635200 | bytes 3145984 | tf_op jit(solution)/shard_map/dot_general | solution.py:68
  117.1 0.2 copy.24
  117.3 1.1 copy.21
  118.4 1.5 %reshape.154 = bf16[4,256,512]{2,1,0:T(8,128)(2,1)} reshape(bf16[4,4,64,2,256]{4,3,2,1,0:T(2,128)(2,1)S(1)} %copy.21) | data formatting | bytes 2097152 | tf_op jit(solution)/shard_map/reshape | solution.py:70
  (5 shorter events, 0.0 us)
Async XLA Ops:
  6.5 1.6 %copy-start = (bf16[1,4,512,512]{3,2,1,0:T(8,128)(2,1)S(1)}, bf16[1,4,512,512]{3,2,1,0:T(8,128)(2,1)}, u32[]{:S(2)}) copy-start(bf16[1,4,512,512]{3,2,1,0:T(8,128)(2,1)} %param.8) | copy-start | bytes 6291460
  6.5 40.8 %reduce-scatter.2.cloned.1.call-start = ((), (), s32[]{:S(2)}) async-start(), calls=%async_computation.3 | async-start | bytes 3145728 | tf_op jit(solution)/shard_map/reduce_scatter | solution.py:25
  14.1 0.7 copy-start.2
  14.1 0.8 copy-start.3
  14.1 8.7 %copy-start.1 = (s32[4]{0:T(128)S(1)}, s32[4]{0:T(128)}, u32[]{:S(2)}) copy-start(s32[4]{0:T(128)} %param.11) | copy-start | bytes 52
  16.2 42.5 %all-to-all-start = ((s32[16,1,4]{2,1,0:T(1,128)}), s32[16,1,4]{2,1,0:T(1,128)S(1)}, u32[]{:S(2)}, u32[]{:S(2)}) async-start(s32[16,1,4]{2,1,0:T(1,128)} %bitcast), calls=%async_computation | async-start | bytes 16384 | tf_op jit(solution)/shard_map/all_to_all | solution.py:62
  58.6 52.4 %all-to-all-start.1 = ((bf16[16,4,16384]{2,1,0:T(4,128)(2,1)}), bf16[16,4,16384]{2,1,0:T(4,128)(2,1)}, u32[]{:S(2)}, u32[]{:S(2)}) async-start(bf16[16,4,16384]{2,1,0:T(4,128)(2,1)} %reshape.151), calls=%async_computation.2 | async-start | bytes 4194304 | tf_op jit(solution)/shard_map/all_to_all | solution.py:61
Sparse Core Ops, SparseCore 0:
  14.3 33.0 reduce-scatter.1
where the time goes:
time: 129 us; the launch traced here: 127 us
  waiting for transfers between devices  69.3 us (54%)
  local copies, waits for them, and re-layouts  16.6 us (13%)
  between operations  13.5 us (10%)
  starting transfers between devices  13 us (10%)
  matrix products  10.1 us (8%)
  other arithmetic  4.28 us (3%)
    all_to_all x1, waiting for transfers between devices, per_device(): lax.all_to_all(send_data, 'sector', split_axis=0, concat_axis=0, tiled=True)  44.8 us
    reduce_scatter x1, waiting for transfers between devices, per_device(): lax.psum_scatter((product * factor[None, :, None]).astype(jnp.bfloat16),...  24.5 us
    all_to_all x1, starting transfers between devices, per_device(): lax.all_to_all(send_code, 'sector', split_axis=0, concat_axis=0, tiled=True)  6.61 us
    all_to_all x1, starting transfers between devices, per_device(): lax.all_to_all(send_data, 'sector', split_axis=0, concat_axis=0, tiled=True)  6.36 us
    dot_general x1, matrix products, per_device(): jnp.einsum('bij,bjk->ibk', left_rows, right_part, preferred_element_type=...  5.97 us
    reshape x1, local copies, waits for them, and re-layouts, per_device(): send_data = send_data.reshape(peer_count, capacity, group_rows * width_part)  4.11 us
    reshape x1, local copies, waits for them, and re-layouts, per_device(): arrived_data.reshape(peer_count * capacity, group_rows * width_part)  3.97 us
  transfers between devices with their start and end apart: 3, of which 2 were waited for; matrix products, arithmetic and copies ran while one was open for 11% of the time, Pallas kernels for 0%

commit v1 on v0

v1 whole, which is shorter than its diff:
```python
import functools

import jax
import jax.numpy as jnp
from jax import lax
from jax.experimental import pallas as pl
from jax.experimental.pallas import tpu as pltpu
from jax.sharding import PartitionSpec as P

ROW_GROUPS = 4
COL_PARTS = 2
PIECES = 8
SLOTS = 2
SPILL = 3
PHASES = 2
LANES = 128
INFO = 16

VMEM = pl.BlockSpec(memory_space=pltpu.VMEM)
SMEM = pl.BlockSpec(memory_space=pltpu.SMEM)
ANY = pl.BlockSpec(memory_space=pl.ANY)


def params(mib):
    return pltpu.CompilerParams(vmem_limit_bytes=mib * 2**20)


def exchange_all(sigma_share, route_owner, route_block):
    row_count, block_count, states = sigma_share.shape
    group_rows = row_count // ROW_GROUPS
    width_part = states // COL_PARTS
    pieces = sigma_share.reshape(ROW_GROUPS, group_rows, block_count, COL_PARTS, width_part)
    pieces = pieces.transpose(2, 0, 3, 1, 4).reshape(block_count * PIECES, group_rows * width_part)
    owners = route_owner[0].reshape(-1)
    target_code = (route_block[0] * PIECES + jnp.arange(PIECES, dtype=jnp.int32)[None, :]).reshape(-1)
    peer_count = lax.axis_size("sector")
    capacity = min(block_count, max(2, (2 * block_count * PIECES + peer_count - 1) // peer_count))
    is_owner = (owners[:, None] == jnp.arange(peer_count, dtype=jnp.int32)[None, :]).astype(jnp.int32)
    before = jnp.cumsum(is_owner, axis=0) - is_owner
    position = jnp.sum(before * is_owner, axis=1)
    destination = owners * capacity + position
    slot_ids = jnp.arange(peer_count * capacity, dtype=jnp.int32)
    placing = slot_ids[:, None] == destination[None, :]
    send_data = jnp.dot(placing.astype(jnp.bfloat16), pieces, preferred_element_type=jnp.float32).astype(jnp.bfloat16)
    send_data = send_data.reshape(peer_count, capacity, group_rows * width_part)
    send_code = (jnp.sum(placing.astype(jnp.int32) * (target_code + 1)[None, :], axis=1) - 1).reshape(peer_count, capacity)
    arrived_data, arrived_code = (
        lax.all_to_all(send_data, "sector", split_axis=0, concat_axis=0, tiled=True),
        lax.all_to_all(send_code, "sector", split_axis=0, concat_axis=0, tiled=True),
    )
    arrived_data = arrived_data.reshape(peer_count * capacity, group_rows * width_part)
    arrived_code = arrived_code.reshape(-1)
    targets = jnp.arange(block_count * PIECES, dtype=jnp.int32)
    collect = (arrived_code[None, :] == targets[:, None]).astype(jnp.bfloat16)
    landed = jnp.dot(collect, arrived_data, preferred_element_type=jnp.float32).astype(jnp.bfloat16)
    landed = landed.reshape(block_count, ROW_GROUPS, COL_PARTS, group_rows, width_part)
    return landed.transpose(0, 1, 3, 2, 4).reshape(block_count, row_count, states)


def general(wavefunction, left_env, right_env, mpo_mask, block_size, route_owner, route_block):
    states = wavefunction.shape[1]
    row_count = states // lax.axis_size("mpo")
    positions = jnp.arange(states, dtype=jnp.int32)
    live_cols = positions[None, :] < block_size[:, None]
    live_mask = live_cols[:, :, None] & live_cols[:, None, :]
    masked = jnp.where(live_mask, wavefunction, jnp.zeros_like(wavefunction))
    right_part = jnp.einsum("bij,bkj->bik", masked, right_env[0], preferred_element_type=jnp.float32).astype(jnp.bfloat16)
    factor = mpo_mask[0].astype(jnp.float32)
    product = jnp.einsum("bij,bjk->ibk", left_env[0], right_part, preferred_element_type=jnp.float32)
    row_share = lax.psum_scatter(
        (product * factor[None, :, None]).astype(jnp.bfloat16), "mpo", scatter_dimension=0, tiled=True
    ).astype(jnp.float32)
    global_rows = lax.axis_index("mpo") * row_count + jnp.arange(row_count, dtype=jnp.int32)
    live_rows = global_rows[:, None] < block_size[None, :]
    share_mask = live_rows[:, :, None] & live_cols[None, :, :]
    sigma_share = jnp.where(share_mask, row_share, jnp.zeros_like(row_share)).astype(jnp.bfloat16)
    return exchange_all(sigma_share, route_owner, route_block)


def route_kernel(peers, blocks, group_rows, width, place_ref, owner_ref, block_ref, size_ref, src_ref, info_ref, count):
    first_row = place_ref[0] * (ROW_GROUPS * group_rows)

    def clear(i, _):
        src_ref[i] = -1
        info_ref[i] = -1
        return 0

    lax.fori_loop(0, LANES, clear, 0)

    def clear_count(i, _):
        count[i] = 0
        return 0

    lax.fori_loop(0, peers, clear_count, 0)
    spill_at = peers * SLOTS

    def one(i, spilled):
        b, k = i // PIECES, i % PIECES
        g, c = k // COL_PARTS, k % COL_PARTS
        size = size_ref[b]
        live = (first_row + g * group_rows < size) & (c * width < size)
        owner = owner_ref[i]
        pos = count[owner]
        index = (b * COL_PARTS + c) * ROW_GROUPS + g
        code = block_ref[i] * PIECES + k
        direct = live & (pos < SLOTS)
        spills = live & (pos >= SLOTS)

        @pl.when(direct)
        def _():
            src_ref[owner * SLOTS + pos] = index
            info_ref[owner * SLOTS + pos] = code
            count[owner] = pos + 1

        @pl.when(spills & (spilled < SPILL))
        def _():
            src_ref[spill_at + spilled] = index
            info_ref[spill_at + spilled] = owner
            info_ref[spill_at + SPILL + spilled] = code

        return spilled + spills.astype(jnp.int32)

    spilled = lax.fori_loop(0, blocks * PIECES, one, 0)
    src_ref[LANES - 1] = (spilled > SPILL).astype(jnp.int32)


def term_kernel(share, width, place_ref, size_ref, mask_ref, wave_ref, left_ref, right_ref, own_ref, send_ref, phase):
    b = pl.program_id(0)
    mine = place_ref[0]
    size = size_ref[b]
    active = mask_ref[b] != 0
    states = wave_ref.shape[1]
    span = right_ref.shape[3]
    rows = lax.broadcasted_iota(jnp.int32, (states, states), 0)
    cols = lax.broadcasted_iota(jnp.int32, (states, states), 1)
    masked = jnp.where((rows < size) & (cols < size), wave_ref[0], jnp.zeros_like(wave_ref[0]))
    right = right_ref[0, :, 0].reshape(COL_PARTS * span, states)
    part = lax.dot_general(masked, right, (((1,), (1,)), ((), ())), preferred_element_type=jnp.float32).astype(jnp.bfloat16)
    row = lax.broadcasted_iota(jnp.int32, (share, COL_PARTS * span), 0)
    lane = lax.broadcasted_iota(jnp.int32, (share, COL_PARTS * span), 1)
    col = (lane // span) * width + phase * span + lane % span
    for target, half in ((send_ref, 1 - mine), (own_ref, mine)):
        start = pl.multiple_of(half * share, share)
        product = jnp.dot(left_ref[0, pl.ds(start, share), :], part, preferred_element_type=jnp.float32)
        keep = (row + start < size) & (col < size) & active
        product = jnp.where(keep, product, 0.0).astype(jnp.bfloat16)
        for c in range(COL_PARTS):
            target[0, c] = product[:, c * span : (c + 1) * span]


def terms(place, sizes, mask, wave, left, right, phase, share):
    blocks, states, _ = wave.shape
    width = states // COL_PARTS
    span = width // PHASES
    right = right.reshape(blocks, COL_PARTS, PHASES, span, states)
    out = jax.ShapeDtypeStruct((blocks, COL_PARTS, share, span), jnp.bfloat16)
    out_spec = pl.BlockSpec((1, COL_PARTS, share, span), lambda b, *_: (b, 0, 0, 0))
    body = functools.partial(term_kernel, share, width, phase=phase)
    return pl.pallas_call(
        body,
        grid_spec=pltpu.PrefetchScalarGridSpec(
            num_scalar_prefetch=3,
            grid=(blocks,),
            in_specs=[
                pl.BlockSpec((1, states, states), lambda b, *_: (b, 0, 0)),
                pl.BlockSpec((1, states, states), lambda b, *_: (b, 0, 0)),
                pl.BlockSpec((1, COL_PARTS, 1, span, states), lambda b, *_: (b, 0, phase, 0, 0)),
            ],
            out_specs=[out_spec, out_spec],
        ),
        out_shape=[out, out],
        compiler_params=params(40),
        cost_estimate=pl.CostEstimate(
            flops=4 * blocks * states * states * width, bytes_accessed=6 * blocks * states * states, transcendentals=0
        ),
        name="terms",
    )(place, sizes, mask, wave, left, right)


def pick_kernel(rows, src_ref, *refs):
    sources, out_ref, sems = refs[:PHASES], refs[PHASES], refs[PHASES + 1]
    copies = []
    for p in range(PHASES):
        for j in range(SPILL):
            at = pl.multiple_of(jnp.maximum(src_ref[j], 0) * rows, rows)
            to = (p * SPILL + j) * rows
            copies.append(pltpu.make_async_copy(sources[p].at[pl.ds(at, rows)], out_ref.at[pl.ds(to, rows)], sems.at[p * SPILL + j]))
    for copy in copies:
        copy.start()
    for copy in copies:
        copy.wait()


def pick(src, arrays, rows):
    return pl.pallas_call(
        functools.partial(pick_kernel, rows),
        in_specs=[SMEM] + [ANY] * PHASES,
        out_specs=VMEM,
        out_shape=jax.ShapeDtypeStruct((PHASES * SPILL * rows, LANES), jnp.bfloat16),
        scratch_shapes=[pltpu.SemaphoreType.DMA((PHASES * SPILL,))],
        compiler_params=params(16),
        name="pick",
    )(src, *arrays)


def spill_kernel(mine_ref, other_ref, info_ref, out_ref):
    count = mine_ref.shape[0]
    out_ref[:count] = (mine_ref[...].astype(jnp.float32) + other_ref[...].astype(jnp.float32)).astype(jnp.bfloat16)
    out_ref[count:] = info_ref[...]


def pack_kernel(rows, slots, src_ref, own_ref, other_ref, out_ref):
    def one(j, _):
        index = src_ref[j]

        @pl.when(index >= 0)
        def _():
            at = pl.ds(pl.multiple_of(index * rows, rows), rows)
            total = own_ref[at, :].astype(jnp.float32) + other_ref[at, :].astype(jnp.float32)
            out_ref[pl.ds(pl.multiple_of(j * rows, rows), rows), :] = total.astype(jnp.bfloat16)

        return 0

    lax.fori_loop(0, slots, one, 0)


def pack(src, own, other, rows, slots):
    return pl.pallas_call(
        functools.partial(pack_kernel, rows, slots),
        in_specs=[SMEM, VMEM, VMEM],
        out_specs=VMEM,
        out_shape=jax.ShapeDtypeStruct((slots * rows, LANES), jnp.bfloat16),
        compiler_params=params(16),
        name="pack",
    )(src, own, other)


def add_spilled(rows, peers, phase, place_ref, info_ref, sets, acc):
    me = place_ref[1]
    spill_at = peers * SLOTS
    chunk = PHASES * SPILL * rows + INFO
    each = peers // len(sets)
    for which, ref in enumerate(sets):

        def one(i, _, which=which, ref=ref):
            source, j = i // SPILL, i % SPILL
            table = which * each + source

            @pl.when(info_ref[table, spill_at + j] == me)
            def _():
                code = info_ref[table, spill_at + SPILL + j]
                start = source * chunk + (phase * SPILL + j) * rows
                at = pl.ds(pl.multiple_of(start, 16), rows)
                to = pl.ds(pl.multiple_of(code * rows, rows), rows)
                acc[to, :] += ref[at, :].astype(jnp.float32)

            return 0

        lax.fori_loop(0, each * SPILL, one, 0)


def add_direct(rows, peers, place_ref, info_ref, arrived_ref, acc):
    me = place_ref[1]
    quarter = peers // 4

    def one(j, _):
        source, slot = j // SLOTS, j % SLOTS
        apart = source ^ me
        table = ((apart & 1) * 2 + ((apart >> 1) & 1)) * quarter + (apart >> 2)
        code = info_ref[table, me * SLOTS + slot]

        @pl.when(code >= 0)
        def _():
            at = pl.ds(pl.multiple_of(j * rows, rows), rows)
            to = pl.ds(pl.multiple_of(code * rows, rows), rows)
            acc[to, :] += arrived_ref[at, :].astype(jnp.float32)

        return 0

    lax.fori_loop(0, peers * SLOTS, one, 0)


def early_kernel(rows, peers, place_ref, info_ref, arrived_ref, *refs):
    sets, done_ref, later_ref, acc = refs[:4], refs[4], refs[5], refs[6]
    acc[...] = jnp.zeros_like(acc)
    later_ref[...] = jnp.zeros_like(later_ref)
    add_spilled(rows, peers, 0, place_ref, info_ref, sets, acc)
    add_spilled(rows, peers, 1, place_ref, info_ref, sets, later_ref)
    add_direct(rows, peers, place_ref, info_ref, arrived_ref, acc)
    done_ref[...] = acc[...].astype(jnp.bfloat16)


def late_kernel(rows, peers, place_ref, info_ref, arrived_ref, done_ref, later_ref, out_ref, acc):
    acc[...] = later_ref[...]
    add_direct(rows, peers, place_ref, info_ref, arrived_ref, acc)
    width = out_ref.shape[2] // COL_PARTS
    span = width // PHASES
    for t in range(out_ref.shape[0]):
        for k in range(PIECES):
            g, c = k // COL_PARTS, k % COL_PARTS
            at = slice((t * PIECES + k) * rows, (t * PIECES + k + 1) * rows)
            out_ref[t, g * rows : (g + 1) * rows, c * width : c * width + span] = done_ref[at, :]
            out_ref[t, g * rows : (g + 1) * rows, c * width + span : (c + 1) * width] = acc[at, :].astype(jnp.bfloat16)


def two_halves(wavefunction, left_env, right_env, mpo_mask, block_size, route_owner, route_block):
    blocks, states, _ = wavefunction.shape
    share = states // 2
    rows = share // ROW_GROUPS
    width = states // COL_PARTS
    span = width // PHASES
    peers = lax.axis_size("sector")
    total = blocks * PIECES
    place = jnp.stack([lax.axis_index("mpo"), lax.axis_index("sector")]).astype(jnp.int32)
    owners, targets = route_owner.reshape(-1), route_block.reshape(-1)
    swap = [(0, 1), (1, 0)]

    src, info = pl.pallas_call(
        functools.partial(route_kernel, peers, blocks, rows, width),
        in_specs=[SMEM] * 4,
        out_specs=[SMEM, SMEM],
        out_shape=[jax.ShapeDtypeStruct((LANES,), jnp.int32)] * 2,
        scratch_shapes=[pltpu.SMEM((peers,), jnp.int32)],
        name="route",
    )(place, owners, targets, block_size)
    spill_src = src[peers * SLOTS : peers * SLOTS + SPILL]
    told = lax.ppermute(src, "mpo", swap)
    more = jnp.maximum(src[LANES - 1], told[LANES - 1])
    lane = lax.broadcasted_iota(jnp.int32, (INFO, LANES), 1)
    table = jnp.where(lane == LANES - 1, more, info[None, :]).astype(jnp.bfloat16)

    own, send, other = [], [], []
    for phase in range(PHASES):
        mine, theirs = terms(place, block_size, mpo_mask[0], wavefunction, left_env[0], right_env[0], phase, share)
        own.append(mine.reshape(total * rows, span))
        send.append(theirs.reshape(total * rows, span))
        other.append(lax.ppermute(send[-1], "mpo", swap))

    asked = told[peers * SLOTS : peers * SLOTS + SPILL]
    spill_other = lax.ppermute(pick(asked, send, rows), "mpo", swap)
    spill_own = pick(spill_src, own, rows)
    chunk = PHASES * SPILL * rows + INFO
    spilled = pl.pallas_call(
        spill_kernel,
        in_specs=[VMEM] * 3,
        out_specs=VMEM,
        out_shape=jax.ShapeDtypeStruct((chunk, LANES), jnp.bfloat16),
        compiler_params=params(16),
        name="spill",
    )(spill_own, spill_other, table)

    def across(x, apart):
        return lax.ppermute(x, "sector", [(i, i ^ apart) for i in range(peers)])

    near = jnp.concatenate([spilled] + [across(spilled, apart) for apart in range(4, peers, 4)], axis=0)
    beside = across(near, 2)
    sets = [near, beside, across(near, 1), across(beside, 1)]
    tables = jnp.concatenate([s.reshape(peers // 4, chunk, LANES)[:, chunk - INFO] for s in sets], axis=0).astype(jnp.int32)

    arrived = []
    for phase in range(PHASES):
        packed = pack(src, own[phase], other[phase], rows, peers * SLOTS)
        packed = packed.reshape(peers, SLOTS * rows, span)
        landed = lax.all_to_all(packed, "sector", split_axis=0, concat_axis=0, tiled=True)
        arrived.append(landed.reshape(peers * SLOTS * rows, span))

    done, later = pl.pallas_call(
        functools.partial(early_kernel, rows, peers),
        in_specs=[SMEM, SMEM] + [VMEM] * 5,
        out_specs=[VMEM, VMEM],
        out_shape=[
            jax.ShapeDtypeStruct((total * rows, span), jnp.bfloat16),
            jax.ShapeDtypeStruct((total * rows, span), jnp.float32),
        ],
        scratch_shapes=[pltpu.VMEM((total * rows, span), jnp.float32)],
        compiler_params=params(32),
        name="early",
    )(place, tables, arrived[0], *sets)

    def fast(place, tables, landed, done, later, *_):
        return pl.pallas_call(
            functools.partial(late_kernel, rows, peers),
            in_specs=[SMEM, SMEM] + [VMEM] * 3,
            out_specs=VMEM,
            out_shape=jax.ShapeDtypeStruct((blocks, share, states), jnp.bfloat16),
            scratch_shapes=[pltpu.VMEM((total * rows, span), jnp.float32)],
            compiler_params=params(32),
            name="late",
        )(place, tables, landed, done, later)

    def slow(place, tables, landed, done, later, own, other):
        whole = [(a.astype(jnp.float32) + b.astype(jnp.float32)).astype(jnp.bfloat16) for a, b in zip(own, other)]
        whole = [w.reshape(blocks, COL_PARTS, share, span) for w in whole]
        sigma = jnp.stack(whole, axis=3).transpose(2, 0, 1, 3, 4).reshape(share, blocks, states)
        return exchange_all(sigma, route_owner, route_block)

    enough = jnp.max(tables[:, LANES - 1]) <= 0
    return lax.cond(enough, fast, slow, place, tables, arrived[1], done, later, tuple(own), tuple(other))


def solution(mesh):
    placed = (
        P("sector", None, None),
        P("mpo", "sector", None, None),
        P("mpo", "sector", None, None),
        P("mpo", "sector"),
        P("sector"),
        P("mpo", "sector", None),
        P("mpo", "sector", None),
    )

    def per_device(wavefunction, *rest):
        states = wavefunction.shape[1]
        peers = mesh.shape["sector"]
        fits = (
            mesh.shape["mpo"] == 2
            and peers >= 8
            and peers & (peers - 1) == 0
            and states // COL_PARTS == PHASES * LANES
            and states // (2 * ROW_GROUPS) % 16 == 0
            and peers * SLOTS + 2 * SPILL < LANES
        )
        return (two_halves if fits else general)(wavefunction, *rest)

    return jax.shard_map(per_device, mesh=mesh, in_specs=placed, out_specs=P("sector", "mpo", None), check_vma=False)
```

time: 129 us -> 96.9 us (0.75)
  waiting for transfers between devices: 69.3 us -> 29.4 us
  Pallas kernels: 0 us -> 24.4 us
  starting transfers between devices: 13 us -> 24.9 us
  between operations: 13.5 us -> 2.05 us
  matrix products: 10.1 us -> 0 us
  other arithmetic: 4.28 us -> 0.83 us
  local copies, waits for them, and re-layouts: 16.6 us -> 13.5 us
    all_to_all x2, waiting for transfers between devices: 44.8 us -> 5.19 us  [two_halves(): lax.all_to_all(packed, 'sector', split_axis=0, concat_axis=0, tiled=True)]
    reduce_scatter x1 -> x0, waiting for transfers between devices: 24.5 us -> none  [per_device(): lax.psum_scatter((product * factor[None, :, None]).astype(jnp.bfloat16),...]
    pallas_call x0 -> x10, Pallas kernels: none -> 24.4 us  [the longest x2 7.59 us: terms(): pl.pallas_call(body, grid_spec=pltpu.PrefetchScalarGridSpec(num_scalar_pr...]
    ppermute x0 -> x10, waiting for transfers between devices: none -> 24.2 us  [the longest x1 9.32 us: two_halves(): spill_other = lax.ppermute(pick(asked, send, rows), 'mpo', swap)]
    dot_general x3 -> x0, matrix products: 10.1 us -> none  [the longest x1 5.97 us: per_device(): jnp.einsum('bij,bjk->ibk', left_rows, right_part, preferred_element_type=...]
    reshape x4 -> x2, local copies, waits for them, and re-layouts: 10.9 us -> 1.25 us  [two_halves(): owners, targets = (route_owner.reshape(-1), route_block.reshape(-1))]
    ppermute x0 -> x10, starting transfers between devices: none -> 9.38 us  [the longest x6 5.27 us: across(): return lax.ppermute(x, 'sector', [(i, i ^ apart) for i in range(peers)])]
    unnamed x10 -> x46, local copies, waits for them, and re-layouts: 1.56 us -> 10.9 us
  transfers between devices with their start and end apart: 3 -> 12, of which waited for: 2 -> 8; matrix products, arithmetic and copies ran while one was open for 11% -> 4% of each run, Pallas kernels for 0% -> 16%
where the time goes in v1:
time: 96.9 us; the launch traced here: 95.1 us
  waiting for transfers between devices  29.4 us (30%)
  starting transfers between devices  24.9 us (26%)
  Pallas kernels  24.4 us (25%)
  local copies, waits for them, and re-layouts  13.5 us (14%)
  between operations  2.05 us (2%)
    all_to_all x2, starting transfers between devices, two_halves(): lax.all_to_all(packed, 'sector', split_axis=0, concat_axis=0, tiled=True)  15.5 us
    unnamed x46, local copies, waits for them, and re-layouts  10.9 us
    ppermute x1, waiting for transfers between devices, two_halves(): spill_other = lax.ppermute(pick(asked, send, rows), 'mpo', swap)  9.32 us
    pallas_call x2, Pallas kernels, terms(): pl.pallas_call(body, grid_spec=pltpu.PrefetchScalarGridSpec(num_scalar_pr...  7.59 us
    ppermute x6, waiting for transfers between devices, across(): return lax.ppermute(x, 'sector', [(i, i ^ apart) for i in range(peers)])  7.48 us
    ppermute x2, waiting for transfers between devices, two_halves(): other.append(lax.ppermute(send[-1], 'mpo', swap))  7.39 us
    pallas_call x1, Pallas kernels, two_halves(): pl.pallas_call(functools.partial(early_kernel, rows, peers), in_specs=[SM...  5.38 us
    ppermute x6, starting transfers between devices, across(): return lax.ppermute(x, 'sector', [(i, i ^ apart) for i in range(peers)])  5.27 us
  transfers between devices with their start and end apart: 12, of which 8 were waited for; matrix products, arithmetic and copies ran while one was open for 4% of the time, Pallas kernels for 16%

profile of v1, /device:TPU:9, one launch (start us, length us, event | category | flops | bytes accessed | tf_op | source)
XLA Modules:
  0.0 95.1 jit_solution(11482912436578639790)
XLA Ops:
  0.0 0.1 pad_add_fusion.place_ref
  0.1 1.6 %copy-done = bf16[4,512,512]{2,1,0:T(8,128)(2,1)S(1)} copy-done((bf16[4,512,512]{2,1,0:T(8,128)(2,1)S(1)}, bf16[4,512,512]{2,1,0:T(8,128)(2,1)}, u32[]{:S(2)}) %copy-start) | copy-done | bytes 2097176
  1.7 1.6 %copy-done.2 = bf16[1,4,512,512]{3,2,1,0:T(8,128)(2,1)S(1)} copy-done((bf16[1,4,512,512]{3,2,1,0:T(8,128)(2,1)S(1)}, bf16[1,4,512,512]{3,2,1,0:T(8,128)(2,1)}, u32[]{:S(2)}) %copy-start.2) | copy-done | bytes 2097176
  3.3 1.6 %copy-done.4 = bf16[1,4,512,512]{3,2,1,0:T(8,128)(2,1)S(1)} copy-done((bf16[1,4,512,512]{3,2,1,0:T(8,128)(2,1)S(1)}, bf16[1,4,512,512]{3,2,1,0:T(8,128)(2,1)}, u32[]{:S(2)}) %copy-start.4) | copy-done | bytes 2097176
  4.9 0.7 copy-done.6
  5.5 0.7 copy-done.8
  6.2 3.8 %terms.2 = (bf16[4,2,256,128]{3,2,1,0:T(8,128)(2,1)S(1)}, bf16[4,2,256,128]{3,2,1,0:T(8,128)(2,1)S(1)}) custom-call(s32[2]{0:T(128)S(1)} %pad_add_fusion.place_ref, s32[4]{0:T(128)S(1)} %copy-done.6, s32[4]{0:T(128)S(1)} %bitcast.61, bf16[4,512,512]{2,1,0:T(8,128)(2,1)S(1)} %copy-done, bf16[4,512,512]{2,1,0:T(8,128)(2,1)S(1)} %bitcast.48, ...), custom_call_target="tpu_custom_call" | custom-call | flops 1073741824 | bytes 6291456 | tf_op jit(solution)/shard_map/terms/pallas_call | solution.py:159
  10.0 0.0 copy-start.1
  10.0 1.3 %collective-permute-start.8 = (bf16[2048,128]{1,0:T(8,128)(2,1)S(1)}, bf16[2048,128]{1,0:T(8,128)(2,1)}, u32[]{:S(2)}, u32[]{:S(2)}) collective-permute-start(bf16[2048,128]{1,0:T(8,128)(2,1)S(1)} %bitcast.56), channel_id=1, source_target_pairs={{0,16},{16,0},{1,17},{17,1},{2,18},{18,2},{3,19},{19,3},{4,20},{20... | collective-permute-start | bytes 1572872 | tf_op jit(solution)/shard_map/ppermute | solution.py:337
  11.3 0.6 reshape.113.owner_ref
  11.9 0.7 reshape.114.block_ref
  12.5 3.0 %route.1 = (s32[128]{0:T(128)}, s32[128]{0:T(128)}) custom-call(s32[2]{0:T(128)S(1)} %pad_add_fusion.place_ref, s32[32]{0:T(128)} %reshape.113.owner_ref, s32[32]{0:T(128)} %reshape.114.block_ref, s32[4]{0:T(128)} %size_ref.5), custom_call_target="tpu_custom_call" | custom-call | tf_op jit(solution)/shard_map/route/pallas_call | solution.py:318
  15.6 7.4 %collective-permute-done.8.other_ref = bf16[2048,128]{1,0:T(8,128)(2,1)} collective-permute-done((bf16[2048,128]{1,0:T(8,128)(2,1)S(1)}, bf16[2048,128]{1,0:T(8,128)(2,1)}, u32[]{:S(2)}, u32[]{:S(2)}) %collective-permute-start.8) | collective-permute-done | bytes 524320 | tf_op jit(solution)/shard_map/ppermute | solution.py:337
  23.0 0.6 copy-done.10
  23.6 2.4 %pack.3 = bf16[2048,128]{1,0:T(8,128)(2,1)} custom-call(s32[128]{0:T(128)S(1)} %copy-done.10, bf16[2048,128]{1,0:T(8,128)(2,1)S(1)} %bitcast.63, bf16[2048,128]{1,0:T(8,128)(2,1)} %collective-permute-done.8.other_ref), custom_call_target="tpu_custom_call" | custom-call | tf_op jit(solution)/shard_map/pack/pallas_call | solution.py:228
  25.9 7.4 %all-to-all-start.3 = ((bf16[16,128,128]{2,1,0:T(8,128)(2,1)}), bf16[16,128,128]{2,1,0:T(8,128)(2,1)S(1)}, u32[]{:S(2)}, u32[]{:S(2)}) async-start(bf16[16,128,128]{2,1,0:T(8,128)(2,1)} %bitcast.26), calls=%async_computation.3 | async-start | bytes 1048576 | tf_op jit(solution)/shard_map/all_to_all | solution.py:364
  33.4 1.2 %collective-permute-start = (s32[128]{0:T(128)S(1)}, s32[128]{0:T(128)S(1)}, u32[]{:S(2)}, u32[]{:S(2)}) collective-permute-start(s32[128]{0:T(128)S(1)} %copy-done.11), channel_id=1, source_target_pairs={{0,16},{16,0},{1,17},{17,1},{2,18},{18,2},{3,19},{19,3},{4,20},{20... | collective-permute-start | bytes 1544 | tf_op jit(solution)/shard_map/ppermute | solution.py:327
  34.6 1.6 %copy-done.3 = bf16[1,4,512,512]{3,2,1,0:T(8,128)(2,1)S(1)} copy-done((bf16[1,4,512,512]{3,2,1,0:T(8,128)(2,1)S(1)}, bf16[1,4,512,512]{3,2,1,0:T(8,128)(2,1)}, u32[]{:S(2)}) %copy-start.3) | copy-done | bytes 2097176
  36.2 1.6 %copy-done.5 = bf16[1,4,512,512]{3,2,1,0:T(8,128)(2,1)S(1)} copy-done((bf16[1,4,512,512]{3,2,1,0:T(8,128)(2,1)S(1)}, bf16[1,4,512,512]{3,2,1,0:T(8,128)(2,1)}, u32[]{:S(2)}) %copy-start.5) | copy-done | bytes 2097176
  37.8 3.8 %terms.3 = (bf16[4,2,256,128]{3,2,1,0:T(8,128)(2,1)S(1)}, bf16[4,2,256,128]{3,2,1,0:T(8,128)(2,1)S(1)}) custom-call(s32[2]{0:T(128)S(1)} %pad_add_fusion.place_ref, s32[4]{0:T(128)S(1)} %copy-done.7, s32[4]{0:T(128)S(1)} %bitcast.62, bf16[4,512,512]{2,1,0:T(8,128)(2,1)S(1)} %copy-done.1, bf16[4,512,512]{2,1,0:T(8,128)(2,1)S(1)} %bitcast.49, ...), custom_call_target="tpu_custom_call" | custom-call | flops 1073741824 | bytes 6291456 | tf_op jit(solution)/shard_map/terms/pallas_call | solution.py:159
  41.6 0.4 collective-permute-start.9
  42.0 0.6 slice.29
  42.6 0.1 slice.27.src_ref
  42.6 0.7 pick.2.mine_ref
  43.4 0.1 slice.28.src_ref
  43.5 0.7 pick.3
  44.2 1.2 %collective-permute-start.1 = (bf16[384,128]{1,0:T(8,128)(2,1)S(1)}, bf16[384,128]{1,0:T(8,128)(2,1)S(1)}, u32[]{:S(2)}, u32[]{:S(2)}) collective-permute-start(bf16[384,128]{1,0:T(8,128)(2,1)S(1)} %pick.3), channel_id=1, source_target_pairs={{0,16},{16,0},{1,17},{17,1},{2,18},{18,2},{3,19},{19,3},{4,20},{20... | collective-permute-start | bytes 294920 | tf_op jit(solution)/shard_map/ppermute | solution.py:340
  45.4 0.6 slice.30
  47.3 9.3 %collective-permute-done.1.other_ref = bf16[384,128]{1,0:T(8,128)(2,1)S(1)} collective-permute-done((bf16[384,128]{1,0:T(8,128)(2,1)S(1)}, bf16[384,128]{1,0:T(8,128)(2,1)S(1)}, u32[]{:S(2)}, u32[]{:S(2)}) %collective-permute-start.1) | collective-permute-done | bytes 98336 | tf_op jit(solution)/shard_map/ppermute | solution.py:340
  56.7 1.2 %collective-permute-start.4 = (bf16[400,128]{1,0:T(8,128)(2,1)S(1)}, bf16[400,128]{1,0:T(8,128)(2,1)S(1)}, u32[]{:S(2)}, u32[]{:S(2)}) collective-permute-start(bf16[400,128]{1,0:T(8,128)(2,1)S(1)} %spill.1), channel_id=1, source_target_pairs={{0,12},{1,13},{2,14},{3,15},{4,8},{5,9},{6,10},{7,11},{8,4},{9,5},... | collective-permute-start | bytes 307208 | tf_op jit(solution)/shard_map/ppermute | solution.py:353
  57.9 1.3 %collective-permute-start.3 = (bf16[400,128]{1,0:T(8,128)(2,1)S(1)}, bf16[400,128]{1,0:T(8,128)(2,1)S(1)}, u32[]{:S(2)}, u32[]{:S(2)}) collective-permute-start(bf16[400,128]{1,0:T(8,128)(2,1)S(1)} %spill.1), channel_id=1, source_target_pairs={{0,8},{1,9},{2,10},{3,11},{4,12},{5,13},{6,14},{7,15},{8,0},{9,1},... | collective-permute-start | bytes 307208 | tf_op jit(solution)/shard_map/ppermute | solution.py:353
  59.2 0.8 collective-permute-start.2
  60.0 0.3 collective-permute-done.4
  60.3 4.2 %collective-permute-done.3 = bf16[400,128]{1,0:T(8,128)(2,1)S(1)} collective-permute-done((bf16[400,128]{1,0:T(8,128)(2,1)S(1)}, bf16[400,128]{1,0:T(8,128)(2,1)S(1)}, u32[]{:S(2)}, u32[]{:S(2)}) %collective-permute-start.3) | collective-permute-done | bytes 102432 | tf_op jit(solution)/shard_map/ppermute | solution.py:353
  64.4 1.4 %collective-permute-done.2 = bf16[400,128]{1,0:T(8,128)(2,1)S(1)} collective-permute-done((bf16[400,128]{1,0:T(8,128)(2,1)S(1)}, bf16[400,128]{1,0:T(8,128)(2,1)S(1)}, u32[]{:S(2)}, u32[]{:S(2)}) %collective-permute-start.2) | collective-permute-done | bytes 102432 | tf_op jit(solution)/shard_map/ppermute | solution.py:353
  65.9 1.3 %collective-permute-start.5 = (bf16[1600,128]{1,0:T(8,128)(2,1)S(1)}, bf16[1600,128]{1,0:T(8,128)(2,1)S(1)}, u32[]{:S(2)}, u32[]{:S(2)}) collective-permute-start(bf16[1600,128]{1,0:T(8,128)(2,1)S(1)} %pad_maximum_fusion.refs_0_), channel_id=1, source_target_pairs={{0,2},{1,3},{2,0},{3,1},{4,6},{5,7},{6,4},{7,5},{8,10},{9,11},{10,... | collective-permute-start | bytes 1228808 | tf_op jit(solution)/shard_map/ppermute | solution.py:353
  67.2 1.9 %pack.2 = bf16[2048,128]{1,0:T(8,128)(2,1)} custom-call(s32[128]{0:T(128)S(1)} %copy-done.11, bf16[2048,128]{1,0:T(8,128)(2,1)S(1)} %bitcast.67, bf16[2048,128]{1,0:T(8,128)(2,1)S(1)} %collective-permute-done.9.other_ref), custom_call_target="tpu_custom_call" | custom-call | tf_op jit(solution)/shard_map/pack/pallas_call | solution.py:228
  69.1 8.1 %all-to-all-start.2 = ((bf16[16,128,128]{2,1,0:T(8,128)(2,1)}), bf16[16,128,128]{2,1,0:T(8,128)(2,1)}, u32[]{:S(2)}, u32[]{:S(2)}) async-start(bf16[16,128,128]{2,1,0:T(8,128)(2,1)} %bitcast.25), calls=%async_computation.2 | async-start | bytes 1048576 | tf_op jit(solution)/shard_map/all_to_all | solution.py:364
  77.2 0.4 collective-permute-start.6
  77.5 0.3 collective-permute-start.7
  77.9 1.0 %collective-permute-done.6.refs_2_ = bf16[1600,128]{1,0:T(8,128)(2,1)S(1)} collective-permute-done((bf16[1600,128]{1,0:T(8,128)(2,1)S(1)}, bf16[1600,128]{1,0:T(8,128)(2,1)S(1)}, u32[]{:S(2)}, u32[]{:S(2)}) %collective-permute-start.6) | collective-permute-done | bytes 409632 | tf_op jit(solution)/shard_map/ppermute | solution.py:353
  79.0 0.6 collective-permute-done.7.refs_3_
  79.5 0.7 slice_reduce_fusion
  80.9 5.4 %early.1 = (bf16[2048,128]{1,0:T(8,128)(2,1)}, f32[2048,128]{1,0:T(8,128)}) custom-call(s32[2]{0:T(128)S(1)} %pad_add_fusion.place_ref, s32[16,128]{1,0:T(8,128)S(1)} %maximum_convert_fusion.info_ref, bf16[2048,128]{1,0:T(8,128)(2,1)S(1)} %bitcast.52, bf16[1600,128]{1,0:T(8,128)(2,1)S(1)} %pad_maximum_fusion.refs_0_, ...), custom_call_target="tpu_custom_call" | custom-call | tf_op jit(solution)/shard_map/early/pallas_call | solution.py:367
  86.3 5.2 %all-to-all-done.2 = bf16[16,128,128]{2,1,0:T(8,128)(2,1)} async-done(((bf16[16,128,128]{2,1,0:T(8,128)(2,1)}), bf16[16,128,128]{2,1,0:T(8,128)(2,1)}, u32[]{:S(2)}, u32[]{:S(2)}) %all-to-all-start.2) | async-done | bytes 524320 | tf_op jit(solution)/shard_map/all_to_all | solution.py:364
  91.5 2.7 %conditional.1 = (bf16[4,256,512]{2,1,0:T(8,128)(2,1)S(1)}) conditional(s32[]{:T(128)} %convert_element_type.41, (s32[1,4,8]{2,1,0:T(4,128)S(1)}, s32[1,4,8]{2,1,0:T(4,128)S(1)}, bf16[2048,128]{1,0:T(8,128)(2,1)S(1)}, bf16[2048,128]{1,0:T(8,128)(2,1)}, bf16[2048,128]{1,0:T(8,128)(2,1)}, /*index=5*/bf16[2048,128]{1,0:T(8,128)(2,1)}) %tuple.24, ...), branch_computations={%region_1.5_spmd, %region_5.6_spmd} | conditional | flops 140014720 | bytes 40924632 | solution.py:398
  91.5 2.7 %late.1 = bf16[4,256,512]{2,1,0:T(8,128)(2,1)S(1)} custom-call(s32[2]{0:T(128)S(1)} %get-tuple-element.37.place_ref, s32[16,128]{1,0:T(8,128)S(1)} %get-tuple-element.38.info_ref, bf16[2048,128]{1,0:T(8,128)(2,1)} %bitcast.6.arrived_ref, bf16[2048,128]{1,0:T(8,128)(2,1)} %get-tuple-element.40.done_ref, f32[2048,128]{1,0:T(8,128)} %get-tuple-element.41.later_ref), custom_call_target="tpu_custom_call" | custom-call | tf_op jit(solution)/shard_map/cond/branch_1_fun/late/pallas_call | solution.py:381
  94.1 1.0 %copy-done.17 = bf16[4,256,512]{2,1,0:T(8,128)(2,1)} copy-done((bf16[4,256,512]{2,1,0:T(8,128)(2,1)}, bf16[4,256,512]{2,1,0:T(8,128)(2,1)S(1)}, u32[]{:S(2)}) %copy-start.17) | copy-done | bytes 1048600
  (49 shorter events, 0.2 us)
Async XLA Ops:
  0.1 1.6 %copy-start = (bf16[4,512,512]{2,1,0:T(8,128)(2,1)S(1)}, bf16[4,512,512]{2,1,0:T(8,128)(2,1)}, u32[]{:S(2)}) copy-start(bf16[4,512,512]{2,1,0:T(8,128)(2,1)} %wave_ref.3) | copy-start | bytes 6291460
  1.7 1.6 %copy-start.2 = (bf16[1,4,512,512]{3,2,1,0:T(8,128)(2,1)S(1)}, bf16[1,4,512,512]{3,2,1,0:T(8,128)(2,1)}, u32[]{:S(2)}) copy-start(bf16[1,4,512,512]{3,2,1,0:T(8,128)(2,1)} %param.10) | copy-start | bytes 6291460
  3.3 1.6 %copy-start.4 = (bf16[1,4,512,512]{3,2,1,0:T(8,128)(2,1)S(1)}, bf16[1,4,512,512]{3,2,1,0:T(8,128)(2,1)}, u32[]{:S(2)}) copy-start(bf16[1,4,512,512]{3,2,1,0:T(8,128)(2,1)} %param.11) | copy-start | bytes 6291460
  4.9 0.7 copy-start.6
  5.5 0.7 copy-start.8
  6.2 5.1 %copy-start.18 = (s32[1,4,8]{2,1,0:T(4,128)S(1)}, s32[1,4,8]{2,1,0:T(4,128)}, u32[]{:S(2)}) copy-start(s32[1,4,8]{2,1,0:T(4,128)} %param.14) | copy-start | bytes 388
  6.2 5.7 %copy-start.19 = (s32[1,4,8]{2,1,0:T(4,128)S(1)}, s32[1,4,8]{2,1,0:T(4,128)}, u32[]{:S(2)}) copy-start(s32[1,4,8]{2,1,0:T(4,128)} %param.15) | copy-start | bytes 388
  10.0 16.0 %copy-start.12 = (bf16[4,2,256,128]{3,2,1,0:T(8,128)(2,1)}, bf16[4,2,256,128]{3,2,1,0:T(8,128)(2,1)S(1)}, u32[]{:S(2)}) copy-start(bf16[4,2,256,128]{3,2,1,0:T(8,128)(2,1)S(1)} %get-tuple-element.51) | copy-start | bytes 1572868
  10.0 24.6 %copy-start.1 = (bf16[4,512,512]{2,1,0:T(8,128)(2,1)S(1)}, bf16[4,512,512]{2,1,0:T(8,128)(2,1)}, u32[]{:S(2)}) copy-start(bf16[4,512,512]{2,1,0:T(8,128)(2,1)} %wave_ref.3) | copy-start | bytes 6291460
  10.0 24.6 %copy-start.7 = (s32[4]{0:T(128)S(1)}, s32[4]{0:T(128)}, u32[]{:S(2)}) copy-start(s32[4]{0:T(128)} %size_ref.5) | copy-start | bytes 52
  10.0 24.6 %copy-start.9 = (s32[1,4]{1,0:T(1,128)S(1)}, s32[1,4]{1,0:T(1,128)}, u32[]{:S(2)}) copy-start(s32[1,4]{1,0:T(1,128)} %param.12) | copy-start | bytes 52
  10.0 13.0 %collective-permute-start.8 = (bf16[2048,128]{1,0:T(8,128)(2,1)S(1)}, bf16[2048,128]{1,0:T(8,128)(2,1)}, u32[]{:S(2)}, u32[]{:S(2)}) collective-permute-start(bf16[2048,128]{1,0:T(8,128)(2,1)S(1)} %bitcast.56), channel_id=1, source_target_pairs={{0,16},{16,0},{1,17},{17,1},{2,18},{18,2},{3,19},{19,3},{4,20},{20... | collective-permute-start | bytes 1572872 | tf_op jit(solution)/shard_map/ppermute | solution.py:337
  23.0 0.6 copy-start.10
  23.6 9.8 %copy-start.11 = (s32[128]{0:T(128)S(1)}, s32[128]{0:T(128)}, u32[]{:S(2)}) copy-start(s32[128]{0:T(128)} %get-tuple-element.50.src_ref) | copy-start | bytes 1540
  25.9 43.1 %all-to-all-start.3 = ((bf16[16,128,128]{2,1,0:T(8,128)(2,1)}), bf16[16,128,128]{2,1,0:T(8,128)(2,1)S(1)}, u32[]{:S(2)}, u32[]{:S(2)}) async-start(bf16[16,128,128]{2,1,0:T(8,128)(2,1)} %bitcast.26), calls=%async_computation.3 | async-start | bytes 1048576 | tf_op jit(solution)/shard_map/all_to_all | solution.py:364
  33.4 10.0 %collective-permute-start = (s32[128]{0:T(128)S(1)}, s32[128]{0:T(128)S(1)}, u32[]{:S(2)}, u32[]{:S(2)}) collective-permute-start(s32[128]{0:T(128)S(1)} %copy-done.11), channel_id=1, source_target_pairs={{0,16},{16,0},{1,17},{17,1},{2,18},{18,2},{3,19},{19,3},{4,20},{20... | collective-permute-start | bytes 1544 | tf_op jit(solution)/shard_map/ppermute | solution.py:327
  34.6 1.6 %copy-start.3 = (bf16[1,4,512,512]{3,2,1,0:T(8,128)(2,1)S(1)}, bf16[1,4,512,512]{3,2,1,0:T(8,128)(2,1)}, u32[]{:S(2)}) copy-start(bf16[1,4,512,512]{3,2,1,0:T(8,128)(2,1)} %param.10) | copy-start | bytes 6291460
  36.2 1.6 %copy-start.5 = (bf16[1,4,512,512]{3,2,1,0:T(8,128)(2,1)S(1)}, bf16[1,4,512,512]{3,2,1,0:T(8,128)(2,1)}, u32[]{:S(2)}) copy-start(bf16[1,4,512,512]{3,2,1,0:T(8,128)(2,1)} %param.11) | copy-start | bytes 6291460
  37.8 4.8 %copy-start.13 = (bf16[4,2,256,128]{3,2,1,0:T(8,128)(2,1)S(1)}, bf16[4,2,256,128]{3,2,1,0:T(8,128)(2,1)}, u32[]{:S(2)}) copy-start(bf16[4,2,256,128]{3,2,1,0:T(8,128)(2,1)} %copy-done.12) | copy-start | bytes 1572868
  41.6 25.6 %copy-start.15 = (bf16[4,2,256,128]{3,2,1,0:T(8,128)(2,1)}, bf16[4,2,256,128]{3,2,1,0:T(8,128)(2,1)S(1)}, u32[]{:S(2)}) copy-start(bf16[4,2,256,128]{3,2,1,0:T(8,128)(2,1)S(1)} %get-tuple-element.52) | copy-start | bytes 1572868
  41.6 5.7 %copy-start.20 = (s32[128]{0:T(128)S(1)}, s32[128]{0:T(128)}, u32[]{:S(2)}) copy-start(s32[128]{0:T(128)} %get-tuple-element.55) | copy-start | bytes 1540
  41.6 25.5 %collective-permute-start.9 = (bf16[2048,128]{1,0:T(8,128)(2,1)S(1)}, bf16[2048,128]{1,0:T(8,128)(2,1)S(1)}, u32[]{:S(2)}, u32[]{:S(2)}) collective-permute-start(bf16[2048,128]{1,0:T(8,128)(2,1)S(1)} %bitcast.54), channel_id=1, source_target_pairs={{0,16},{16,0},{1,17},{17,1},{2,18},{18,2},{3,19},{19,3},{4,20},{20... | collective-permute-start | bytes 1572872 | tf_op jit(solution)/shard_map/ppermute | solution.py:337
  44.2 12.4 %collective-permute-start.1 = (bf16[384,128]{1,0:T(8,128)(2,1)S(1)}, bf16[384,128]{1,0:T(8,128)(2,1)S(1)}, u32[]{:S(2)}, u32[]{:S(2)}) collective-permute-start(bf16[384,128]{1,0:T(8,128)(2,1)S(1)} %pick.3), channel_id=1, source_target_pairs={{0,16},{16,0},{1,17},{17,1},{2,18},{18,2},{3,19},{19,3},{4,20},{20... | collective-permute-start | bytes 294920 | tf_op jit(solution)/shard_map/ppermute | solution.py:340
  56.7 3.6 %collective-permute-start.4 = (bf16[400,128]{1,0:T(8,128)(2,1)S(1)}, bf16[400,128]{1,0:T(8,128)(2,1)S(1)}, u32[]{:S(2)}, u32[]{:S(2)}) collective-permute-start(bf16[400,128]{1,0:T(8,128)(2,1)S(1)} %spill.1), channel_id=1, source_target_pairs={{0,12},{1,13},{2,14},{3,15},{4,8},{5,9},{6,10},{7,11},{8,4},{9,5},... | collective-permute-start | bytes 307208 | tf_op jit(solution)/shard_map/ppermute | solution.py:353
  57.9 6.5 %collective-permute-start.3 = (bf16[400,128]{1,0:T(8,128)(2,1)S(1)}, bf16[400,128]{1,0:T(8,128)(2,1)S(1)}, u32[]{:S(2)}, u32[]{:S(2)}) collective-permute-start(bf16[400,128]{1,0:T(8,128)(2,1)S(1)} %spill.1), channel_id=1, source_target_pairs={{0,8},{1,9},{2,10},{3,11},{4,12},{5,13},{6,14},{7,15},{8,0},{9,1},... | collective-permute-start | bytes 307208 | tf_op jit(solution)/shard_map/ppermute | solution.py:353
  59.2 6.6 %collective-permute-start.2 = (bf16[400,128]{1,0:T(8,128)(2,1)S(1)}, bf16[400,128]{1,0:T(8,128)(2,1)S(1)}, u32[]{:S(2)}, u32[]{:S(2)}) collective-permute-start(bf16[400,128]{1,0:T(8,128)(2,1)S(1)} %spill.1), channel_id=1, source_target_pairs={{0,4},{1,5},{2,6},{3,7},{4,0},{5,1},{6,2},{7,3},{8,12},{9,13},{10,... | collective-permute-start | bytes 307208 | tf_op jit(solution)/shard_map/ppermute | solution.py:353
  65.9 25.6 %copy-start.14 = (bf16[4,2,256,128]{3,2,1,0:T(8,128)(2,1)S(1)}, bf16[4,2,256,128]{3,2,1,0:T(8,128)(2,1)}, u32[]{:S(2)}) copy-start(bf16[4,2,256,128]{3,2,1,0:T(8,128)(2,1)} %copy-done.12) | copy-start | bytes 1572868
  65.9 11.6 %collective-permute-start.5 = (bf16[1600,128]{1,0:T(8,128)(2,1)S(1)}, bf16[1600,128]{1,0:T(8,128)(2,1)S(1)}, u32[]{:S(2)}, u32[]{:S(2)}) collective-permute-start(bf16[1600,128]{1,0:T(8,128)(2,1)S(1)} %pad_maximum_fusion.refs_0_), channel_id=1, source_target_pairs={{0,2},{1,3},{2,0},{3,1},{4,6},{5,7},{6,4},{7,5},{8,10},{9,11},{10,... | collective-permute-start | bytes 1228808 | tf_op jit(solution)/shard_map/ppermute | solution.py:353
  67.2 1.9 %copy-start.16 = (bf16[2048,128]{1,0:T(8,128)(2,1)}, bf16[2048,128]{1,0:T(8,128)(2,1)S(1)}, u32[]{:S(2)}) copy-start(bf16[2048,128]{1,0:T(8,128)(2,1)S(1)} %collective-permute-done.9.other_ref) | copy-start | bytes 1572868
  69.1 22.4 %all-to-all-start.2 = ((bf16[16,128,128]{2,1,0:T(8,128)(2,1)}), bf16[16,128,128]{2,1,0:T(8,128)(2,1)}, u32[]{:S(2)}, u32[]{:S(2)}) async-start(bf16[16,128,128]{2,1,0:T(8,128)(2,1)} %bitcast.25), calls=%async_computation.2 | async-start | bytes 1048576 | tf_op jit(solution)/shard_map/all_to_all | solution.py:364
  77.2 1.7 %collective-permute-start.6 = (bf16[1600,128]{1,0:T(8,128)(2,1)S(1)}, bf16[1600,128]{1,0:T(8,128)(2,1)S(1)}, u32[]{:S(2)}, u32[]{:S(2)}) collective-permute-start(bf16[1600,128]{1,0:T(8,128)(2,1)S(1)} %pad_maximum_fusion.refs_0_), channel_id=1, source_target_pairs={{0,1},{1,0},{2,3},{3,2},{4,5},{5,4},{6,7},{7,6},{8,9},{9,8},{10,11... | collective-permute-start | bytes 1228808 | tf_op jit(solution)/shard_map/ppermute | solution.py:353
  77.5 2.0 %collective-permute-start.7 = (bf16[1600,128]{1,0:T(8,128)(2,1)S(1)}, bf16[1600,128]{1,0:T(8,128)(2,1)S(1)}, u32[]{:S(2)}, u32[]{:S(2)}) collective-permute-start(bf16[1600,128]{1,0:T(8,128)(2,1)S(1)} %collective-permute-done.5.refs_1_), channel_id=1, source_target_pairs={{0,1},{1,0},{2,3},{3,2},{4,5},{5,4},{6,7},{7,6},{8,9},{9,8},{10,11... | collective-permute-start | bytes 1228808 | tf_op jit(solution)/shard_map/ppermute | solution.py:353
  94.1 1.0 %copy-start.17 = (bf16[4,256,512]{2,1,0:T(8,128)(2,1)}, bf16[4,256,512]{2,1,0:T(8,128)(2,1)S(1)}, u32[]{:S(2)}) copy-start(bf16[4,256,512]{2,1,0:T(8,128)(2,1)S(1)} %get-tuple-element.82) | copy-start | bytes 3145732

commit v2 on v0

v2 whole, which is shorter than its diff:
```python
import functools

import jax
import jax.numpy as jnp
from jax import lax
from jax.experimental import pallas as pl
from jax.experimental.pallas import tpu as pltpu
from jax.sharding import PartitionSpec as P

ROW_GROUPS = 4
COL_PARTS = 2
PIECES = 8
SLOTS = 2
SPILL = 3
SPILL_BLOCKS = 2
INFO = 16
TABLE = 256

VMEM = pl.BlockSpec(memory_space=pltpu.VMEM)
SMEM = pl.BlockSpec(memory_space=pltpu.SMEM)
ANY = pl.BlockSpec(memory_space=pl.ANY)
HBM = pl.BlockSpec(memory_space=pltpu.HBM)


def params(mib):
    return pltpu.CompilerParams(vmem_limit_bytes=mib * 2**20)


def exchange_all(sigma_share, route_owner, route_block):
    row_count, block_count, states = sigma_share.shape
    group_rows = row_count // ROW_GROUPS
    width_part = states // COL_PARTS
    pieces = sigma_share.reshape(ROW_GROUPS, group_rows, block_count, COL_PARTS, width_part)
    pieces = pieces.transpose(2, 0, 3, 1, 4).reshape(block_count * PIECES, group_rows * width_part)
    owners = route_owner[0].reshape(-1)
    target_code = (route_block[0] * PIECES + jnp.arange(PIECES, dtype=jnp.int32)[None, :]).reshape(-1)
    peer_count = lax.axis_size("sector")
    capacity = min(block_count, max(2, (2 * block_count * PIECES + peer_count - 1) // peer_count))
    is_owner = (owners[:, None] == jnp.arange(peer_count, dtype=jnp.int32)[None, :]).astype(jnp.int32)
    before = jnp.cumsum(is_owner, axis=0) - is_owner
    position = jnp.sum(before * is_owner, axis=1)
    destination = owners * capacity + position
    slot_ids = jnp.arange(peer_count * capacity, dtype=jnp.int32)
    placing = slot_ids[:, None] == destination[None, :]
    send_data = jnp.dot(placing.astype(jnp.bfloat16), pieces, preferred_element_type=jnp.float32).astype(jnp.bfloat16)
    send_data = send_data.reshape(peer_count, capacity, group_rows * width_part)
    send_code = (jnp.sum(placing.astype(jnp.int32) * (target_code + 1)[None, :], axis=1) - 1).reshape(peer_count, capacity)
    arrived_data, arrived_code = (
        lax.all_to_all(send_data, "sector", split_axis=0, concat_axis=0, tiled=True),
        lax.all_to_all(send_code, "sector", split_axis=0, concat_axis=0, tiled=True),
    )
    arrived_data = arrived_data.reshape(peer_count * capacity, group_rows * width_part)
    arrived_code = arrived_code.reshape(-1)
    targets = jnp.arange(block_count * PIECES, dtype=jnp.int32)
    collect = (arrived_code[None, :] == targets[:, None]).astype(jnp.bfloat16)
    landed = jnp.dot(collect, arrived_data, preferred_element_type=jnp.float32).astype(jnp.bfloat16)
    landed = landed.reshape(block_count, ROW_GROUPS, COL_PARTS, group_rows, width_part)
    return landed.transpose(0, 1, 3, 2, 4).reshape(block_count, row_count, states)


def general(wavefunction, left_env, right_env, mpo_mask, block_size, route_owner, route_block):
    states = wavefunction.shape[1]
    row_count = states // lax.axis_size("mpo")
    positions = jnp.arange(states, dtype=jnp.int32)
    live_cols = positions[None, :] < block_size[:, None]
    live_mask = live_cols[:, :, None] & live_cols[:, None, :]
    masked = jnp.where(live_mask, wavefunction, jnp.zeros_like(wavefunction))
    right_part = jnp.einsum("bij,bkj->bik", masked, right_env[0], preferred_element_type=jnp.float32).astype(jnp.bfloat16)
    factor = mpo_mask[0].astype(jnp.float32)
    product = jnp.einsum("bij,bjk->ibk", left_env[0], right_part, preferred_element_type=jnp.float32)
    row_share = lax.psum_scatter(
        (product * factor[None, :, None]).astype(jnp.bfloat16), "mpo", scatter_dimension=0, tiled=True
    ).astype(jnp.float32)
    global_rows = lax.axis_index("mpo") * row_count + jnp.arange(row_count, dtype=jnp.int32)
    live_rows = global_rows[:, None] < block_size[None, :]
    share_mask = live_rows[:, :, None] & live_cols[None, :, :]
    sigma_share = jnp.where(share_mask, row_share, jnp.zeros_like(row_share)).astype(jnp.bfloat16)
    return exchange_all(sigma_share, route_owner, route_block)


def route_kernel(peers, blocks, group_rows, width, owner_ref, block_ref, size_ref, behind_ref, sent_ref, info_ref, count):
    first_row = lax.axis_index("mpo") * (ROW_GROUPS * group_rows)
    spill_at = peers * SLOTS
    for i in range(spill_at + 2 * SPILL):
        info_ref[i] = -1
    for i in range(SPILL):
        sent_ref[blocks * PIECES + i] = -1
    for i in range(peers):
        count[i] = 0

    nowhere = TABLE - 2

    def one(step, spilled):
        b, k = blocks - 1 - step // PIECES, step % PIECES
        i = b * PIECES + k
        g, c = k // COL_PARTS, k % COL_PARTS
        size = size_ref[b]
        live = (first_row + g * group_rows < size) & (c * width < size)
        owner = owner_ref[0, b, k]
        pos = count[owner]
        code = block_ref[0, b, k] * PIECES + k
        direct = live & (pos < SLOTS)
        kept = live & (pos >= SLOTS) & (spilled < SPILL)
        sent_ref[i] = jnp.where(direct, owner * SLOTS + pos, -1)
        info_ref[jnp.where(direct, owner * SLOTS + pos, nowhere)] = code
        count[owner] = pos + direct.astype(jnp.int32)
        sent_ref[jnp.where(kept, blocks * PIECES + spilled, nowhere)] = i
        info_ref[jnp.where(kept, spill_at + spilled, nowhere)] = owner
        info_ref[jnp.where(kept, spill_at + SPILL + spilled, nowhere)] = code
        return spilled + (live & (pos >= SLOTS)).astype(jnp.int32)

    spilled = lax.fori_loop(0, blocks * PIECES, one, 0, unroll=PIECES)
    sent_ref[TABLE - 1] = (spilled > SPILL).astype(jnp.int32)


def term_kernel(first, size_ref, mask_ref, wave_ref, left_ref, right_ref, *refs):
    own_ref, send_ref, wave, left, right, own, send, come, go = refs[-9:]
    count, states, _ = wave.shape
    share = states // 2
    rows, width = share // ROW_GROUPS, states // COL_PARTS
    mine = lax.axis_index("mpo").astype(jnp.int32)
    arrive = []
    for n in range(count):
        arrive.append(
            [
                pltpu.make_async_copy(source.at[first + n], target.at[n], come.at[n, i])
                for i, (source, target) in enumerate(((wave_ref, wave), (right_ref, right), (left_ref, left)))
            ]
        )
        for copy in arrive[-1]:
            copy.start()
    row = lax.broadcasted_iota(jnp.int32, (states, states), 0)
    col = lax.broadcasted_iota(jnp.int32, (states, states), 1)
    leave = []
    for n in range(count):
        size = size_ref[first + n]
        active = mask_ref[0, first + n] != 0
        arrive[n][0].wait()
        masked = jnp.where((row < size) & (col < size), wave[n], jnp.zeros_like(wave[n]))
        arrive[n][1].wait()
        part = lax.dot_general(masked, right[n], (((1,), (1,)), ((), ())), preferred_element_type=jnp.float32)
        part = part.astype(jnp.bfloat16)
        arrive[n][2].wait()
        for which, (target, out_ref, half) in enumerate(((send, send_ref, 1 - mine), (own, own_ref, mine))):
            start = pl.multiple_of(half * share, share)
            product = jnp.dot(left[n, pl.ds(start, share), :], part, preferred_element_type=jnp.float32)
            keep = (row[:share] + start < size) & (col[:share] < size) & active
            product = jnp.where(keep, product, 0.0).astype(jnp.bfloat16)
            for k in range(PIECES):
                g, c = k // COL_PARTS, k % COL_PARTS
                target[n, k * rows : (k + 1) * rows, :] = product[g * rows : (g + 1) * rows, c * width : (c + 1) * width]
            to = pl.ds(n * PIECES * rows, PIECES * rows)
            leave.append(pltpu.make_async_copy(target.at[n], out_ref.at[to], go.at[n, which]))
            leave[-1].start()
    for copy in leave:
        copy.wait()


def terms(first, count, sizes, mask, wave, left, right, behind):
    states = wave.shape[1]
    rows, width = states // 2 * COL_PARTS, states // COL_PARTS
    out = jax.ShapeDtypeStruct((count * rows, width), jnp.bfloat16)
    return pl.pallas_call(
        functools.partial(term_kernel, first),
        in_specs=[SMEM] * 2 + [HBM] * 3 + [ANY] * len(behind),
        out_specs=[HBM, HBM],
        out_shape=[out, out],
        scratch_shapes=[pltpu.VMEM((count, states, states), jnp.bfloat16)] * 3
        + [pltpu.VMEM((count, rows, width), jnp.bfloat16)] * 2
        + [pltpu.SemaphoreType.DMA((count, 3)), pltpu.SemaphoreType.DMA((count, 2))],
        compiler_params=params(63),
        name="terms",
    )(sizes, mask, wave, left, right, *behind)


def add(a, b):
    return (a.astype(jnp.float32) + b.astype(jnp.float32)).astype(jnp.bfloat16)


def fetch_spill(rows, blocks, sent_ref, sources, target, sems):
    for j in range(SPILL):
        index = sent_ref[blocks * PIECES + j]
        for b in range(SPILL_BLOCKS):

            def copy(b=b, j=j, index=index):
                at = pl.ds(pl.multiple_of((index - b * PIECES) * rows, rows), rows)
                return pltpu.make_async_copy(sources[b].at[at], target.at[pl.ds(j * rows, rows)], sems.at[j])

            yield (index >= b * PIECES) & (index < (b + 1) * PIECES), copy


def run_copies(copies):
    copies = list(copies)
    for step in ("start", "wait"):
        for there, copy in copies:

            @pl.when(there)
            def _(copy=copy, step=step):
                getattr(copy(), step)()


def spill_kernel(rows, blocks, sent_ref, info_ref, *refs):
    own_refs, other_refs = refs[:SPILL_BLOCKS], refs[SPILL_BLOCKS : 2 * SPILL_BLOCKS]
    out_ref, own, other, own_sems, other_sems = refs[2 * SPILL_BLOCKS + 1 :]
    run_copies(
        [*fetch_spill(rows, blocks, sent_ref, own_refs, own, own_sems), *fetch_spill(rows, blocks, sent_ref, other_refs, other, other_sems)]
    )
    out_ref[: SPILL * rows, :] = add(own[...], other[...])
    lane = lax.broadcasted_iota(jnp.int32, (INFO, TABLE), 1)
    table = jnp.where(lane == TABLE - 1, sent_ref[TABLE - 1], info_ref[...])
    out_ref[SPILL * rows :, :] = table.astype(jnp.float32).astype(jnp.bfloat16)


def join_kernel(count, *refs):
    out_ref, sems = refs[-2:]
    copies = []
    for i, ref in enumerate(refs[:count]):
        copies.append(pltpu.make_async_copy(ref, out_ref.at[pl.ds(i * ref.shape[0], ref.shape[0])], sems.at[i]))
        copies[-1].start()
    for copy in copies:
        copy.wait()


def join(behind, *parts):
    rows, width = parts[0].shape
    return pl.pallas_call(
        functools.partial(join_kernel, len(parts)),
        in_specs=[HBM] * len(parts) + [ANY] * len(behind),
        out_specs=HBM,
        out_shape=jax.ShapeDtypeStruct((len(parts) * rows, width), jnp.bfloat16),
        scratch_shapes=[pltpu.SemaphoreType.DMA((len(parts),))],
        compiler_params=params(63),
        name="join",
    )(*parts, *behind)


def pack_kernel(first, rows, pairs, sent_ref, *refs):
    own_refs, other_refs = refs[:pairs], refs[pairs : 2 * pairs]
    out_ref, stage, sems = refs[-3:]
    done = 0
    copies = []
    for own_ref, other_ref in zip(own_refs, other_refs):
        count = own_ref.shape[0] // rows
        stage[done * rows : (done + count) * rows, :] = add(own_ref[...], other_ref[...])
        for k in range(done, done + count):
            slot = sent_ref[first * PIECES + k]

            def copy(k=k, slot=slot):
                to = pl.ds(pl.multiple_of(slot * rows, rows), rows)
                return pltpu.make_async_copy(stage.at[pl.ds(k * rows, rows)], out_ref.at[to], sems.at[k])

            copies.append((slot >= 0, copy))

            @pl.when(slot >= 0)
            def _(copy=copy):
                copy().start()

        done += count
    for there, copy in copies:

        @pl.when(there)
        def _(copy=copy):
            copy().wait()


def pack(first, sent, own, other, packed, rows, slots, behind):
    total, width = sum(x.shape[0] for x in own), own[0].shape[1]
    before = [] if packed is None else [packed]
    pairs = len(own)
    return pl.pallas_call(
        functools.partial(pack_kernel, first, rows, pairs),
        in_specs=[SMEM] + [VMEM] * (2 * pairs) + [HBM] * len(before) + [ANY] * len(behind),
        out_specs=HBM,
        out_shape=jax.ShapeDtypeStruct((slots * rows, width), jnp.bfloat16),
        scratch_shapes=[pltpu.VMEM((total, width), jnp.bfloat16), pltpu.SemaphoreType.DMA((total // rows,))],
        input_output_aliases={1 + 2 * pairs: 0} if before else {},
        compiler_params=params(63),
        name="pack",
    )(sent, *own, *other, *before, *behind)


def list_kernel(rows, peers, blocks, *refs):
    sets, (order_ref, begin_ref, more_ref, lines, values, table, codes, count, sems) = refs[:4], refs[4:]
    me = lax.axis_index("sector")
    quarter = peers // 4
    chunk = SPILL * rows + INFO
    slots, targets = peers * SLOTS, blocks * PIECES
    copies = []
    for which, ref in enumerate(sets):
        for z in range(quarter):
            i = which * quarter + z
            copies.append(pltpu.make_async_copy(ref.at[pl.ds((z + 1) * chunk - INFO, INFO)], lines.at[i], sems.at[i]))
            copies[-1].start()
    for i in range(targets):
        count[i] = 0
    for i, copy in enumerate(copies):
        copy.wait()
        values[i : i + 1, :] = lines[i].astype(jnp.float32).astype(jnp.int32)[:1, :]
    copy = pltpu.make_async_copy(values, table, sems.at[peers])
    copy.start()
    copy.wait()

    def note(i, code):
        codes[i] = code

        @pl.when(code >= 0)
        def _():
            count[code] += 1

    def source(j, more):
        apart = j ^ me
        line = ((apart & 1) * 2 + ((apart >> 1) & 1)) * quarter + (apart >> 2)
        for slot in range(SLOTS):
            note(j * SLOTS + slot, table[line, me * SLOTS + slot])
        for i in range(SPILL):
            owner = table[j, slots + i]
            note(slots + j * SPILL + i, jnp.where(owner == me, table[j, slots + SPILL + i], -1))
        return jnp.maximum(more, table[j, TABLE - 1])

    more_ref[0] = lax.fori_loop(0, peers, source, 0)

    def total(t, before):
        begin_ref[t] = before
        after = before + count[t]
        count[t] = before
        return after

    begin_ref[targets] = lax.fori_loop(0, targets, total, 0)

    def put(i, _):
        code = codes[i]

        @pl.when(code >= 0)
        def _():
            place = count[code]
            order_ref[place] = i
            count[code] = place + 1

        return 0

    lax.fori_loop(0, slots + peers * SPILL, put, 0)


def land_kernel(rows, peers, order_ref, begin_ref, arrived_ref, *refs):
    sets, (out_ref, held, stage, sems, out_sems) = refs[:4], refs[4:]
    quarter = peers // 4
    chunk = SPILL * rows + INFO
    slots = peers * SLOTS
    blocks, share, states = stage.shape
    width = states // COL_PARTS

    def at(start, unit=rows):
        return pl.ds(pl.multiple_of(start, unit), rows)

    def fetch(i, ref, start):
        return pltpu.make_async_copy(ref.at[at(start, 16)], held.at[at(i * rows)], sems.at[i])

    def begin(n, _):
        i = order_ref[n]

        @pl.when(i < slots)
        def _():
            fetch(i, arrived_ref, i * rows).start()

        @pl.when(i >= slots)
        def _():
            source, j = (i - slots) // SPILL, (i - slots) % SPILL
            for which in range(4):

                @pl.when(source // quarter == which)
                def _(which=which):
                    fetch(i, sets[which], source % quarter * chunk + j * rows).start()

        return 0

    lax.fori_loop(0, begin_ref[blocks * PIECES], begin, 0)

    copies = []
    for t in range(blocks):
        for k in range(PIECES):
            g, c = k // COL_PARTS, k % COL_PARTS
            first, last = begin_ref[t * PIECES + k], begin_ref[t * PIECES + k + 1]

            def more(n, total):
                i = order_ref[n]
                fetch(i, arrived_ref, 0).wait()
                return total + held[at(i * rows), :].astype(jnp.float32)

            total = lax.fori_loop(first, last, more, jnp.zeros((rows, width), jnp.float32))
            stage[t, g * rows : (g + 1) * rows, c * width : (c + 1) * width] = total.astype(jnp.bfloat16)
        copies.append(pltpu.make_async_copy(stage.at[t], out_ref.at[t], out_sems.at[t]))
        copies[-1].start()
    for copy in copies:
        copy.wait()


def two_halves(wavefunction, left_env, right_env, mpo_mask, block_size, route_owner, route_block):
    blocks, states, _ = wavefunction.shape
    share = states // 2
    rows = share // ROW_GROUPS
    width = states // COL_PARTS
    peers = lax.axis_size("sector")
    chunk = SPILL * rows + INFO

    def bf16(*shape):
        return jax.ShapeDtypeStruct(shape, jnp.bfloat16)

    def int32(*shape):
        return jax.ShapeDtypeStruct(shape, jnp.int32)

    def swap(x):
        return lax.ppermute(x, "mpo", [(0, 1), (1, 0)])

    def across(x, apart):
        return lax.ppermute(x, "sector", [(i, i ^ apart) for i in range(peers)])

    own, send, other = [], [], []

    def run(first, count, behind):
        mine, theirs = terms(first, count, block_size, mpo_mask, wavefunction, left_env[0], right_env[0], behind)
        own.append(mine)
        send.append(theirs)
        other.append(swap(theirs))

    for b in range(SPILL_BLOCKS):
        run(b, 1, send[-1:])
    run(SPILL_BLOCKS, blocks - SPILL_BLOCKS, send[-1:])
    sent, info = pl.pallas_call(
        functools.partial(route_kernel, peers, blocks, rows, width),
        in_specs=[SMEM] * 3 + [ANY],
        out_specs=[SMEM, SMEM],
        out_shape=[int32(TABLE)] * 2,
        scratch_shapes=[pltpu.SMEM((peers,), jnp.int32)],
        name="route",
    )(route_owner, route_block, block_size, send[-1])
    spilled = pl.pallas_call(
        functools.partial(spill_kernel, rows, blocks),
        in_specs=[SMEM, VMEM] + [HBM] * (2 * SPILL_BLOCKS) + [ANY],
        out_specs=VMEM,
        out_shape=bf16(chunk, width),
        scratch_shapes=[pltpu.VMEM((SPILL * rows, width), jnp.bfloat16)] * 2 + [pltpu.SemaphoreType.DMA((SPILL,))] * 2,
        compiler_params=params(63),
        name="spill",
    )(sent, info.reshape(1, TABLE), *own[:SPILL_BLOCKS], *other[:SPILL_BLOCKS], send[-1])
    packed = pack(0, sent, own[:SPILL_BLOCKS], other[:SPILL_BLOCKS], None, rows, peers * SLOTS, [])
    near = join([packed], spilled, *[across(spilled, apart) for apart in range(4, peers, 4)])
    beside = across(near, 2)
    sets = [near, beside, across(near, 1), across(beside, 1)]
    packed = pack(SPILL_BLOCKS, sent, own[SPILL_BLOCKS:], other[SPILL_BLOCKS:], packed, rows, peers * SLOTS, [near])
    arrived = lax.all_to_all(packed.reshape(peers, SLOTS * rows, width), "sector", split_axis=0, concat_axis=0, tiled=True)
    arrived = arrived.reshape(peers * SLOTS * rows, width)

    pieces = peers * (SLOTS + SPILL)
    order, begin, more = pl.pallas_call(
        functools.partial(list_kernel, rows, peers, blocks),
        in_specs=[HBM] * 4,
        out_specs=[SMEM] * 3,
        out_shape=[int32(pieces), int32(blocks * PIECES + 1), int32(1)],
        scratch_shapes=[
            pltpu.VMEM((peers, INFO, TABLE), jnp.bfloat16),
            pltpu.VMEM((peers, TABLE), jnp.int32),
            pltpu.SMEM((peers, TABLE), jnp.int32),
            pltpu.SMEM((pieces,), jnp.int32),
            pltpu.SMEM((blocks * PIECES,), jnp.int32),
            pltpu.SemaphoreType.DMA((peers + 1,)),
        ],
        compiler_params=params(63),
        cost_estimate=pl.CostEstimate(flops=16000000000, bytes_accessed=0, transcendentals=0),
        name="list",
    )(*sets)

    def fast(order, begin, arrived, sets, *_):
        return pl.pallas_call(
            functools.partial(land_kernel, rows, peers),
            in_specs=[SMEM, SMEM] + [HBM] * 5,
            out_specs=HBM,
            out_shape=bf16(blocks, share, states),
            scratch_shapes=[
                pltpu.VMEM((pieces * rows, width), jnp.bfloat16),
                pltpu.VMEM((blocks, share, states), jnp.bfloat16),
                pltpu.SemaphoreType.DMA((pieces,)),
                pltpu.SemaphoreType.DMA((blocks,)),
            ],
            compiler_params=params(63),
            name="land",
        )(order, begin, arrived, *sets)

    def slow(order, begin, arrived, sets, own, other):
        sums = jnp.concatenate([add(a, b) for a, b in zip(own, other)], axis=0)
        sums = sums.reshape(blocks, ROW_GROUPS, COL_PARTS, rows, width).transpose(1, 3, 0, 2, 4)
        return exchange_all(sums.reshape(share, blocks, states), route_owner, route_block)

    more = jnp.maximum(more, swap(more))
    return lax.cond(more[0] <= 0, fast, slow, order, begin, arrived, tuple(sets), tuple(own), tuple(other))


def solution(mesh):
    placed = (
        P("sector", None, None),
        P("mpo", "sector", None, None),
        P("mpo", "sector", None, None),
        P("mpo", "sector"),
        P("sector"),
        P("mpo", "sector", None),
        P("mpo", "sector", None),
    )

    def per_device(wavefunction, *rest):
        states = wavefunction.shape[1]
        peers = mesh.shape["sector"]
        fits = (
            mesh.shape["mpo"] == 2
            and peers >= 8
            and peers & (peers - 1) == 0
            and wavefunction.shape[0] == SLOTS + SPILL_BLOCKS
            and states // COL_PARTS == TABLE
            and states // (2 * ROW_GROUPS) % 16 == 0
            and peers * SLOTS + 2 * SPILL < TABLE
        )
        return (two_halves if fits else general)(wavefunction, *rest)

    return jax.shard_map(per_device, mesh=mesh, in_specs=placed, out_specs=P("sector", "mpo", None), check_vma=False)
```

time: 129 us -> 70.7 us (0.55); the launches traced: 127 us -> 70.1 us
  waiting for transfers between devices: 69.3 us -> 23.1 us
  Pallas kernels: 0 us -> 28.1 us
  local copies, waits for them, and re-layouts: 16.6 us -> 0.78 us
  between operations: 13.5 us -> 1.38 us
  matrix products: 10.1 us -> 0 us
  other arithmetic: 4.28 us -> 0 us
  starting transfers between devices: 13 us -> 16.8 us
    all_to_all x2 -> x1, waiting for transfers between devices: 44.8 us -> 13.5 us  [two_halves(): lax.all_to_all(packed.reshape(peers, SLOTS * rows, width), 'sector', spli...]
    pallas_call x0 -> x10, Pallas kernels: none -> 28.1 us  [the longest x3 11.6 us: terms(): pl.pallas_call(functools.partial(term_kernel, first), in_specs=[SMEM] * 2...]
    reduce_scatter x1 -> x0, waiting for transfers between devices: 24.5 us -> none  [per_device(): lax.psum_scatter((product * factor[None, :, None]).astype(jnp.bfloat16),...]
    reshape x4 -> x0, local copies, waits for them, and re-layouts: 10.9 us -> none  [the longest x1 4.11 us: per_device(): send_data = send_data.reshape(peer_count, capacity, group_rows * width_part)]
    dot_general x3 -> x0, matrix products: 10.1 us -> none  [the longest x1 5.97 us: per_device(): jnp.einsum('bij,bjk->ibk', left_rows, right_part, preferred_element_type=...]
    ppermute x0 -> x10, waiting for transfers between devices: none -> 9.64 us  [the longest x6 6.39 us: across(): return lax.ppermute(x, 'sector', [(i, i ^ apart) for i in range(peers)])]
    ppermute x0 -> x10, starting transfers between devices: none -> 9.15 us  [the longest x6 6.2 us: across(): return lax.ppermute(x, 'sector', [(i, i ^ apart) for i in range(peers)])]
    all_to_all x2 -> x1, starting transfers between devices: 13 us -> 7.64 us  [two_halves(): lax.all_to_all(packed.reshape(peers, SLOTS * rows, width), 'sector', spli...]
  transfers between devices with their start and end apart: 3 -> 11, of which waited for: 2 -> 7; matrix products, arithmetic and copies ran while one was open for 11% -> 0% of each run, Pallas kernels for 0% -> 31%
where the time goes in v2:
time: 70.7 us; the launch traced here: 70.1 us
  Pallas kernels  28.1 us (40%)
  waiting for transfers between devices  23.1 us (33%)
  starting transfers between devices  16.8 us (24%)
  between operations  1.38 us (2%)
  local copies, waits for them, and re-layouts  0.78 us (1%)
    all_to_all x1, waiting for transfers between devices, two_halves(): lax.all_to_all(packed.reshape(peers, SLOTS * rows, width), 'sector', spli...  13.5 us
    pallas_call x3, Pallas kernels, terms(): pl.pallas_call(functools.partial(term_kernel, first), in_specs=[SMEM] * 2...  11.6 us
    all_to_all x1, starting transfers between devices, two_halves(): lax.all_to_all(packed.reshape(peers, SLOTS * rows, width), 'sector', spli...  7.64 us
    ppermute x6, waiting for transfers between devices, across(): return lax.ppermute(x, 'sector', [(i, i ^ apart) for i in range(peers)])  6.39 us
    ppermute x6, starting transfers between devices, across(): return lax.ppermute(x, 'sector', [(i, i ^ apart) for i in range(peers)])  6.2 us
    pallas_call x1, Pallas kernels, two_halves(): pl.pallas_call(functools.partial(list_kernel, rows, peers, blocks), in_sp...  4.41 us
    pallas_call x2, Pallas kernels, pack(): pl.pallas_call(functools.partial(pack_kernel, first, rows, pairs), in_spe...  4.09 us
    ppermute x4, waiting for transfers between devices, swap(): return lax.ppermute(x, 'mpo', [(0, 1), (1, 0)])  3.25 us
  transfers between devices with their start and end apart: 11, of which 7 were waited for; matrix products, arithmetic and copies ran while one was open for 0% of the time, Pallas kernels for 31%

profile of v2, /device:TPU:9, one launch (start us, length us, event | category | flops | bytes accessed | tf_op | source)
XLA Modules:
  0.0 70.1 jit_solution(14279996440148909668)
XLA Ops:
  0.0 3.4 %terms.3 = (bf16[512,256]{1,0:T(8,128)(2,1)S(1)}, bf16[512,256]{1,0:T(8,128)(2,1)}) custom-call(s32[4]{0:T(128)} %size_ref.7, s32[1,4]{1,0:T(1,128)} %mask_ref.5, bf16[4,512,512]{2,1,0:T(8,128)(2,1)} %wave_ref.5, bf16[4,512,512]{2,1,0:T(8,128)(2,1)} %bitcast.14, bf16[4,512,512]{2,1,0:T(8,128)(2,1)} %bitcast.17), custom_call_target="tpu_custom_call" | custom-call | tf_op jit(solution)/shard_map/terms/pallas_call | solution.py:163
  3.4 1.3 %collective-permute-start = (bf16[512,256]{1,0:T(8,128)(2,1)}, bf16[512,256]{1,0:T(8,128)(2,1)S(1)}, u32[]{:S(2)}, u32[]{:S(2)}) collective-permute-start(bf16[512,256]{1,0:T(8,128)(2,1)} %get-tuple-element.65.refs_0_), channel_id=1, source_target_pairs={{0,16},{16,0},{1,17},{17,1},{2,18},{18,2},{3,19},{19,3},{4,20},{20... | collective-permute-start | bytes 786440 | tf_op jit(solution)/shard_map/ppermute | solution.py:412
  4.7 3.5 %terms.4 = (bf16[512,256]{1,0:T(8,128)(2,1)S(1)}, bf16[512,256]{1,0:T(8,128)(2,1)}) custom-call(s32[4]{0:T(128)} %size_ref.7, s32[1,4]{1,0:T(1,128)} %mask_ref.5, bf16[4,512,512]{2,1,0:T(8,128)(2,1)} %wave_ref.5, bf16[4,512,512]{2,1,0:T(8,128)(2,1)} %bitcast.15, bf16[4,512,512]{2,1,0:T(8,128)(2,1)} %bitcast.18, bf16[512,256]{1,0:T(8,128)(2,1)} %get-tuple-element.65.refs_0_), custom_call_target="tpu_custom_call" | custom-call | tf_op jit(solution)/shard_map/terms/pallas_call | solution.py:163
  8.2 0.0 copy-start
  8.2 0.0 copy-start.3
  8.2 0.0 copy-start.4
  8.2 0.3 collective-permute-start.1
  8.5 4.7 %terms.5 = (bf16[1024,256]{1,0:T(8,128)(2,1)}, bf16[1024,256]{1,0:T(8,128)(2,1)}) custom-call(s32[4]{0:T(128)} %size_ref.7, s32[1,4]{1,0:T(1,128)} %mask_ref.5, bf16[4,512,512]{2,1,0:T(8,128)(2,1)} %wave_ref.5, bf16[4,512,512]{2,1,0:T(8,128)(2,1)} %bitcast.16, bf16[4,512,512]{2,1,0:T(8,128)(2,1)} %bitcast.19, bf16[512,256]{1,0:T(8,128)(2,1)} %get-tuple-element.66.refs_0_), custom_call_target="tpu_custom_call" | custom-call | tf_op jit(solution)/shard_map/terms/pallas_call | solution.py:163
  13.3 1.3 %collective-permute-start.9 = (bf16[1024,256]{1,0:T(8,128)(2,1)}, bf16[1024,256]{1,0:T(8,128)(2,1)}, u32[]{:S(2)}, u32[]{:S(2)}) collective-permute-start(bf16[1024,256]{1,0:T(8,128)(2,1)} %get-tuple-element.67.behind_ref.refs_4_), channel_id=1, source_target_pairs={{0,16},{16,0},{1,17},{17,1},{2,18},{18,2},{3,19},{19,3},{4,20},{20... | collective-permute-start | bytes 1572872 | tf_op jit(solution)/shard_map/ppermute | solution.py:412
  14.6 0.0 copy-done.3
  14.6 0.0 copy-done.4
  14.6 2.2 %route.1 = (s32[256]{0:T(256)}, s32[256]{0:T(256)}) custom-call(s32[1,4,8]{2,1,0:T(4,128)S(1)} %copy-done.3, s32[1,4,8]{2,1,0:T(4,128)S(1)} %copy-done.4, s32[4]{0:T(128)} %size_ref.7, bf16[1024,256]{1,0:T(8,128)(2,1)} %get-tuple-element.67.behind_ref.refs_4_), custom_call_target="tpu_custom_call" | custom-call | tf_op jit(solution)/shard_map/route/pallas_call | solution.py:428
  16.7 0.0 collective-permute-done.refs_2_
  16.7 0.3 collective-permute-done.1.refs_3_
  17.0 1.5 %spill.1.refs_0_ = bf16[208,256]{1,0:T(8,128)(2,1)} custom-call(s32[256]{0:T(256)} %get-tuple-element.68.sent_ref, s32[1,256]{1,0:T(1,128)} %bitcast.23, bf16[512,256]{1,0:T(8,128)(2,1)S(1)} %get-tuple-element.70.refs_0_, bf16[512,256]{1,0:T(8,128)(2,1)S(1)} %get-tuple-element.71.refs_1_, bf16[512,256]{1,0:T(8,128)(2,1)S(1)} %collective-permute-done.refs_2_, ...), custom_call_target="tpu_custom_call" | custom-call | tf_op jit(solution)/shard_map/spill/pallas_call | solution.py:436
  18.5 2.2 %collective-permute-start.4 = (bf16[208,256]{1,0:T(8,128)(2,1)}, bf16[208,256]{1,0:T(8,128)(2,1)S(1)}, u32[]{:S(2)}, u32[]{:S(2)}) collective-permute-start(bf16[208,256]{1,0:T(8,128)(2,1)} %spill.1.refs_0_), channel_id=1, source_target_pairs={{0,12},{1,13},{2,14},{3,15},{4,8},{5,9},{6,10},{7,11},{8,4},{9,5},... | collective-permute-start | bytes 319496 | tf_op jit(solution)/shard_map/ppermute | solution.py:415
  20.7 0.7 collective-permute-start.3
  21.3 0.7 collective-permute-start.2
  22.0 0.0 copy-done
  22.0 1.9 %pack.2.refs_4_.refs_2_ = bf16[2048,256]{1,0:T(8,128)(2,1)} custom-call(s32[256]{0:T(256)} %get-tuple-element.68.sent_ref, bf16[512,256]{1,0:T(8,128)(2,1)S(1)} %get-tuple-element.70.refs_0_, bf16[512,256]{1,0:T(8,128)(2,1)S(1)} %get-tuple-element.71.refs_1_, bf16[512,256]{1,0:T(8,128)(2,1)S(1)} %collective-permute-done.refs_2_, ...), custom_call_target="tpu_custom_call" | custom-call | tf_op jit(solution)/shard_map/pack/pallas_call | solution.py:270
  24.0 0.6 collective-permute-done.4.refs_3_
  24.5 0.0 copy-start.2
  24.5 4.9 %collective-permute-done.3.refs_2_ = bf16[208,256]{1,0:T(8,128)(2,1)} collective-permute-done((bf16[208,256]{1,0:T(8,128)(2,1)}, bf16[208,256]{1,0:T(8,128)(2,1)}, u32[]{:S(2)}, u32[]{:S(2)}) %collective-permute-start.3) | collective-permute-done | bytes 106528 | tf_op jit(solution)/shard_map/ppermute | solution.py:415
  29.4 0.0 copy-done.2
  29.4 0.0 collective-permute-done.2.refs_1_
  29.4 1.1 %join.1.refs_0_.refs_3_ = bf16[832,256]{1,0:T(8,128)(2,1)S(1)} custom-call(bf16[208,256]{1,0:T(8,128)(2,1)} %spill.1.refs_0_, bf16[208,256]{1,0:T(8,128)(2,1)} %collective-permute-done.2.refs_1_, bf16[208,256]{1,0:T(8,128)(2,1)} %collective-permute-done.3.refs_2_, bf16[208,256]{1,0:T(8,128)(2,1)} %copy-done.2, bf16[2048,256]{1,0:T(8,128)(2,1)} %pack.2.refs_4_.refs_2_), custom_call_target="tpu_custom_call" | custom-call | tf_op jit(solution)/shard_map/join/pallas_call | solution.py:226
  30.5 1.6 %collective-permute-start.5 = (bf16[832,256]{1,0:T(8,128)(2,1)S(1)}, bf16[832,256]{1,0:T(8,128)(2,1)}, u32[]{:S(2)}, u32[]{:S(2)}) collective-permute-start(bf16[832,256]{1,0:T(8,128)(2,1)S(1)} %join.1.refs_0_.refs_3_), channel_id=1, source_target_pairs={{0,2},{1,3},{2,0},{3,1},{4,6},{5,7},{6,4},{7,5},{8,10},{9,11},{10,... | collective-permute-start | bytes 1277960 | tf_op jit(solution)/shard_map/ppermute | solution.py:415
  32.1 0.0 collective-permute-done.9.refs_1_
  32.1 2.2 %pack.3 = bf16[2048,256]{1,0:T(8,128)(2,1)} custom-call(s32[256]{0:T(256)} %get-tuple-element.68.sent_ref, bf16[1024,256]{1,0:T(8,128)(2,1)} %get-tuple-element.73.refs_0_, bf16[1024,256]{1,0:T(8,128)(2,1)} %collective-permute-done.9.refs_1_, bf16[2048,256]{1,0:T(8,128)(2,1)} %pack.2.refs_4_.refs_2_, ...), custom_call_target="tpu_custom_call", output_to_operand_aliasing={{}: (3, {})} | custom-call | tf_op jit(solution)/shard_map/pack/pallas_call | solution.py:270
  34.3 7.6 %all-to-all-start.2 = ((bf16[16,128,256]{2,1,0:T(8,128)(2,1)}), bf16[16,128,256]{2,1,0:T(8,128)(2,1)}, u32[]{:S(2)}, u32[]{:S(2)}) async-start(bf16[16,128,256]{2,1,0:T(8,128)(2,1)} %bitcast.20), calls=%async_computation.2 | async-start | bytes 2097152 | tf_op jit(solution)/shard_map/all_to_all | solution.py:450
  41.9 0.4 collective-permute-start.6
  42.3 0.0 collective-permute-done.5.refs_1_
  42.3 0.7 collective-permute-start.7
  43.0 0.7 %collective-permute-done.6.refs_2_ = bf16[832,256]{1,0:T(8,128)(2,1)S(1)} collective-permute-done((bf16[832,256]{1,0:T(8,128)(2,1)S(1)}, bf16[832,256]{1,0:T(8,128)(2,1)S(1)}, u32[]{:S(2)}, u32[]{:S(2)}) %collective-permute-start.6) | collective-permute-done | bytes 426016 | tf_op jit(solution)/shard_map/ppermute | solution.py:415
  43.7 0.0 copy-start.1
  43.7 0.8 %copy-done.1 = bf16[832,256]{1,0:T(8,128)(2,1)} copy-done((bf16[832,256]{1,0:T(8,128)(2,1)}, bf16[832,256]{1,0:T(8,128)(2,1)S(1)}, u32[]{:S(2)}) %copy-start.1) | copy-done | bytes 426008
  44.4 0.3 collective-permute-done.7.refs_3_
  44.7 4.4 %list.1 = (s32[80]{0:T(128)S(1)}, s32[33]{0:T(128)S(1)}, s32[1]{0:T(128)}) custom-call(bf16[832,256]{1,0:T(8,128)(2,1)S(1)} %join.1.refs_0_.refs_3_, bf16[832,256]{1,0:T(8,128)(2,1)} %collective-permute-done.5.refs_1_, bf16[832,256]{1,0:T(8,128)(2,1)} %copy-done.1, bf16[832,256]{1,0:T(8,128)(2,1)} %collective-permute-done.7.refs_3_), custom_call_target="tpu_custom_call" | custom-call | flops 16000000000 | tf_op jit(solution)/shard_map/list/pallas_call | solution.py:454
  49.1 0.1 collective-permute-start.8
  49.2 3.0 %collective-permute-done.8 = s32[1]{0:T(128)} collective-permute-done((s32[1]{0:T(128)}, s32[1]{0:T(128)}, u32[]{:S(2)}, u32[]{:S(2)}) %collective-permute-start.8) | collective-permute-done | bytes 36 | tf_op jit(solution)/shard_map/ppermute | solution.py:412
  53.4 13.5 %all-to-all-done.2 = bf16[16,128,256]{2,1,0:T(8,128)(2,1)} async-done(((bf16[16,128,256]{2,1,0:T(8,128)(2,1)}), bf16[16,128,256]{2,1,0:T(8,128)(2,1)}, u32[]{:S(2)}, u32[]{:S(2)}) %all-to-all-start.2) | async-done | bytes 1048608 | tf_op jit(solution)/shard_map/all_to_all | solution.py:450
  66.9 3.2 %conditional.1 = (bf16[4,256,512]{2,1,0:T(8,128)(2,1)}) conditional(s32[]{:T(128)} %bitcast.6, (s32[1,4,8]{2,1,0:T(4,128)S(1)}, s32[1,4,8]{2,1,0:T(4,128)S(1)}, bf16[512,256]{1,0:T(8,128)(2,1)S(1)}, bf16[512,256]{1,0:T(8,128)(2,1)S(1)}, bf16[512,256]{1,0:T(8,128)(2,1)}, /*index=5*/bf16[512,256]{1,0:T(8,128)(2,1)}, bf16[1024,256]{1,0:T(8,128)(2,1)}, ...), branch_computations={%region_0.4_spmd, %region_4.5_spmd} | conditional | flops 141063296 | bytes 34633176 | solution.py:494
  66.9 3.2 %land.1 = bf16[4,256,512]{2,1,0:T(8,128)(2,1)} custom-call(s32[80]{0:T(128)S(1)} %get-tuple-element.47.order_ref, s32[33]{0:T(128)S(1)} %get-tuple-element.48.begin_ref, bf16[2048,256]{1,0:T(8,128)(2,1)} %bitcast.2.arrived_ref, bf16[832,256]{1,0:T(8,128)(2,1)S(1)} %get-tuple-element.50.refs_0_, bf16[832,256]{1,0:T(8,128)(2,1)} %get-tuple-element.51.refs_1_, ...), custom_call_target="tpu_custom_call" | custom-call | tf_op jit(solution)/shard_map/cond/branch_1_fun/land/pallas_call | solution.py:473
Async XLA Ops:
  3.4 13.3 %collective-permute-start = (bf16[512,256]{1,0:T(8,128)(2,1)}, bf16[512,256]{1,0:T(8,128)(2,1)S(1)}, u32[]{:S(2)}, u32[]{:S(2)}) collective-permute-start(bf16[512,256]{1,0:T(8,128)(2,1)} %get-tuple-element.65.refs_0_), channel_id=1, source_target_pairs={{0,16},{16,0},{1,17},{17,1},{2,18},{18,2},{3,19},{19,3},{4,20},{20... | collective-permute-start | bytes 786440 | tf_op jit(solution)/shard_map/ppermute | solution.py:412
  8.2 13.8 %copy-start = (bf16[512,256]{1,0:T(8,128)(2,1)}, bf16[512,256]{1,0:T(8,128)(2,1)S(1)}, u32[]{:S(2)}) copy-start(bf16[512,256]{1,0:T(8,128)(2,1)S(1)} %get-tuple-element.71.refs_1_) | copy-start | bytes 786436
  8.2 6.4 %copy-start.3 = (s32[1,4,8]{2,1,0:T(4,128)S(1)}, s32[1,4,8]{2,1,0:T(4,128)}, u32[]{:S(2)}) copy-start(s32[1,4,8]{2,1,0:T(4,128)} %owner_ref.1) | copy-start | bytes 388
  8.2 6.4 %copy-start.4 = (s32[1,4,8]{2,1,0:T(4,128)S(1)}, s32[1,4,8]{2,1,0:T(4,128)}, u32[]{:S(2)}) copy-start(s32[1,4,8]{2,1,0:T(4,128)} %block_ref.1) | copy-start | bytes 388
  8.2 8.8 %collective-permute-start.1 = (bf16[512,256]{1,0:T(8,128)(2,1)}, bf16[512,256]{1,0:T(8,128)(2,1)}, u32[]{:S(2)}, u32[]{:S(2)}) collective-permute-start(bf16[512,256]{1,0:T(8,128)(2,1)} %get-tuple-element.66.refs_0_), channel_id=1, source_target_pairs={{0,16},{16,0},{1,17},{17,1},{2,18},{18,2},{3,19},{19,3},{4,20},{20... | collective-permute-start | bytes 786440 | tf_op jit(solution)/shard_map/ppermute | solution.py:412
  13.3 18.8 %collective-permute-start.9 = (bf16[1024,256]{1,0:T(8,128)(2,1)}, bf16[1024,256]{1,0:T(8,128)(2,1)}, u32[]{:S(2)}, u32[]{:S(2)}) collective-permute-start(bf16[1024,256]{1,0:T(8,128)(2,1)} %get-tuple-element.67.behind_ref.refs_4_), channel_id=1, source_target_pairs={{0,16},{16,0},{1,17},{17,1},{2,18},{18,2},{3,19},{19,3},{4,20},{20... | collective-permute-start | bytes 1572872 | tf_op jit(solution)/shard_map/ppermute | solution.py:412
  18.5 6.0 %collective-permute-start.4 = (bf16[208,256]{1,0:T(8,128)(2,1)}, bf16[208,256]{1,0:T(8,128)(2,1)S(1)}, u32[]{:S(2)}, u32[]{:S(2)}) collective-permute-start(bf16[208,256]{1,0:T(8,128)(2,1)} %spill.1.refs_0_), channel_id=1, source_target_pairs={{0,12},{1,13},{2,14},{3,15},{4,8},{5,9},{6,10},{7,11},{8,4},{9,5},... | collective-permute-start | bytes 319496 | tf_op jit(solution)/shard_map/ppermute | solution.py:415
  20.7 8.7 %collective-permute-start.3 = (bf16[208,256]{1,0:T(8,128)(2,1)}, bf16[208,256]{1,0:T(8,128)(2,1)}, u32[]{:S(2)}, u32[]{:S(2)}) collective-permute-start(bf16[208,256]{1,0:T(8,128)(2,1)} %spill.1.refs_0_), channel_id=1, source_target_pairs={{0,8},{1,9},{2,10},{3,11},{4,12},{5,13},{6,14},{7,15},{8,0},{9,1},... | collective-permute-start | bytes 319496 | tf_op jit(solution)/shard_map/ppermute | solution.py:415
  21.3 8.0 %collective-permute-start.2 = (bf16[208,256]{1,0:T(8,128)(2,1)}, bf16[208,256]{1,0:T(8,128)(2,1)}, u32[]{:S(2)}, u32[]{:S(2)}) collective-permute-start(bf16[208,256]{1,0:T(8,128)(2,1)} %spill.1.refs_0_), channel_id=1, source_target_pairs={{0,4},{1,5},{2,6},{3,7},{4,0},{5,1},{6,2},{7,3},{8,12},{9,13},{10,... | collective-permute-start | bytes 319496 | tf_op jit(solution)/shard_map/ppermute | solution.py:415
  24.5 4.9 %copy-start.2 = (bf16[208,256]{1,0:T(8,128)(2,1)}, bf16[208,256]{1,0:T(8,128)(2,1)S(1)}, u32[]{:S(2)}) copy-start(bf16[208,256]{1,0:T(8,128)(2,1)S(1)} %collective-permute-done.4.refs_3_) | copy-start | bytes 319492
  30.5 11.8 %collective-permute-start.5 = (bf16[832,256]{1,0:T(8,128)(2,1)S(1)}, bf16[832,256]{1,0:T(8,128)(2,1)}, u32[]{:S(2)}, u32[]{:S(2)}) collective-permute-start(bf16[832,256]{1,0:T(8,128)(2,1)S(1)} %join.1.refs_0_.refs_3_), channel_id=1, source_target_pairs={{0,2},{1,3},{2,0},{3,1},{4,6},{5,7},{6,4},{7,5},{8,10},{9,11},{10,... | collective-permute-start | bytes 1277960 | tf_op jit(solution)/shard_map/ppermute | solution.py:415
  34.3 32.6 %all-to-all-start.2 = ((bf16[16,128,256]{2,1,0:T(8,128)(2,1)}), bf16[16,128,256]{2,1,0:T(8,128)(2,1)}, u32[]{:S(2)}, u32[]{:S(2)}) async-start(bf16[16,128,256]{2,1,0:T(8,128)(2,1)} %bitcast.20), calls=%async_computation.2 | async-start | bytes 2097152 | tf_op jit(solution)/shard_map/all_to_all | solution.py:450
  41.9 1.8 %collective-permute-start.6 = (bf16[832,256]{1,0:T(8,128)(2,1)S(1)}, bf16[832,256]{1,0:T(8,128)(2,1)S(1)}, u32[]{:S(2)}, u32[]{:S(2)}) collective-permute-start(bf16[832,256]{1,0:T(8,128)(2,1)S(1)} %join.1.refs_0_.refs_3_), channel_id=1, source_target_pairs={{0,1},{1,0},{2,3},{3,2},{4,5},{5,4},{6,7},{7,6},{8,9},{9,8},{10,11... | collective-permute-start | bytes 1277960 | tf_op jit(solution)/shard_map/ppermute | solution.py:415
  42.3 2.4 %collective-permute-start.7 = (bf16[832,256]{1,0:T(8,128)(2,1)}, bf16[832,256]{1,0:T(8,128)(2,1)}, u32[]{:S(2)}, u32[]{:S(2)}) collective-permute-start(bf16[832,256]{1,0:T(8,128)(2,1)} %collective-permute-done.5.refs_1_), channel_id=1, source_target_pairs={{0,1},{1,0},{2,3},{3,2},{4,5},{5,4},{6,7},{7,6},{8,9},{9,8},{10,11... | collective-permute-start | bytes 1277960 | tf_op jit(solution)/shard_map/ppermute | solution.py:415
  43.7 0.8 %copy-start.1 = (bf16[832,256]{1,0:T(8,128)(2,1)}, bf16[832,256]{1,0:T(8,128)(2,1)S(1)}, u32[]{:S(2)}) copy-start(bf16[832,256]{1,0:T(8,128)(2,1)S(1)} %collective-permute-done.6.refs_2_) | copy-start | bytes 1277956
  49.1 3.1 %collective-permute-start.8 = (s32[1]{0:T(128)}, s32[1]{0:T(128)}, u32[]{:S(2)}, u32[]{:S(2)}) collective-permute-start(s32[1]{0:T(128)} %get-tuple-element.72), channel_id=1, source_target_pairs={{0,16},{16,0},{1,17},{17,1},{2,18},{18,2},{3,19},{19,3},{4,20},{20... | collective-permute-start | bytes 20 | tf_op jit(solution)/shard_map/ppermute | solution.py:412

commit v3 on v2

--- a/solution.py
+++ b/solution.py
@@ -78,7 +78,7 @@
     return exchange_all(sigma_share, route_owner, route_block)
 
 
-def route_kernel(peers, blocks, group_rows, width, owner_ref, block_ref, size_ref, behind_ref, sent_ref, info_ref, count):
+def route(peers, blocks, group_rows, width, owner_ref, block_ref, size_ref, sent_ref, info_ref, count):
     first_row = lax.axis_index("mpo") * (ROW_GROUPS * group_rows)
     spill_at = peers * SLOTS
     for i in range(spill_at + 2 * SPILL):
@@ -113,8 +113,13 @@
     sent_ref[TABLE - 1] = (spilled > SPILL).astype(jnp.int32)
 
 
-def term_kernel(first, size_ref, mask_ref, wave_ref, left_ref, right_ref, *refs):
-    own_ref, send_ref, wave, left, right, own, send, come, go = refs[-9:]
+def term_kernel(first, plan, size_ref, mask_ref, wave_ref, left_ref, right_ref, *refs):
+    tables = ()
+    if plan:
+        tables = (*refs[:2], size_ref, *refs[-11:-9], refs[-1])
+        refs = refs[2:-11] + refs[-9:-1]
+    wave, left, right, own, send, mark, come, go = refs[-8:]
+    results = refs[-8 - 2 * wave.shape[0] : -8]
     count, states, _ = wave.shape
     share = states // 2
     rows, width = share // ROW_GROUPS, states // COL_PARTS
@@ -129,9 +134,14 @@
         )
         for copy in arrive[-1]:
             copy.start()
+    leave = []
+    if plan:
+        route(*plan, *tables)
+        mark[...] = jnp.full(mark.shape, tables[3][TABLE - 1], jnp.int32).astype(jnp.float32).astype(jnp.bfloat16)
+        leave.append(pltpu.make_async_copy(mark, results[2 * count - 1].at[pl.ds(PIECES * rows, INFO)], go.at[count, 0]))
+        leave[-1].start()
     row = lax.broadcasted_iota(jnp.int32, (states, states), 0)
     col = lax.broadcasted_iota(jnp.int32, (states, states), 1)
-    leave = []
     for n in range(count):
         size = size_ref[first + n]
         active = mask_ref[0, first + n] != 0
@@ -141,7 +151,7 @@
         part = lax.dot_general(masked, right[n], (((1,), (1,)), ((), ())), preferred_element_type=jnp.float32)
         part = part.astype(jnp.bfloat16)
         arrive[n][2].wait()
-        for which, (target, out_ref, half) in enumerate(((send, send_ref, 1 - mine), (own, own_ref, mine))):
+        for which, (target, out_ref, half) in enumerate(((send, results[2 * n + 1], 1 - mine), (own, results[2 * n], mine))):
             start = pl.multiple_of(half * share, share)
             product = jnp.dot(left[n, pl.ds(start, share), :], part, preferred_element_type=jnp.float32)
             keep = (row[:share] + start < size) & (col[:share] < size) & active
@@ -149,28 +159,34 @@
             for k in range(PIECES):
                 g, c = k // COL_PARTS, k % COL_PARTS
                 target[n, k * rows : (k + 1) * rows, :] = product[g * rows : (g + 1) * rows, c * width : (c + 1) * width]
-            to = pl.ds(n * PIECES * rows, PIECES * rows)
-            leave.append(pltpu.make_async_copy(target.at[n], out_ref.at[to], go.at[n, which]))
+            leave.append(pltpu.make_async_copy(target.at[n], out_ref.at[pl.ds(0, PIECES * rows)], go.at[n, which]))
             leave[-1].start()
     for copy in leave:
         copy.wait()
 
 
-def terms(first, count, sizes, mask, wave, left, right, behind):
-    states = wave.shape[1]
-    rows, width = states // 2 * COL_PARTS, states // COL_PARTS
-    out = jax.ShapeDtypeStruct((count * rows, width), jnp.bfloat16)
+def terms(first, count, sizes, mask, wave, left, right, plan, behind):
+    blocks, states, _ = wave.shape
+    group_rows, width = states // 2 // ROW_GROUPS, states // COL_PARTS
+    rows = PIECES * group_rows
+    out = jax.ShapeDtypeStruct((rows, width), jnp.bfloat16)
+    longer = jax.ShapeDtypeStruct((rows + INFO, width), jnp.bfloat16)
+    table = jax.ShapeDtypeStruct((TABLE,), jnp.int32)
+    peers = lax.axis_size("sector")
+    scratch = [pltpu.VMEM((count, states, states), jnp.bfloat16)] * 3 + [pltpu.VMEM((count, rows, width), jnp.bfloat16)] * 2
+    scratch += [pltpu.VMEM((INFO, width), jnp.bfloat16), pltpu.SemaphoreType.DMA((count, 3)), pltpu.SemaphoreType.DMA((count + 1, 2))]
+    if plan:
+        scratch += [pltpu.SMEM((peers,), jnp.int32)]
     return pl.pallas_call(
-        functools.partial(term_kernel, first),
-        in_specs=[SMEM] * 2 + [HBM] * 3 + [ANY] * len(behind),
-        out_specs=[HBM, HBM],
-        out_shape=[out, out],
-        scratch_shapes=[pltpu.VMEM((count, states, states), jnp.bfloat16)] * 3
-        + [pltpu.VMEM((count, rows, width), jnp.bfloat16)] * 2
-        + [pltpu.SemaphoreType.DMA((count, 3)), pltpu.SemaphoreType.DMA((count, 2))],
+        functools.partial(term_kernel, first, (peers, blocks, group_rows, width) if plan else None),
+        in_specs=[SMEM] * 2 + [HBM] * 3 + [SMEM] * len(plan) + [ANY] * len(behind),
+        out_specs=[HBM] * (2 * count) + [SMEM] * len(plan),
+        out_shape=[out] * (2 * count - 1) + [longer if plan else out] + [table] * len(plan),
+        scratch_shapes=scratch,
         compiler_params=params(63),
+        cost_estimate=pl.CostEstimate(flops=3000000000, bytes_accessed=1, transcendentals=0),
         name="terms",
-    )(sizes, mask, wave, left, right, *behind)
+    )(sizes, mask, wave, left, right, *plan, *behind)
 
 
 def add(a, b):
@@ -201,23 +217,33 @@
 
 def spill_kernel(rows, blocks, sent_ref, info_ref, *refs):
     own_refs, other_refs = refs[:SPILL_BLOCKS], refs[SPILL_BLOCKS : 2 * SPILL_BLOCKS]
-    out_ref, own, other, own_sems, other_sems = refs[2 * SPILL_BLOCKS + 1 :]
+    out_ref, own, other, mark, own_sems, other_sems = refs[2 * SPILL_BLOCKS + 1 :]
+    flag = pltpu.make_async_copy(other_refs[-1].at[pl.ds(PIECES * rows, INFO)], mark, other_sems.at[SPILL])
+    flag.start()
     run_copies(
         [*fetch_spill(rows, blocks, sent_ref, own_refs, own, own_sems), *fetch_spill(rows, blocks, sent_ref, other_refs, other, other_sems)]
     )
     out_ref[: SPILL * rows, :] = add(own[...], other[...])
     lane = lax.broadcasted_iota(jnp.int32, (INFO, TABLE), 1)
-    table = jnp.where(lane == TABLE - 1, sent_ref[TABLE - 1], info_ref[...])
+    flag.wait()
+    more = jnp.maximum(mark[...].astype(jnp.float32).astype(jnp.int32), sent_ref[TABLE - 1])
+    table = jnp.where(lane == TABLE - 1, more, info_ref[...])
     out_ref[SPILL * rows :, :] = table.astype(jnp.float32).astype(jnp.bfloat16)
 
 
 def join_kernel(count, *refs):
-    out_ref, sems = refs[-2:]
-    copies = []
-    for i, ref in enumerate(refs[:count]):
-        copies.append(pltpu.make_async_copy(ref, out_ref.at[pl.ds(i * ref.shape[0], ref.shape[0])], sems.at[i]))
-        copies[-1].start()
-    for copy in copies:
+    out_ref, held, come, go = refs[-4:]
+    rows = refs[0].shape[0]
+    arrive = [pltpu.make_async_copy(ref, held.at[pl.ds(i * rows, rows)], come.at[i]) for i, ref in enumerate(refs[:count])]
+    for copy in arrive:
+        copy.start()
+    leave = []
+    for i, copy in enumerate(arrive):
+        copy.wait()
+        at = pl.ds(i * rows, rows)
+        leave.append(pltpu.make_async_copy(held.at[at], out_ref.at[at], go.at[i]))
+        leave[-1].start()
+    for copy in leave:
         copy.wait()
 
 
@@ -225,10 +251,10 @@
     rows, width = parts[0].shape
     return pl.pallas_call(
         functools.partial(join_kernel, len(parts)),
-        in_specs=[HBM] * len(parts) + [ANY] * len(behind),
+        in_specs=[ANY] * (len(parts) + len(behind)),
         out_specs=HBM,
         out_shape=jax.ShapeDtypeStruct((len(parts) * rows, width), jnp.bfloat16),
-        scratch_shapes=[pltpu.SemaphoreType.DMA((len(parts),))],
+        scratch_shapes=[pltpu.VMEM((len(parts) * rows, width), jnp.bfloat16)] + [pltpu.SemaphoreType.DMA((len(parts),))] * 2,
         compiler_params=params(63),
         name="join",
     )(*parts, *behind)
@@ -241,7 +267,7 @@
     copies = []
     for own_ref, other_ref in zip(own_refs, other_refs):
         count = own_ref.shape[0] // rows
-        stage[done * rows : (done + count) * rows, :] = add(own_ref[...], other_ref[...])
+        stage[done * rows : (done + count) * rows, :] = add(own_ref[...], other_ref[: count * rows, :])
         for k in range(done, done + count):
             slot = sent_ref[first * PIECES + k]
 
@@ -291,7 +317,7 @@
             i = which * quarter + z
             copies.append(pltpu.make_async_copy(ref.at[pl.ds((z + 1) * chunk - INFO, INFO)], lines.at[i], sems.at[i]))
             copies[-1].start()
-    for i in range(targets):
+    for i in range(targets + 1):
         count[i] = 0
     for i, copy in enumerate(copies):
         copy.wait()
@@ -301,11 +327,9 @@
     copy.wait()
 
     def note(i, code):
-        codes[i] = code
-
-        @pl.when(code >= 0)
-        def _():
-            count[code] += 1
+        to = jnp.where(code >= 0, code, targets)
+        codes[i] = to
+        count[to] += 1
 
     def source(j, more):
         apart = j ^ me
@@ -317,7 +341,7 @@
             note(slots + j * SPILL + i, jnp.where(owner == me, table[j, slots + SPILL + i], -1))
         return jnp.maximum(more, table[j, TABLE - 1])
 
-    more_ref[0] = lax.fori_loop(0, peers, source, 0)
+    more_ref[0] = lax.fori_loop(0, peers, source, 0, unroll=4)
 
     def total(t, before):
         begin_ref[t] = before
@@ -325,20 +349,16 @@
         count[t] = before
         return after
 
-    begin_ref[targets] = lax.fori_loop(0, targets, total, 0)
+    lax.fori_loop(0, targets + 1, total, 0, unroll=True)
 
     def put(i, _):
         code = codes[i]
-
-        @pl.when(code >= 0)
-        def _():
-            place = count[code]
-            order_ref[place] = i
-            count[code] = place + 1
-
+        place = count[code]
+        order_ref[place] = i
+        count[code] = place + 1
         return 0
 
-    lax.fori_loop(0, slots + peers * SPILL, put, 0)
+    lax.fori_loop(0, slots + peers * SPILL, put, 0, unroll=peers // 2)
 
 
 def land_kernel(rows, peers, order_ref, begin_ref, arrived_ref, *refs):
@@ -416,44 +436,44 @@
 
     own, send, other = [], [], []
 
-    def run(first, count, behind):
-        mine, theirs = terms(first, count, block_size, mpo_mask, wavefunction, left_env[0], right_env[0], behind)
-        own.append(mine)
-        send.append(theirs)
-        other.append(swap(theirs))
+    def run(first, count, plan, behind):
+        made = terms(first, count, block_size, mpo_mask, wavefunction, left_env[0], right_env[0], plan, behind)
+        for n in range(count):
+            own.append(made[2 * n])
+            send.append(made[2 * n + 1])
+            other.append(swap(send[-1]))
+        return made[2 * count :]
 
     for b in range(SPILL_BLOCKS):
-        run(b, 1, send[-1:])
-    run(SPILL_BLOCKS, blocks - SPILL_BLOCKS, send[-1:])
-    sent, info = pl.pallas_call(
-        functools.partial(route_kernel, peers, blocks, rows, width),
-        in_specs=[SMEM] * 3 + [ANY],
-        out_specs=[SMEM, SMEM],
-        out_shape=[int32(TABLE)] * 2,
-        scratch_shapes=[pltpu.SMEM((peers,), jnp.int32)],
-        name="route",
-    )(route_owner, route_block, block_size, send[-1])
+        tables = run(b, 1, [route_owner, route_block] if b == SPILL_BLOCKS - 1 else [], send[-1:])
+    sent, info = tables
+    run(SPILL_BLOCKS, blocks - SPILL_BLOCKS, [], send[-1:])
+
     spilled = pl.pallas_call(
         functools.partial(spill_kernel, rows, blocks),
-        in_specs=[SMEM, VMEM] + [HBM] * (2 * SPILL_BLOCKS) + [ANY],
+        in_specs=[SMEM, VMEM] + [ANY] * (2 * SPILL_BLOCKS + 1),
         out_specs=VMEM,
         out_shape=bf16(chunk, width),
-        scratch_shapes=[pltpu.VMEM((SPILL * rows, width), jnp.bfloat16)] * 2 + [pltpu.SemaphoreType.DMA((SPILL,))] * 2,
+        scratch_shapes=[pltpu.VMEM((SPILL * rows, width), jnp.bfloat16)] * 2
+        + [pltpu.VMEM((INFO, width), jnp.bfloat16)]
+        + [pltpu.SemaphoreType.DMA((SPILL,)), pltpu.SemaphoreType.DMA((SPILL + 1,))],
         compiler_params=params(63),
         name="spill",
     )(sent, info.reshape(1, TABLE), *own[:SPILL_BLOCKS], *other[:SPILL_BLOCKS], send[-1])
-    packed = pack(0, sent, own[:SPILL_BLOCKS], other[:SPILL_BLOCKS], None, rows, peers * SLOTS, [])
-    near = join([packed], spilled, *[across(spilled, apart) for apart in range(4, peers, 4)])
+    last = blocks - 1
+    along = [across(spilled, apart) for apart in range(4, peers, 4)]
+    packed = pack(0, sent, own[:last], other[:last], None, rows, peers * SLOTS, [])
+    packed = pack(last, sent, own[last:], other[last:], packed, rows, peers * SLOTS, [])
+    near = join([packed], spilled, *along)
     beside = across(near, 2)
     sets = [near, beside, across(near, 1), across(beside, 1)]
-    packed = pack(SPILL_BLOCKS, sent, own[SPILL_BLOCKS:], other[SPILL_BLOCKS:], packed, rows, peers * SLOTS, [near])
     arrived = lax.all_to_all(packed.reshape(peers, SLOTS * rows, width), "sector", split_axis=0, concat_axis=0, tiled=True)
     arrived = arrived.reshape(peers * SLOTS * rows, width)
 
     pieces = peers * (SLOTS + SPILL)
     order, begin, more = pl.pallas_call(
         functools.partial(list_kernel, rows, peers, blocks),
-        in_specs=[HBM] * 4,
+        in_specs=[ANY] * 4,
         out_specs=[SMEM] * 3,
         out_shape=[int32(pieces), int32(blocks * PIECES + 1), int32(1)],
         scratch_shapes=[
@@ -461,18 +481,18 @@
             pltpu.VMEM((peers, TABLE), jnp.int32),
             pltpu.SMEM((peers, TABLE), jnp.int32),
             pltpu.SMEM((pieces,), jnp.int32),
-            pltpu.SMEM((blocks * PIECES,), jnp.int32),
+            pltpu.SMEM((blocks * PIECES + 1,), jnp.int32),
             pltpu.SemaphoreType.DMA((peers + 1,)),
         ],
         compiler_params=params(63),
-        cost_estimate=pl.CostEstimate(flops=16000000000, bytes_accessed=0, transcendentals=0),
+        cost_estimate=pl.CostEstimate(flops=12000000000, bytes_accessed=0, transcendentals=0),
         name="list",
     )(*sets)
 
     def fast(order, begin, arrived, sets, *_):
         return pl.pallas_call(
             functools.partial(land_kernel, rows, peers),
-            in_specs=[SMEM, SMEM] + [HBM] * 5,
+            in_specs=[SMEM, SMEM] + [ANY] * 5,
             out_specs=HBM,
             out_shape=bf16(blocks, share, states),
             scratch_shapes=[
@@ -486,11 +506,10 @@
         )(order, begin, arrived, *sets)
 
     def slow(order, begin, arrived, sets, own, other):
-        sums = jnp.concatenate([add(a, b) for a, b in zip(own, other)], axis=0)
+        sums = jnp.concatenate([add(a, b[: a.shape[0]]) for a, b in zip(own, other)], axis=0)
         sums = sums.reshape(blocks, ROW_GROUPS, COL_PARTS, rows, width).transpose(1, 3, 0, 2, 4)
         return exchange_all(sums.reshape(share, blocks, states), route_owner, route_block)
 
-    more = jnp.maximum(more, swap(more))
     return lax.cond(more[0] <= 0, fast, slow, order, begin, arrived, tuple(sets), tuple(own), tuple(other))
 
 

time: 70.7 us -> 69.7 us (0.986)
  starting transfers between devices: 16.8 us -> 18.9 us
  waiting for transfers between devices: 23.1 us -> 21.2 us
  Pallas kernels: 28.1 us -> 26.8 us
    ppermute x6, waiting for transfers between devices: 6.39 us -> 2.84 us  [across(): return lax.ppermute(x, 'sector', [(i, i ^ apart) for i in range(peers)])]
    ppermute x6, starting transfers between devices: 6.2 us -> 9.23 us  [across(): return lax.ppermute(x, 'sector', [(i, i ^ apart) for i in range(peers)])]
    ppermute x4, waiting for transfers between devices: 3.25 us -> 5.42 us  [swap(): return lax.ppermute(x, 'mpo', [(0, 1), (1, 0)])]
    pallas_call x1, Pallas kernels: 4.41 us -> 3.33 us  [two_halves(): pl.pallas_call(functools.partial(list_kernel, rows, peers, blocks), in_sp...]
    all_to_all x1, starting transfers between devices: 7.64 us -> 6.59 us  [two_halves(): lax.all_to_all(packed.reshape(peers, SLOTS * rows, width), 'sector', spli...]
    pallas_call x5 -> x4, Pallas kernels: 14.9 us -> 14.3 us  [the longest x3 12.6 us: terms(): pl.pallas_call(functools.partial(term_kernel, first, (peers, blocks, grou...]
  transfers between devices with their start and end apart: 11 -> 11, of which waited for: 7 -> 6; matrix products, arithmetic and copies ran while one was open for 0% -> 0% of each run, Pallas kernels for 31% -> 26%
where the time goes in v3:
time: 69.7 us; the launch traced here: 69 us
  Pallas kernels  26.8 us (38%)
  waiting for transfers between devices  21.2 us (30%)
  starting transfers between devices  18.9 us (27%)
  local copies, waits for them, and re-layouts  1.38 us (2%)
    all_to_all x1, waiting for transfers between devices, two_halves(): lax.all_to_all(packed.reshape(peers, SLOTS * rows, width), 'sector', spli...  12.9 us
    pallas_call x3, Pallas kernels, terms(): pl.pallas_call(functools.partial(term_kernel, first, (peers, blocks, grou...  12.6 us
    ppermute x6, starting transfers between devices, across(): return lax.ppermute(x, 'sector', [(i, i ^ apart) for i in range(peers)])  9.23 us
    all_to_all x1, starting transfers between devices, two_halves(): lax.all_to_all(packed.reshape(peers, SLOTS * rows, width), 'sector', spli...  6.59 us
    ppermute x4, waiting for transfers between devices, swap(): return lax.ppermute(x, 'mpo', [(0, 1), (1, 0)])  5.42 us
    pallas_call x2, Pallas kernels, pack(): pl.pallas_call(functools.partial(pack_kernel, first, rows, pairs), in_spe...  4.05 us
    pallas_call x1, Pallas kernels, fast(): pl.pallas_call(functools.partial(land_kernel, rows, peers), in_specs=[SME...  3.57 us
    pallas_call x1, Pallas kernels, two_halves(): pl.pallas_call(functools.partial(list_kernel, rows, peers, blocks), in_sp...  3.33 us
  transfers between devices with their start and end apart: 11, of which 6 were waited for; matrix products, arithmetic and copies ran while one was open for 0% of the time, Pallas kernels for 26%

profile of v3, /device:TPU:9, one launch (start us, length us, event | category | flops | bytes accessed | tf_op | source)
XLA Modules:
  0.0 69.0 jit_solution(1533270819911375256)
XLA Ops:
  0.0 0.0 copy-start.4
  0.0 0.0 copy-start.5
  0.0 3.6 %terms.3 = (bf16[512,256]{1,0:T(8,128)(2,1)S(1)}, bf16[512,256]{1,0:T(8,128)(2,1)}) custom-call(s32[4]{0:T(128)} %size_ref.5, s32[1,4]{1,0:T(1,128)} %mask_ref.5, bf16[4,512,512]{2,1,0:T(8,128)(2,1)} %wave_ref.5, bf16[4,512,512]{2,1,0:T(8,128)(2,1)} %bitcast.18, bf16[4,512,512]{2,1,0:T(8,128)(2,1)} %bitcast.21), custom_call_target="tpu_custom_call" | custom-call | flops 3000000000 | bytes 1 | tf_op jit(solution)/shard_map/terms/pallas_call | solution.py:180
  3.6 1.3 %collective-permute-start = (bf16[512,256]{1,0:T(8,128)(2,1)}, bf16[512,256]{1,0:T(8,128)(2,1)S(1)}, u32[]{:S(2)}, u32[]{:S(2)}) collective-permute-start(bf16[512,256]{1,0:T(8,128)(2,1)} %get-tuple-element.73.refs_2_), channel_id=1, source_target_pairs={{0,16},{16,0},{1,17},{17,1},{2,18},{18,2},{3,19},{19,3},{4,20},{20... | collective-permute-start | bytes 786440 | tf_op jit(solution)/shard_map/ppermute | solution.py:432
  4.9 0.0 copy-done.4
  4.9 0.0 copy-done.5
  4.9 4.2 %terms.4 = (bf16[512,256]{1,0:T(8,128)(2,1)}, bf16[528,256]{1,0:T(8,128)(2,1)}, s32[256]{0:T(256)}, s32[256]{0:T(256)}) custom-call(s32[4]{0:T(128)} %size_ref.5, s32[1,4]{1,0:T(1,128)} %mask_ref.5, bf16[4,512,512]{2,1,0:T(8,128)(2,1)} %wave_ref.5, bf16[4,512,512]{2,1,0:T(8,128)(2,1)} %bitcast.19, bf16[4,512,512]{2,1,0:T(8,128)(2,1)} %bitcast.22, ...), custom_call_target="tpu_custom_call" | custom-call | flops 3000000000 | bytes 1 | tf_op jit(solution)/shard_map/terms/pallas_call | solution.py:180
  9.1 0.3 collective-permute-start.1
  9.4 4.8 %terms.5 = (bf16[512,256]{1,0:T(8,128)(2,1)}, bf16[512,256]{1,0:T(8,128)(2,1)}, bf16[512,256]{1,0:T(8,128)(2,1)}, bf16[512,256]{1,0:T(8,128)(2,1)}) custom-call(s32[4]{0:T(128)} %size_ref.5, s32[1,4]{1,0:T(1,128)} %mask_ref.5, bf16[4,512,512]{2,1,0:T(8,128)(2,1)} %wave_ref.5, bf16[4,512,512]{2,1,0:T(8,128)(2,1)} %bitcast.20, bf16[4,512,512]{2,1,0:T(8,128)(2,1)} %bitcast.23, ...), custom_call_target="tpu_custom_call" | custom-call | flops 3000000000 | bytes 1 | tf_op jit(solution)/shard_map/terms/pallas_call | solution.py:180
  14.2 1.3 %collective-permute-start.6 = (bf16[512,256]{1,0:T(8,128)(2,1)}, bf16[512,256]{1,0:T(8,128)(2,1)}, u32[]{:S(2)}, u32[]{:S(2)}) collective-permute-start(bf16[512,256]{1,0:T(8,128)(2,1)} %get-tuple-element.82), channel_id=1, source_target_pairs={{0,16},{16,0},{1,17},{17,1},{2,18},{18,2},{3,19},{19,3},{4,20},{20... | collective-permute-start | bytes 786440 | tf_op jit(solution)/shard_map/ppermute | solution.py:432
  15.5 0.3 collective-permute-start.5
  15.7 0.0 collective-permute-done.refs_2_.refs_3_
  15.7 0.9 %collective-permute-done.1.refs_3_.refs_4_ = bf16[528,256]{1,0:T(8,128)(2,1)S(1)} collective-permute-done((bf16[528,256]{1,0:T(8,128)(2,1)}, bf16[528,256]{1,0:T(8,128)(2,1)S(1)}, u32[]{:S(2)}, u32[]{:S(2)}) %collective-permute-start.1) | collective-permute-done | bytes 270368 | tf_op jit(solution)/shard_map/ppermute | solution.py:432
  16.7 1.6 %spill.1.refs_0_ = bf16[208,256]{1,0:T(8,128)(2,1)} custom-call(s32[256]{0:T(256)} %get-tuple-element.74.sent_ref, s32[1,256]{1,0:T(1,128)} %bitcast.17, bf16[512,256]{1,0:T(8,128)(2,1)S(1)} %get-tuple-element.76.refs_0_, bf16[512,256]{1,0:T(8,128)(2,1)} %get-tuple-element.77.refs_1_, bf16[512,256]{1,0:T(8,128)(2,1)S(1)} %collective-permute-done.refs_2_.refs_3_, ...), custom_call_target="tpu_custom_call" | custom-call | tf_op jit(solution)/shard_map/spill/pallas_call | solution.py:452
  18.3 2.0 %collective-permute-start.4 = (bf16[208,256]{1,0:T(8,128)(2,1)}, bf16[208,256]{1,0:T(8,128)(2,1)S(1)}, u32[]{:S(2)}, u32[]{:S(2)}) collective-permute-start(bf16[208,256]{1,0:T(8,128)(2,1)} %spill.1.refs_0_), channel_id=1, source_target_pairs={{0,12},{1,13},{2,14},{3,15},{4,8},{5,9},{6,10},{7,11},{8,4},{9,5},... | collective-permute-start | bytes 319496 | tf_op jit(solution)/shard_map/ppermute | solution.py:435
  20.2 0.7 collective-permute-start.3
  20.9 0.8 %collective-permute-start.2 = (bf16[208,256]{1,0:T(8,128)(2,1)}, bf16[208,256]{1,0:T(8,128)(2,1)}, u32[]{:S(2)}, u32[]{:S(2)}) collective-permute-start(bf16[208,256]{1,0:T(8,128)(2,1)} %spill.1.refs_0_), channel_id=1, source_target_pairs={{0,4},{1,5},{2,6},{3,7},{4,0},{5,1},{6,2},{7,3},{8,12},{9,13},{10,... | collective-permute-start | bytes 319496 | tf_op jit(solution)/shard_map/ppermute | solution.py:435
  21.7 1.1 %collective-permute-done.6.refs_5_ = bf16[512,256]{1,0:T(8,128)(2,1)} collective-permute-done((bf16[512,256]{1,0:T(8,128)(2,1)}, bf16[512,256]{1,0:T(8,128)(2,1)}, u32[]{:S(2)}, u32[]{:S(2)}) %collective-permute-start.6) | collective-permute-done | bytes 262176 | tf_op jit(solution)/shard_map/ppermute | solution.py:432
  22.8 2.2 %pack.2.refs_2_ = bf16[2048,256]{1,0:T(8,128)(2,1)} custom-call(s32[256]{0:T(256)} %get-tuple-element.74.sent_ref, bf16[512,256]{1,0:T(8,128)(2,1)S(1)} %get-tuple-element.76.refs_0_, bf16[512,256]{1,0:T(8,128)(2,1)} %get-tuple-element.77.refs_1_, bf16[512,256]{1,0:T(8,128)(2,1)} %get-tuple-element.81.refs_2_, ...), custom_call_target="tpu_custom_call" | custom-call | tf_op jit(solution)/shard_map/pack/pallas_call | solution.py:296
  25.0 3.4 %collective-permute-done.5.refs_1_ = bf16[512,256]{1,0:T(8,128)(2,1)} collective-permute-done((bf16[512,256]{1,0:T(8,128)(2,1)}, bf16[512,256]{1,0:T(8,128)(2,1)}, u32[]{:S(2)}, u32[]{:S(2)}) %collective-permute-start.5) | collective-permute-done | bytes 262176 | tf_op jit(solution)/shard_map/ppermute | solution.py:432
  28.4 1.9 %pack.3.refs_4_ = bf16[2048,256]{1,0:T(8,128)(2,1)} custom-call(s32[256]{0:T(256)} %get-tuple-element.74.sent_ref, bf16[512,256]{1,0:T(8,128)(2,1)} %get-tuple-element.80.refs_0_, bf16[512,256]{1,0:T(8,128)(2,1)} %collective-permute-done.5.refs_1_, bf16[2048,256]{1,0:T(8,128)(2,1)} %pack.2.refs_2_), custom_call_target="tpu_custom_call", output_to_operand_aliasing={{}: (3, {})} | custom-call | tf_op jit(solution)/shard_map/pack/pallas_call | solution.py:296
  30.3 0.0 collective-permute-done.4.refs_3_
  30.3 0.0 copy-start.3
  30.3 0.0 collective-permute-done.3.refs_2_
  30.3 0.0 collective-permute-done.2.refs_1_
  30.3 0.6 copy-done.3
  30.9 1.8 %join.1.refs_0_ = bf16[832,256]{1,0:T(8,128)(2,1)} custom-call(bf16[208,256]{1,0:T(8,128)(2,1)} %spill.1.refs_0_, bf16[208,256]{1,0:T(8,128)(2,1)} %collective-permute-done.2.refs_1_, bf16[208,256]{1,0:T(8,128)(2,1)} %collective-permute-done.3.refs_2_, bf16[208,256]{1,0:T(8,128)(2,1)} %copy-done.3, bf16[2048,256]{1,0:T(8,128)(2,1)} %pack.3.refs_4_), custom_call_target="tpu_custom_call" | custom-call | tf_op jit(solution)/shard_map/join/pallas_call | solution.py:252
  32.7 0.0 copy-start
  32.7 1.3 %collective-permute-start.7 = (bf16[832,256]{1,0:T(8,128)(2,1)}, bf16[832,256]{1,0:T(8,128)(2,1)S(1)}, u32[]{:S(2)}, u32[]{:S(2)}) collective-permute-start(bf16[832,256]{1,0:T(8,128)(2,1)} %join.1.refs_0_), channel_id=1, source_target_pairs={{0,2},{1,3},{2,0},{3,1},{4,6},{5,7},{6,4},{7,5},{8,10},{9,11},{10,... | collective-permute-start | bytes 1277960 | tf_op jit(solution)/shard_map/ppermute | solution.py:435
  33.9 6.6 %all-to-all-start.2 = ((bf16[16,128,256]{2,1,0:T(8,128)(2,1)}), bf16[16,128,256]{2,1,0:T(8,128)(2,1)}, u32[]{:S(2)}, u32[]{:S(2)}) async-start(bf16[16,128,256]{2,1,0:T(8,128)(2,1)} %bitcast.14), calls=%async_computation.2 | async-start | bytes 2097152 | tf_op jit(solution)/shard_map/all_to_all | solution.py:470
  40.5 0.0 copy-done
  40.5 0.4 collective-permute-start.8
  41.0 2.1 %collective-permute-done.7.refs_1_ = bf16[832,256]{1,0:T(8,128)(2,1)S(1)} collective-permute-done((bf16[832,256]{1,0:T(8,128)(2,1)}, bf16[832,256]{1,0:T(8,128)(2,1)S(1)}, u32[]{:S(2)}, u32[]{:S(2)}) %collective-permute-start.7) | collective-permute-done | bytes 426016 | tf_op jit(solution)/shard_map/ppermute | solution.py:435
  43.0 0.0 copy-start.1
  43.0 4.1 %collective-permute-start.9 = (bf16[832,256]{1,0:T(8,128)(2,1)S(1)}, bf16[832,256]{1,0:T(8,128)(2,1)}, u32[]{:S(2)}, u32[]{:S(2)}) collective-permute-start(bf16[832,256]{1,0:T(8,128)(2,1)S(1)} %collective-permute-done.7.refs_1_), channel_id=1, source_target_pairs={{0,1},{1,0},{2,3},{3,2},{4,5},{5,4},{6,7},{7,6},{8,9},{9,8},{10,11... | collective-permute-start | bytes 1277960 | tf_op jit(solution)/shard_map/ppermute | solution.py:435
  47.1 0.0 collective-permute-done.8.refs_2_
  47.1 0.0 copy-done.1
  47.1 0.0 copy-start.2
  47.1 0.8 %copy-done.2 = bf16[832,256]{1,0:T(8,128)(2,1)} copy-done((bf16[832,256]{1,0:T(8,128)(2,1)}, bf16[832,256]{1,0:T(8,128)(2,1)S(1)}, u32[]{:S(2)}) %copy-start.2) | copy-done | bytes 426008
  47.9 0.8 %collective-permute-done.9.refs_3_ = bf16[832,256]{1,0:T(8,128)(2,1)} collective-permute-done((bf16[832,256]{1,0:T(8,128)(2,1)S(1)}, bf16[832,256]{1,0:T(8,128)(2,1)}, u32[]{:S(2)}, u32[]{:S(2)}) %collective-permute-start.9) | collective-permute-done | bytes 426016 | tf_op jit(solution)/shard_map/ppermute | solution.py:435
  48.6 3.3 %list.1 = (s32[80]{0:T(128)S(1)}, s32[33]{0:T(128)S(1)}, s32[1]{0:T(128)}) custom-call(bf16[832,256]{1,0:T(8,128)(2,1)} %join.1.refs_0_, bf16[832,256]{1,0:T(8,128)(2,1)} %copy-done.1, bf16[832,256]{1,0:T(8,128)(2,1)} %copy-done.2, bf16[832,256]{1,0:T(8,128)(2,1)} %collective-permute-done.9.refs_3_), custom_call_target="tpu_custom_call" | custom-call | flops 12000000000 | tf_op jit(solution)/shard_map/list/pallas_call | solution.py:474
  52.5 12.9 %all-to-all-done.2 = bf16[16,128,256]{2,1,0:T(8,128)(2,1)} async-done(((bf16[16,128,256]{2,1,0:T(8,128)(2,1)}), bf16[16,128,256]{2,1,0:T(8,128)(2,1)}, u32[]{:S(2)}, u32[]{:S(2)}) %all-to-all-start.2) | async-done | bytes 1048608 | tf_op jit(solution)/shard_map/all_to_all | solution.py:470
  65.5 3.6 %conditional.1 = (bf16[4,256,512]{2,1,0:T(8,128)(2,1)}) conditional(s32[]{:T(128)} %bitcast.6, (s32[1,4,8]{2,1,0:T(4,128)S(1)}, s32[1,4,8]{2,1,0:T(4,128)S(1)}, bf16[512,256]{1,0:T(8,128)(2,1)S(1)}, bf16[512,256]{1,0:T(8,128)(2,1)S(1)}, bf16[512,256]{1,0:T(8,128)(2,1)}, /*index=5*/bf16[528,256]{1,0:T(8,128)(2,1)S(1)}, bf16[512,256]{1,0:T(8,128)(2,1)}, ...), branch_computations={%region_0.4_spmd, %region_4.5_spmd} | conditional | flops 142111872 | bytes 34633176 | solution.py:513
  65.5 3.6 %land.1 = bf16[4,256,512]{2,1,0:T(8,128)(2,1)} custom-call(s32[80]{0:T(128)S(1)} %get-tuple-element.53.order_ref, s32[33]{0:T(128)S(1)} %get-tuple-element.54.begin_ref, bf16[2048,256]{1,0:T(8,128)(2,1)} %bitcast.2.arrived_ref, bf16[832,256]{1,0:T(8,128)(2,1)} %get-tuple-element.56.refs_0_, bf16[832,256]{1,0:T(8,128)(2,1)} %get-tuple-element.57.refs_1_, ...), custom_call_target="tpu_custom_call" | custom-call | tf_op jit(solution)/shard_map/cond/branch_1_fun/land/pallas_call | solution.py:493
Async XLA Ops:
  0.0 4.9 %copy-start.4 = (s32[1,4,8]{2,1,0:T(4,128)S(1)}, s32[1,4,8]{2,1,0:T(4,128)}, u32[]{:S(2)}) copy-start(s32[1,4,8]{2,1,0:T(4,128)} %refs_0_.1) | copy-start | bytes 388
  0.0 4.9 %copy-start.5 = (s32[1,4,8]{2,1,0:T(4,128)S(1)}, s32[1,4,8]{2,1,0:T(4,128)}, u32[]{:S(2)}) copy-start(s32[1,4,8]{2,1,0:T(4,128)} %refs_1_.1) | copy-start | bytes 388
  3.6 12.1 %collective-permute-start = (bf16[512,256]{1,0:T(8,128)(2,1)}, bf16[512,256]{1,0:T(8,128)(2,1)S(1)}, u32[]{:S(2)}, u32[]{:S(2)}) collective-permute-start(bf16[512,256]{1,0:T(8,128)(2,1)} %get-tuple-element.73.refs_2_), channel_id=1, source_target_pairs={{0,16},{16,0},{1,17},{17,1},{2,18},{18,2},{3,19},{19,3},{4,20},{20... | collective-permute-start | bytes 786440 | tf_op jit(solution)/shard_map/ppermute | solution.py:432
  9.1 7.6 %collective-permute-start.1 = (bf16[528,256]{1,0:T(8,128)(2,1)}, bf16[528,256]{1,0:T(8,128)(2,1)S(1)}, u32[]{:S(2)}, u32[]{:S(2)}) collective-permute-start(bf16[528,256]{1,0:T(8,128)(2,1)} %get-tuple-element.78.refs_0_), channel_id=1, source_target_pairs={{0,16},{16,0},{1,17},{17,1},{2,18},{18,2},{3,19},{19,3},{4,20},{20... | collective-permute-start | bytes 811016 | tf_op jit(solution)/shard_map/ppermute | solution.py:432
  14.2 8.6 %collective-permute-start.6 = (bf16[512,256]{1,0:T(8,128)(2,1)}, bf16[512,256]{1,0:T(8,128)(2,1)}, u32[]{:S(2)}, u32[]{:S(2)}) collective-permute-start(bf16[512,256]{1,0:T(8,128)(2,1)} %get-tuple-element.82), channel_id=1, source_target_pairs={{0,16},{16,0},{1,17},{17,1},{2,18},{18,2},{3,19},{19,3},{4,20},{20... | collective-permute-start | bytes 786440 | tf_op jit(solution)/shard_map/ppermute | solution.py:432
  15.5 12.9 %collective-permute-start.5 = (bf16[512,256]{1,0:T(8,128)(2,1)}, bf16[512,256]{1,0:T(8,128)(2,1)}, u32[]{:S(2)}, u32[]{:S(2)}) collective-permute-start(bf16[512,256]{1,0:T(8,128)(2,1)} %get-tuple-element.79.refs_4_), channel_id=1, source_target_pairs={{0,16},{16,0},{1,17},{17,1},{2,18},{18,2},{3,19},{19,3},{4,20},{20... | collective-permute-start | bytes 786440 | tf_op jit(solution)/shard_map/ppermute | solution.py:432
  18.3 12.0 %collective-permute-start.4 = (bf16[208,256]{1,0:T(8,128)(2,1)}, bf16[208,256]{1,0:T(8,128)(2,1)S(1)}, u32[]{:S(2)}, u32[]{:S(2)}) collective-permute-start(bf16[208,256]{1,0:T(8,128)(2,1)} %spill.1.refs_0_), channel_id=1, source_target_pairs={{0,12},{1,13},{2,14},{3,15},{4,8},{5,9},{6,10},{7,11},{8,4},{9,5},... | collective-permute-start | bytes 319496 | tf_op jit(solution)/shard_map/ppermute | solution.py:435
  20.2 10.0 %collective-permute-start.3 = (bf16[208,256]{1,0:T(8,128)(2,1)}, bf16[208,256]{1,0:T(8,128)(2,1)}, u32[]{:S(2)}, u32[]{:S(2)}) collective-permute-start(bf16[208,256]{1,0:T(8,128)(2,1)} %spill.1.refs_0_), channel_id=1, source_target_pairs={{0,8},{1,9},{2,10},{3,11},{4,12},{5,13},{6,14},{7,15},{8,0},{9,1},... | collective-permute-start | bytes 319496 | tf_op jit(solution)/shard_map/ppermute | solution.py:435
  20.9 9.4 %collective-permute-start.2 = (bf16[208,256]{1,0:T(8,128)(2,1)}, bf16[208,256]{1,0:T(8,128)(2,1)}, u32[]{:S(2)}, u32[]{:S(2)}) collective-permute-start(bf16[208,256]{1,0:T(8,128)(2,1)} %spill.1.refs_0_), channel_id=1, source_target_pairs={{0,4},{1,5},{2,6},{3,7},{4,0},{5,1},{6,2},{7,3},{8,12},{9,13},{10,... | collective-permute-start | bytes 319496 | tf_op jit(solution)/shard_map/ppermute | solution.py:435
  30.3 0.6 copy-start.3
  32.7 7.9 %copy-start = (bf16[832,256]{1,0:T(8,128)(2,1)S(1)}, bf16[832,256]{1,0:T(8,128)(2,1)}, u32[]{:S(2)}) copy-start(bf16[832,256]{1,0:T(8,128)(2,1)} %join.1.refs_0_) | copy-start | bytes 1277956
  32.7 10.3 %collective-permute-start.7 = (bf16[832,256]{1,0:T(8,128)(2,1)}, bf16[832,256]{1,0:T(8,128)(2,1)S(1)}, u32[]{:S(2)}, u32[]{:S(2)}) collective-permute-start(bf16[832,256]{1,0:T(8,128)(2,1)} %join.1.refs_0_), channel_id=1, source_target_pairs={{0,2},{1,3},{2,0},{3,1},{4,6},{5,7},{6,4},{7,5},{8,10},{9,11},{10,... | collective-permute-start | bytes 1277960 | tf_op jit(solution)/shard_map/ppermute | solution.py:435
  33.9 31.5 %all-to-all-start.2 = ((bf16[16,128,256]{2,1,0:T(8,128)(2,1)}), bf16[16,128,256]{2,1,0:T(8,128)(2,1)}, u32[]{:S(2)}, u32[]{:S(2)}) async-start(bf16[16,128,256]{2,1,0:T(8,128)(2,1)} %bitcast.14), calls=%async_computation.2 | async-start | bytes 2097152 | tf_op jit(solution)/shard_map/all_to_all | solution.py:470
  40.5 6.6 %collective-permute-start.8 = (bf16[832,256]{1,0:T(8,128)(2,1)S(1)}, bf16[832,256]{1,0:T(8,128)(2,1)S(1)}, u32[]{:S(2)}, u32[]{:S(2)}) collective-permute-start(bf16[832,256]{1,0:T(8,128)(2,1)S(1)} %copy-done), channel_id=1, source_target_pairs={{0,1},{1,0},{2,3},{3,2},{4,5},{5,4},{6,7},{7,6},{8,9},{9,8},{10,11... | collective-permute-start | bytes 1277960 | tf_op jit(solution)/shard_map/ppermute | solution.py:435
  43.0 4.1 %copy-start.1 = (bf16[832,256]{1,0:T(8,128)(2,1)}, bf16[832,256]{1,0:T(8,128)(2,1)S(1)}, u32[]{:S(2)}) copy-start(bf16[832,256]{1,0:T(8,128)(2,1)S(1)} %collective-permute-done.7.refs_1_) | copy-start | bytes 1277956
  43.0 5.6 %collective-permute-start.9 = (bf16[832,256]{1,0:T(8,128)(2,1)S(1)}, bf16[832,256]{1,0:T(8,128)(2,1)}, u32[]{:S(2)}, u32[]{:S(2)}) collective-permute-start(bf16[832,256]{1,0:T(8,128)(2,1)S(1)} %collective-permute-done.7.refs_1_), channel_id=1, source_target_pairs={{0,1},{1,0},{2,3},{3,2},{4,5},{5,4},{6,7},{7,6},{8,9},{9,8},{10,11... | collective-permute-start | bytes 1277960 | tf_op jit(solution)/shard_map/ppermute | solution.py:435
  47.1 0.8 %copy-start.2 = (bf16[832,256]{1,0:T(8,128)(2,1)}, bf16[832,256]{1,0:T(8,128)(2,1)S(1)}, u32[]{:S(2)}) copy-start(bf16[832,256]{1,0:T(8,128)(2,1)S(1)} %collective-permute-done.8.refs_2_) | copy-start | bytes 1277956

commit v4 on v3

--- a/solution.py
+++ b/solution.py
@@ -13,6 +13,7 @@
 SLOTS = 2
 SPILL = 3
 SPILL_BLOCKS = 2
+CROSS = 8
 INFO = 16
 TABLE = 256
 
@@ -231,30 +232,61 @@
     out_ref[SPILL * rows :, :] = table.astype(jnp.float32).astype(jnp.bfloat16)
 
 
-def join_kernel(count, *refs):
-    out_ref, held, come, go = refs[-4:]
-    rows = refs[0].shape[0]
-    arrive = [pltpu.make_async_copy(ref, held.at[pl.ds(i * rows, rows)], come.at[i]) for i, ref in enumerate(refs[:count])]
+def join_kernel(rows, peers, count, *refs):
+    near_ref, tables_ref, cross_ref, held, values, table, come, go = refs[-8:]
+    me = lax.axis_index("sector").astype(jnp.int32)
+    chunk = refs[0].shape[0]
+    spill_at = peers * SLOTS
+    arrive = [pltpu.make_async_copy(ref, held.at[pl.ds(i * chunk, chunk)], come.at[i]) for i, ref in enumerate(refs[:count])]
     for copy in arrive:
         copy.start()
     leave = []
     for i, copy in enumerate(arrive):
         copy.wait()
-        at = pl.ds(i * rows, rows)
-        leave.append(pltpu.make_async_copy(held.at[at], out_ref.at[at], go.at[i]))
+        at, info = pl.ds(i * chunk, chunk), pl.ds((i + 1) * chunk - INFO, INFO)
+        leave.append(pltpu.make_async_copy(held.at[info], tables_ref.at[pl.ds(i * INFO, INFO)], go.at[count + i]))
+        leave.append(pltpu.make_async_copy(held.at[at], near_ref.at[at], go.at[i]))
+        leave[-2].start()
         leave[-1].start()
+        values[i : i + 1, :] = held[(i + 1) * chunk - INFO : (i + 1) * chunk, :].astype(jnp.float32).astype(jnp.int32)[:1, :]
+    copy = pltpu.make_async_copy(values, table, go.at[2 * count])
+    copy.start()
+    copy.wait()
+    moves = []
+    place = 0
+    for i in range(count):
+        for j in range(SPILL):
+            owner = table[i, spill_at + j]
+            there = (owner >= 0) & (owner // 4 == me // 4) & ((owner ^ me) & 2 == 2)
+            fits = there & (place < CROSS)
+
+            def move(i=i, j=j, place=place):
+                to = pl.ds(pl.multiple_of(place * rows, rows), rows)
+                sem = go.at[2 * count + 1 + i * SPILL + j]
+                return pltpu.make_async_copy(held.at[pl.ds(i * chunk + j * rows, rows)], cross_ref.at[to], sem)
+
+            moves.append((fits, move))
+            place = place + there.astype(jnp.int32)
+    run_copies(moves)
     for copy in leave:
         copy.wait()
 
 
-def join(behind, *parts):
-    rows, width = parts[0].shape
+def join(rows, peers, behind, *parts):
+    chunk, width = parts[0].shape
+    count = len(parts)
     return pl.pallas_call(
-        functools.partial(join_kernel, len(parts)),
-        in_specs=[ANY] * (len(parts) + len(behind)),
-        out_specs=HBM,
-        out_shape=jax.ShapeDtypeStruct((len(parts) * rows, width), jnp.bfloat16),
-        scratch_shapes=[pltpu.VMEM((len(parts) * rows, width), jnp.bfloat16)] + [pltpu.SemaphoreType.DMA((len(parts),))] * 2,
+        functools.partial(join_kernel, rows, peers, count),
+        in_specs=[ANY] * (count + len(behind)),
+        out_specs=[HBM] * 3,
+        out_shape=[jax.ShapeDtypeStruct((n, width), jnp.bfloat16) for n in (count * chunk, count * INFO, CROSS * rows)],
+        scratch_shapes=[
+            pltpu.VMEM((count * chunk, width), jnp.bfloat16),
+            pltpu.VMEM((count, TABLE), jnp.int32),
+            pltpu.SMEM((count, TABLE), jnp.int32),
+            pltpu.SemaphoreType.DMA((count,)),
+            pltpu.SemaphoreType.DMA((2 * count + 1 + count * SPILL,)),
+        ],
         compiler_params=params(63),
         name="join",
     )(*parts, *behind)
@@ -306,7 +338,7 @@
 
 
 def list_kernel(rows, peers, blocks, *refs):
-    sets, (order_ref, begin_ref, more_ref, lines, values, table, codes, count, sems) = refs[:4], refs[4:]
+    sets, (order_ref, begin_ref, where_ref, more_ref, lines, values, table, codes, count, cross, sems) = refs[:4], refs[4:]
     me = lax.axis_index("sector")
     quarter = peers // 4
     chunk = SPILL * rows + INFO
@@ -315,7 +347,7 @@
     for which, ref in enumerate(sets):
         for z in range(quarter):
             i = which * quarter + z
-            copies.append(pltpu.make_async_copy(ref.at[pl.ds((z + 1) * chunk - INFO, INFO)], lines.at[i], sems.at[i]))
+            copies.append(pltpu.make_async_copy(ref.at[pl.ds(z * INFO, INFO)], lines.at[i], sems.at[i]))
             copies[-1].start()
     for i in range(targets + 1):
         count[i] = 0
@@ -341,7 +373,28 @@
             note(slots + j * SPILL + i, jnp.where(owner == me, table[j, slots + SPILL + i], -1))
         return jnp.maximum(more, table[j, TABLE - 1])
 
-    more_ref[0] = lax.fori_loop(0, peers, source, 0, unroll=4)
+    more = lax.fori_loop(0, peers, source, 0, unroll=4)
+
+    for i in range(peers):
+        cross[i] = 0
+
+    def passed(line, place):
+        which, z = line // quarter, line % quarter
+        origin = me ^ (z * 4 + which % 2 * 2 + which // 2)
+        place = jnp.where(z == 0, 0, place)
+        for j in range(SPILL):
+            owner = table[line, slots + j]
+            change = (owner >= 0) & ((owner ^ origin) & 2 == 2)
+            to = jnp.maximum(owner, 0) // 4 * 4 + origin % 4
+            cross[to] += change.astype(jnp.int32)
+            where_ref[line * SPILL + j] = place
+            place = place + (change & (owner // 4 == me // 4)).astype(jnp.int32)
+        return place
+
+    lax.fori_loop(0, peers, passed, 0, unroll=4)
+    for i in range(peers):
+        more = jnp.maximum(more, (cross[i] > CROSS).astype(jnp.int32))
+    more_ref[0] = more
 
     def total(t, before):
         begin_ref[t] = before
@@ -361,7 +414,7 @@
     lax.fori_loop(0, slots + peers * SPILL, put, 0, unroll=peers // 2)
 
 
-def land_kernel(rows, peers, order_ref, begin_ref, arrived_ref, *refs):
+def land_kernel(rows, peers, order_ref, begin_ref, where_ref, arrived_ref, *refs):
     sets, (out_ref, held, stage, sems, out_sems) = refs[:4], refs[4:]
     quarter = peers // 4
     chunk = SPILL * rows + INFO
@@ -389,7 +442,8 @@
 
                 @pl.when(source // quarter == which)
                 def _(which=which):
-                    fetch(i, sets[which], source % quarter * chunk + j * rows).start()
+                    start = where_ref[i - slots] * rows if which % 2 else source % quarter * chunk + j * rows
+                    fetch(i, sets[which], start).start()
 
         return 0
 
@@ -451,7 +505,7 @@
 
     spilled = pl.pallas_call(
         functools.partial(spill_kernel, rows, blocks),
-        in_specs=[SMEM, VMEM] + [ANY] * (2 * SPILL_BLOCKS + 1),
+        in_specs=[SMEM, VMEM] + [HBM] * (2 * SPILL_BLOCKS) + [ANY],
         out_specs=VMEM,
         out_shape=bf16(chunk, width),
         scratch_shapes=[pltpu.VMEM((SPILL * rows, width), jnp.bfloat16)] * 2
@@ -464,35 +518,41 @@
     along = [across(spilled, apart) for apart in range(4, peers, 4)]
     packed = pack(0, sent, own[:last], other[:last], None, rows, peers * SLOTS, [])
     packed = pack(last, sent, own[last:], other[last:], packed, rows, peers * SLOTS, [])
-    near = join([packed], spilled, *along)
-    beside = across(near, 2)
-    sets = [near, beside, across(near, 1), across(beside, 1)]
+    near, tables, crossing = join(rows, peers, [packed], spilled, *along)
+    tables_beside, tables_mate = across(tables, 2), across(tables, 1)
+    tables = [tables, tables_beside, tables_mate, across(tables_beside, 1)]
+    beside = across(crossing, 2)
     arrived = lax.all_to_all(packed.reshape(peers, SLOTS * rows, width), "sector", split_axis=0, concat_axis=0, tiled=True)
     arrived = arrived.reshape(peers * SLOTS * rows, width)
 
     pieces = peers * (SLOTS + SPILL)
-    order, begin, more = pl.pallas_call(
+    order, begin, where, more = pl.pallas_call(
         functools.partial(list_kernel, rows, peers, blocks),
-        in_specs=[ANY] * 4,
-        out_specs=[SMEM] * 3,
-        out_shape=[int32(pieces), int32(blocks * PIECES + 1), int32(1)],
+        in_specs=[HBM] * 4,
+        out_specs=[SMEM] * 4,
+        out_shape=[int32(pieces), int32(blocks * PIECES + 1), int32(peers * SPILL), int32(1)],
         scratch_shapes=[
             pltpu.VMEM((peers, INFO, TABLE), jnp.bfloat16),
             pltpu.VMEM((peers, TABLE), jnp.int32),
             pltpu.SMEM((peers, TABLE), jnp.int32),
             pltpu.SMEM((pieces,), jnp.int32),
             pltpu.SMEM((blocks * PIECES + 1,), jnp.int32),
+            pltpu.SMEM((peers,), jnp.int32),
             pltpu.SemaphoreType.DMA((peers + 1,)),
         ],
         compiler_params=params(63),
-        cost_estimate=pl.CostEstimate(flops=12000000000, bytes_accessed=0, transcendentals=0),
+        cost_estimate=pl.CostEstimate(flops=17000000000, bytes_accessed=0, transcendentals=0),
         name="list",
-    )(*sets)
-
-    def fast(order, begin, arrived, sets, *_):
+    )(*tables)
+
+    more = jnp.maximum(more, swap(more))
+    beside, begin, more = lax.optimization_barrier((beside, begin, more))
+    sets = [near, beside, across(near, 1), across(beside, 1)]
+
+    def fast(order, begin, where, arrived, sets, *_):
         return pl.pallas_call(
             functools.partial(land_kernel, rows, peers),
-            in_specs=[SMEM, SMEM] + [ANY] * 5,
+            in_specs=[SMEM] * 3 + [ANY] * 5,
             out_specs=HBM,
             out_shape=bf16(blocks, share, states),
             scratch_shapes=[
@@ -503,14 +563,14 @@
             ],
             compiler_params=params(63),
             name="land",
-        )(order, begin, arrived, *sets)
-
-    def slow(order, begin, arrived, sets, own, other):
+        )(order, begin, where, arrived, *sets)
+
+    def slow(order, begin, where, arrived, sets, own, other):
         sums = jnp.concatenate([add(a, b[: a.shape[0]]) for a, b in zip(own, other)], axis=0)
         sums = sums.reshape(blocks, ROW_GROUPS, COL_PARTS, rows, width).transpose(1, 3, 0, 2, 4)
         return exchange_all(sums.reshape(share, blocks, states), route_owner, route_block)
 
-    return lax.cond(more[0] <= 0, fast, slow, order, begin, arrived, tuple(sets), tuple(own), tuple(other))
+    return lax.cond(more[0] <= 0, fast, slow, order, begin, where, arrived, tuple(sets), tuple(own), tuple(other))
 
 
 def solution(mesh):

time: 69.7 us -> 66.8 us (0.958)
  waiting for transfers between devices: 21.2 us -> 14.8 us
  Pallas kernels: 26.8 us -> 28.2 us
  starting transfers between devices: 18.9 us -> 20.1 us
  between operations: 0.68 us -> 1.38 us
    all_to_all x1, waiting for transfers between devices: 12.9 us -> 2.02 us  [two_halves(): lax.all_to_all(packed.reshape(peers, SLOTS * rows, width), 'sector', spli...]
    ppermute x6 -> x9, waiting for transfers between devices: 2.84 us -> 5.68 us  [across(): return lax.ppermute(x, 'sector', [(i, i ^ apart) for i in range(peers)])]
    ppermute x4 -> x5, waiting for transfers between devices: 5.42 us -> 7.14 us  [swap(): return lax.ppermute(x, 'mpo', [(0, 1), (1, 0)])]
    pallas_call x1, Pallas kernels: 3.33 us -> 4.26 us  [two_halves(): pl.pallas_call(functools.partial(list_kernel, rows, peers, blocks), in_sp...]
    ppermute x4 -> x5, starting transfers between devices: 3.13 us -> 3.79 us  [swap(): return lax.ppermute(x, 'mpo', [(0, 1), (1, 0)])]
    ppermute x6 -> x9, starting transfers between devices: 9.23 us -> 9.06 us  [across(): return lax.ppermute(x, 'sector', [(i, i ^ apart) for i in range(peers)])]
  transfers between devices with their start and end apart: 11 -> 15, of which waited for: 6 -> 9; matrix products, arithmetic and copies ran while one was open for 0% -> 0% of each run, Pallas kernels for 26% -> 32%
where the time goes in v4:
time: 66.8 us; the launch traced here: 66.2 us
  Pallas kernels  28.2 us (42%)
  starting transfers between devices  20.1 us (30%)
  waiting for transfers between devices  14.8 us (22%)
  local copies, waits for them, and re-layouts  1.62 us (2%)
  between operations  1.38 us (2%)
    pallas_call x3, Pallas kernels, terms(): pl.pallas_call(functools.partial(term_kernel, first, (peers, blocks, grou...  12.5 us
    ppermute x9, starting transfers between devices, across(): return lax.ppermute(x, 'sector', [(i, i ^ apart) for i in range(peers)])  9.06 us
    all_to_all x1, starting transfers between devices, two_halves(): lax.all_to_all(packed.reshape(peers, SLOTS * rows, width), 'sector', spli...  7.27 us
    ppermute x5, waiting for transfers between devices, swap(): return lax.ppermute(x, 'mpo', [(0, 1), (1, 0)])  7.14 us
    ppermute x9, waiting for transfers between devices, across(): return lax.ppermute(x, 'sector', [(i, i ^ apart) for i in range(peers)])  5.68 us
    pallas_call x1, Pallas kernels, two_halves(): pl.pallas_call(functools.partial(list_kernel, rows, peers, blocks), in_sp...  4.26 us
    pallas_call x2, Pallas kernels, pack(): pl.pallas_call(functools.partial(pack_kernel, first, rows, pairs), in_spe...  3.98 us
    ppermute x5, starting transfers between devices, swap(): return lax.ppermute(x, 'mpo', [(0, 1), (1, 0)])  3.79 us
  transfers between devices with their start and end apart: 15, of which 9 were waited for; matrix products, arithmetic and copies ran while one was open for 0% of the time, Pallas kernels for 32%

profile of v4, /device:TPU:9, one launch (start us, length us, event | category | flops | bytes accessed | tf_op | source)
XLA Modules:
  0.0 66.2 jit_solution(5992699249009495148)
XLA Ops:
  0.0 0.0 copy-start.1
  0.0 3.6 %terms.3 = (bf16[512,256]{1,0:T(8,128)(2,1)S(1)}, bf16[512,256]{1,0:T(8,128)(2,1)}) custom-call(s32[4]{0:T(128)} %size_ref.5, s32[1,4]{1,0:T(1,128)} %mask_ref.5, bf16[4,512,512]{2,1,0:T(8,128)(2,1)} %wave_ref.5, bf16[4,512,512]{2,1,0:T(8,128)(2,1)} %bitcast.18, bf16[4,512,512]{2,1,0:T(8,128)(2,1)} %bitcast.21), custom_call_target="tpu_custom_call" | custom-call | flops 3000000000 | bytes 1 | tf_op jit(solution)/shard_map/terms/pallas_call | solution.py:181
  3.6 1.3 %collective-permute-start = (bf16[512,256]{1,0:T(8,128)(2,1)}, bf16[512,256]{1,0:T(8,128)(2,1)S(1)}, u32[]{:S(2)}, u32[]{:S(2)}) collective-permute-start(bf16[512,256]{1,0:T(8,128)(2,1)} %get-tuple-element.83.refs_2_), channel_id=1, source_target_pairs={{0,16},{16,0},{1,17},{17,1},{2,18},{18,2},{3,19},{19,3},{4,20},{20... | collective-permute-start | bytes 786440 | tf_op jit(solution)/shard_map/ppermute | solution.py:486
  4.9 0.0 copy-done.1
  4.9 0.0 copy-done.2
  4.9 4.2 %terms.4 = (bf16[512,256]{1,0:T(8,128)(2,1)}, bf16[528,256]{1,0:T(8,128)(2,1)}, s32[256]{0:T(256)}, s32[256]{0:T(256)}) custom-call(s32[4]{0:T(128)} %size_ref.5, s32[1,4]{1,0:T(1,128)} %mask_ref.5, bf16[4,512,512]{2,1,0:T(8,128)(2,1)} %wave_ref.5, bf16[4,512,512]{2,1,0:T(8,128)(2,1)} %bitcast.19, bf16[4,512,512]{2,1,0:T(8,128)(2,1)} %bitcast.22, ...), custom_call_target="tpu_custom_call" | custom-call | flops 3000000000 | bytes 1 | tf_op jit(solution)/shard_map/terms/pallas_call | solution.py:181
  9.1 0.3 collective-permute-start.1
  9.4 4.8 %terms.5 = (bf16[512,256]{1,0:T(8,128)(2,1)}, bf16[512,256]{1,0:T(8,128)(2,1)}, bf16[512,256]{1,0:T(8,128)(2,1)}, bf16[512,256]{1,0:T(8,128)(2,1)}) custom-call(s32[4]{0:T(128)} %size_ref.5, s32[1,4]{1,0:T(1,128)} %mask_ref.5, bf16[4,512,512]{2,1,0:T(8,128)(2,1)} %wave_ref.5, bf16[4,512,512]{2,1,0:T(8,128)(2,1)} %bitcast.20, bf16[4,512,512]{2,1,0:T(8,128)(2,1)} %bitcast.23, ...), custom_call_target="tpu_custom_call" | custom-call | flops 3000000000 | bytes 1 | tf_op jit(solution)/shard_map/terms/pallas_call | solution.py:181
  14.2 1.3 %collective-permute-start.6 = (bf16[512,256]{1,0:T(8,128)(2,1)}, bf16[512,256]{1,0:T(8,128)(2,1)}, u32[]{:S(2)}, u32[]{:S(2)}) collective-permute-start(bf16[512,256]{1,0:T(8,128)(2,1)} %get-tuple-element.92), channel_id=1, source_target_pairs={{0,16},{16,0},{1,17},{17,1},{2,18},{18,2},{3,19},{19,3},{4,20},{20... | collective-permute-start | bytes 786440 | tf_op jit(solution)/shard_map/ppermute | solution.py:486
  15.4 0.3 collective-permute-start.5
  15.7 0.0 collective-permute-done.refs_2_.refs_3_
  15.7 1.0 %collective-permute-done.1.refs_3_.refs_4_ = bf16[528,256]{1,0:T(8,128)(2,1)S(1)} collective-permute-done((bf16[528,256]{1,0:T(8,128)(2,1)}, bf16[528,256]{1,0:T(8,128)(2,1)S(1)}, u32[]{:S(2)}, u32[]{:S(2)}) %collective-permute-start.1) | collective-permute-done | bytes 270368 | tf_op jit(solution)/shard_map/ppermute | solution.py:486
  16.7 1.7 %spill.1.refs_0_ = bf16[208,256]{1,0:T(8,128)(2,1)} custom-call(s32[256]{0:T(256)} %get-tuple-element.84.sent_ref, s32[1,256]{1,0:T(1,128)} %bitcast.17, bf16[512,256]{1,0:T(8,128)(2,1)S(1)} %get-tuple-element.86.refs_0_, bf16[512,256]{1,0:T(8,128)(2,1)} %get-tuple-element.87.refs_1_, bf16[512,256]{1,0:T(8,128)(2,1)S(1)} %collective-permute-done.refs_2_.refs_3_, ...), custom_call_target="tpu_custom_call" | custom-call | tf_op jit(solution)/shard_map/spill/pallas_call | solution.py:506
  18.3 1.2 %collective-permute-start.4 = (bf16[208,256]{1,0:T(8,128)(2,1)}, bf16[208,256]{1,0:T(8,128)(2,1)S(1)}, u32[]{:S(2)}, u32[]{:S(2)}) collective-permute-start(bf16[208,256]{1,0:T(8,128)(2,1)} %spill.1.refs_0_), channel_id=1, source_target_pairs={{0,12},{1,13},{2,14},{3,15},{4,8},{5,9},{6,10},{7,11},{8,4},{9,5},... | collective-permute-start | bytes 319496 | tf_op jit(solution)/shard_map/ppermute | solution.py:489
  19.5 1.8 %collective-permute-start.3 = (bf16[208,256]{1,0:T(8,128)(2,1)}, bf16[208,256]{1,0:T(8,128)(2,1)}, u32[]{:S(2)}, u32[]{:S(2)}) collective-permute-start(bf16[208,256]{1,0:T(8,128)(2,1)} %spill.1.refs_0_), channel_id=1, source_target_pairs={{0,8},{1,9},{2,10},{3,11},{4,12},{5,13},{6,14},{7,15},{8,0},{9,1},... | collective-permute-start | bytes 319496 | tf_op jit(solution)/shard_map/ppermute | solution.py:489
  21.3 1.1 %collective-permute-start.2 = (bf16[208,256]{1,0:T(8,128)(2,1)}, bf16[208,256]{1,0:T(8,128)(2,1)}, u32[]{:S(2)}, u32[]{:S(2)}) collective-permute-start(bf16[208,256]{1,0:T(8,128)(2,1)} %spill.1.refs_0_), channel_id=1, source_target_pairs={{0,4},{1,5},{2,6},{3,7},{4,0},{5,1},{6,2},{7,3},{8,12},{9,13},{10,... | collective-permute-start | bytes 319496 | tf_op jit(solution)/shard_map/ppermute | solution.py:489
  22.4 0.3 collective-permute-done.6.refs_5_
  22.8 2.2 %pack.2.refs_2_ = bf16[2048,256]{1,0:T(8,128)(2,1)} custom-call(s32[256]{0:T(256)} %get-tuple-element.84.sent_ref, bf16[512,256]{1,0:T(8,128)(2,1)S(1)} %get-tuple-element.86.refs_0_, bf16[512,256]{1,0:T(8,128)(2,1)} %get-tuple-element.87.refs_1_, bf16[512,256]{1,0:T(8,128)(2,1)} %get-tuple-element.91.refs_2_, ...), custom_call_target="tpu_custom_call" | custom-call | tf_op jit(solution)/shard_map/pack/pallas_call | solution.py:328
  25.0 3.4 %collective-permute-done.5.refs_1_ = bf16[512,256]{1,0:T(8,128)(2,1)} collective-permute-done((bf16[512,256]{1,0:T(8,128)(2,1)}, bf16[512,256]{1,0:T(8,128)(2,1)}, u32[]{:S(2)}, u32[]{:S(2)}) %collective-permute-start.5) | collective-permute-done | bytes 262176 | tf_op jit(solution)/shard_map/ppermute | solution.py:486
  28.4 1.8 %pack.3.refs_4_ = bf16[2048,256]{1,0:T(8,128)(2,1)} custom-call(s32[256]{0:T(256)} %get-tuple-element.84.sent_ref, bf16[512,256]{1,0:T(8,128)(2,1)} %get-tuple-element.90.refs_0_, bf16[512,256]{1,0:T(8,128)(2,1)} %collective-permute-done.5.refs_1_, bf16[2048,256]{1,0:T(8,128)(2,1)} %pack.2.refs_2_), custom_call_target="tpu_custom_call", output_to_operand_aliasing={{}: (3, {})} | custom-call | tf_op jit(solution)/shard_map/pack/pallas_call | solution.py:328
  30.2 7.3 %all-to-all-start.2 = ((bf16[16,128,256]{2,1,0:T(8,128)(2,1)}), bf16[16,128,256]{2,1,0:T(8,128)(2,1)}, u32[]{:S(2)}, u32[]{:S(2)}) async-start(bf16[16,128,256]{2,1,0:T(8,128)(2,1)} %bitcast.14), calls=%async_computation.2 | async-start | bytes 2097152 | tf_op jit(solution)/shard_map/all_to_all | solution.py:525
  37.5 0.0 collective-permute-done.4.refs_3_
  37.5 0.0 copy-start
  37.5 0.0 collective-permute-done.3.refs_2_
  37.5 0.0 collective-permute-done.2.refs_1_
  37.5 0.6 copy-done
  38.1 2.0 %join.1 = (bf16[832,256]{1,0:T(8,128)(2,1)}, bf16[64,256]{1,0:T(8,128)(2,1)}, bf16[512,256]{1,0:T(8,128)(2,1)}) custom-call(bf16[208,256]{1,0:T(8,128)(2,1)} %spill.1.refs_0_, bf16[208,256]{1,0:T(8,128)(2,1)} %collective-permute-done.2.refs_1_, bf16[208,256]{1,0:T(8,128)(2,1)} %collective-permute-done.3.refs_2_, bf16[208,256]{1,0:T(8,128)(2,1)} %copy-done, ...), custom_call_target="tpu_custom_call" | custom-call | tf_op jit(solution)/shard_map/join/pallas_call | solution.py:278
  40.2 1.2 %collective-permute-start.8 = (bf16[64,256]{1,0:T(8,128)(2,1)}, bf16[64,256]{1,0:T(8,128)(2,1)S(1)}, u32[]{:S(2)}, u32[]{:S(2)}) collective-permute-start(bf16[64,256]{1,0:T(8,128)(2,1)} %get-tuple-element.94.refs_0_), channel_id=1, source_target_pairs={{0,2},{1,3},{2,0},{3,1},{4,6},{5,7},{6,4},{7,5},{8,10},{9,11},{10,... | collective-permute-start | bytes 98312 | tf_op jit(solution)/shard_map/ppermute | solution.py:489
  41.4 0.6 collective-permute-start.9
  42.1 1.5 %collective-permute-done.8.refs_1_ = bf16[64,256]{1,0:T(8,128)(2,1)S(1)} collective-permute-done((bf16[64,256]{1,0:T(8,128)(2,1)}, bf16[64,256]{1,0:T(8,128)(2,1)S(1)}, u32[]{:S(2)}, u32[]{:S(2)}) %collective-permute-start.8) | collective-permute-done | bytes 32800 | tf_op jit(solution)/shard_map/ppermute | solution.py:489
  43.6 2.0 %collective-permute-start.10 = (bf16[64,256]{1,0:T(8,128)(2,1)S(1)}, bf16[64,256]{1,0:T(8,128)(2,1)S(1)}, u32[]{:S(2)}, u32[]{:S(2)}) collective-permute-start(bf16[64,256]{1,0:T(8,128)(2,1)S(1)} %collective-permute-done.8.refs_1_), channel_id=1, source_target_pairs={{0,1},{1,0},{2,3},{3,2},{4,5},{5,4},{6,7},{7,6},{8,9},{9,8},{10,11... | collective-permute-start | bytes 98312 | tf_op jit(solution)/shard_map/ppermute | solution.py:489
  45.5 0.4 collective-permute-start.7
  45.9 0.3 collective-permute-start.12
  46.2 0.0 collective-permute-done.9.refs_2_
  46.2 0.2 collective-permute-done.10.refs_3_
  46.4 0.0 copy-done.3
  46.4 0.4 copy-done.4
  46.8 0.6 copy-done.5
  47.4 4.3 %list.1 = (s32[80]{0:T(128)S(1)}, s32[33]{0:T(128)S(1)}, s32[48]{0:T(128)S(1)}, s32[1]{0:T(128)}) custom-call(bf16[64,256]{1,0:T(8,128)(2,1)} %get-tuple-element.94.refs_0_, bf16[64,256]{1,0:T(8,128)(2,1)} %copy-done.3, bf16[64,256]{1,0:T(8,128)(2,1)} %copy-done.4, bf16[64,256]{1,0:T(8,128)(2,1)} %copy-done.5), custom_call_target="tpu_custom_call" | custom-call | flops 16999999488 | tf_op jit(solution)/shard_map/list/pallas_call | solution.py:529
  51.7 0.7 %collective-permute-start.11 = (s32[1]{0:T(128)}, s32[1]{0:T(128)}, u32[]{:S(2)}, u32[]{:S(2)}) collective-permute-start(s32[1]{0:T(128)} %get-tuple-element.96), channel_id=1, source_target_pairs={{0,16},{16,0},{1,17},{17,1},{2,18},{18,2},{3,19},{19,3},{4,20},{20... | collective-permute-start | bytes 20 | tf_op jit(solution)/shard_map/ppermute | solution.py:486
  52.3 2.4 %collective-permute-done.11 = s32[1]{0:T(128)} collective-permute-done((s32[1]{0:T(128)}, s32[1]{0:T(128)}, u32[]{:S(2)}, u32[]{:S(2)}) %collective-permute-start.11) | collective-permute-done | bytes 36 | tf_op jit(solution)/shard_map/ppermute | solution.py:486
  56.0 2.5 %collective-permute-done.7 = bf16[512,256]{1,0:T(8,128)(2,1)} collective-permute-done((bf16[512,256]{1,0:T(8,128)(2,1)}, bf16[512,256]{1,0:T(8,128)(2,1)}, u32[]{:S(2)}, u32[]{:S(2)}) %collective-permute-start.7) | collective-permute-done | bytes 262176 | tf_op jit(solution)/shard_map/ppermute | solution.py:489
  58.5 0.4 collective-permute-start.13
  58.9 0.0 collective-permute-done.12
  58.9 1.5 %collective-permute-done.13 = bf16[512,256]{1,0:T(8,128)(2,1)} collective-permute-done((bf16[512,256]{1,0:T(8,128)(2,1)}, bf16[512,256]{1,0:T(8,128)(2,1)}, u32[]{:S(2)}, u32[]{:S(2)}) %collective-permute-start.13) | collective-permute-done | bytes 262176 | tf_op jit(solution)/shard_map/ppermute | solution.py:489
  60.4 2.0 %all-to-all-done.2 = bf16[16,128,256]{2,1,0:T(8,128)(2,1)} async-done(((bf16[16,128,256]{2,1,0:T(8,128)(2,1)}), bf16[16,128,256]{2,1,0:T(8,128)(2,1)}, u32[]{:S(2)}, u32[]{:S(2)}) %all-to-all-start.2) | async-done | bytes 1048608 | tf_op jit(solution)/shard_map/all_to_all | solution.py:525
  62.4 3.7 %conditional.1 = (bf16[4,256,512]{2,1,0:T(8,128)(2,1)}) conditional(s32[]{:T(128)} %bitcast.6, (s32[1,4,8]{2,1,0:T(4,128)S(1)}, s32[1,4,8]{2,1,0:T(4,128)S(1)}, bf16[512,256]{1,0:T(8,128)(2,1)S(1)}, bf16[512,256]{1,0:T(8,128)(2,1)S(1)}, bf16[512,256]{1,0:T(8,128)(2,1)}, /*index=5*/bf16[528,256]{1,0:T(8,128)(2,1)S(1)}, bf16[512,256]{1,0:T(8,128)(2,1)}, ...), branch_computations={%region_0.4_spmd, %region_4.5_spmd} | conditional | flops 142111872 | bytes 34633176 | solution.py:573
  62.4 3.7 %land.1 = bf16[4,256,512]{2,1,0:T(8,128)(2,1)} custom-call(s32[80]{0:T(128)S(1)} %get-tuple-element.55.order_ref, s32[33]{0:T(128)S(1)} %get-tuple-element.56.begin_ref, s32[48]{0:T(128)S(1)} %get-tuple-element.57.where_ref, bf16[2048,256]{1,0:T(8,128)(2,1)} %bitcast.2.arrived_ref, bf16[832,256]{1,0:T(8,128)(2,1)} %get-tuple-element.59.refs_0_, ...), custom_call_target="tpu_custom_call" | custom-call | tf_op jit(solution)/shard_map/cond/branch_1_fun/land/pallas_call | solution.py:553
  (4 shorter events, 0.0 us)
Async XLA Ops:
  0.0 4.9 %copy-start.1 = (s32[1,4,8]{2,1,0:T(4,128)S(1)}, s32[1,4,8]{2,1,0:T(4,128)}, u32[]{:S(2)}) copy-start(s32[1,4,8]{2,1,0:T(4,128)} %refs_0_.1) | copy-start | bytes 388
  0.0 4.9 %copy-start.2 = (s32[1,4,8]{2,1,0:T(4,128)S(1)}, s32[1,4,8]{2,1,0:T(4,128)}, u32[]{:S(2)}) copy-start(s32[1,4,8]{2,1,0:T(4,128)} %refs_1_.1) | copy-start | bytes 388
  3.6 12.1 %collective-permute-start = (bf16[512,256]{1,0:T(8,128)(2,1)}, bf16[512,256]{1,0:T(8,128)(2,1)S(1)}, u32[]{:S(2)}, u32[]{:S(2)}) collective-permute-start(bf16[512,256]{1,0:T(8,128)(2,1)} %get-tuple-element.83.refs_2_), channel_id=1, source_target_pairs={{0,16},{16,0},{1,17},{17,1},{2,18},{18,2},{3,19},{19,3},{4,20},{20... | collective-permute-start | bytes 786440 | tf_op jit(solution)/shard_map/ppermute | solution.py:486
  9.1 7.6 %collective-permute-start.1 = (bf16[528,256]{1,0:T(8,128)(2,1)}, bf16[528,256]{1,0:T(8,128)(2,1)S(1)}, u32[]{:S(2)}, u32[]{:S(2)}) collective-permute-start(bf16[528,256]{1,0:T(8,128)(2,1)} %get-tuple-element.88.refs_0_), channel_id=1, source_target_pairs={{0,16},{16,0},{1,17},{17,1},{2,18},{18,2},{3,19},{19,3},{4,20},{20... | collective-permute-start | bytes 811016 | tf_op jit(solution)/shard_map/ppermute | solution.py:486
  14.2 8.6 %collective-permute-start.6 = (bf16[512,256]{1,0:T(8,128)(2,1)}, bf16[512,256]{1,0:T(8,128)(2,1)}, u32[]{:S(2)}, u32[]{:S(2)}) collective-permute-start(bf16[512,256]{1,0:T(8,128)(2,1)} %get-tuple-element.92), channel_id=1, source_target_pairs={{0,16},{16,0},{1,17},{17,1},{2,18},{18,2},{3,19},{19,3},{4,20},{20... | collective-permute-start | bytes 786440 | tf_op jit(solution)/shard_map/ppermute | solution.py:486
  15.4 13.0 %collective-permute-start.5 = (bf16[512,256]{1,0:T(8,128)(2,1)}, bf16[512,256]{1,0:T(8,128)(2,1)}, u32[]{:S(2)}, u32[]{:S(2)}) collective-permute-start(bf16[512,256]{1,0:T(8,128)(2,1)} %get-tuple-element.89.refs_4_), channel_id=1, source_target_pairs={{0,16},{16,0},{1,17},{17,1},{2,18},{18,2},{3,19},{19,3},{4,20},{20... | collective-permute-start | bytes 786440 | tf_op jit(solution)/shard_map/ppermute | solution.py:486
  18.3 19.1 %collective-permute-start.4 = (bf16[208,256]{1,0:T(8,128)(2,1)}, bf16[208,256]{1,0:T(8,128)(2,1)S(1)}, u32[]{:S(2)}, u32[]{:S(2)}) collective-permute-start(bf16[208,256]{1,0:T(8,128)(2,1)} %spill.1.refs_0_), channel_id=1, source_target_pairs={{0,12},{1,13},{2,14},{3,15},{4,8},{5,9},{6,10},{7,11},{8,4},{9,5},... | collective-permute-start | bytes 319496 | tf_op jit(solution)/shard_map/ppermute | solution.py:489
  19.5 18.0 %collective-permute-start.3 = (bf16[208,256]{1,0:T(8,128)(2,1)}, bf16[208,256]{1,0:T(8,128)(2,1)}, u32[]{:S(2)}, u32[]{:S(2)}) collective-permute-start(bf16[208,256]{1,0:T(8,128)(2,1)} %spill.1.refs_0_), channel_id=1, source_target_pairs={{0,8},{1,9},{2,10},{3,11},{4,12},{5,13},{6,14},{7,15},{8,0},{9,1},... | collective-permute-start | bytes 319496 | tf_op jit(solution)/shard_map/ppermute | solution.py:489
  21.3 16.2 %collective-permute-start.2 = (bf16[208,256]{1,0:T(8,128)(2,1)}, bf16[208,256]{1,0:T(8,128)(2,1)}, u32[]{:S(2)}, u32[]{:S(2)}) collective-permute-start(bf16[208,256]{1,0:T(8,128)(2,1)} %spill.1.refs_0_), channel_id=1, source_target_pairs={{0,4},{1,5},{2,6},{3,7},{4,0},{5,1},{6,2},{7,3},{8,12},{9,13},{10,... | collective-permute-start | bytes 319496 | tf_op jit(solution)/shard_map/ppermute | solution.py:489
  30.2 32.2 %all-to-all-start.2 = ((bf16[16,128,256]{2,1,0:T(8,128)(2,1)}), bf16[16,128,256]{2,1,0:T(8,128)(2,1)}, u32[]{:S(2)}, u32[]{:S(2)}) async-start(bf16[16,128,256]{2,1,0:T(8,128)(2,1)} %bitcast.14), calls=%async_computation.2 | async-start | bytes 2097152 | tf_op jit(solution)/shard_map/all_to_all | solution.py:525
  37.5 0.6 copy-start
  40.2 3.4 %collective-permute-start.8 = (bf16[64,256]{1,0:T(8,128)(2,1)}, bf16[64,256]{1,0:T(8,128)(2,1)S(1)}, u32[]{:S(2)}, u32[]{:S(2)}) collective-permute-start(bf16[64,256]{1,0:T(8,128)(2,1)} %get-tuple-element.94.refs_0_), channel_id=1, source_target_pairs={{0,2},{1,3},{2,0},{3,1},{4,6},{5,7},{6,4},{7,5},{8,10},{9,11},{10,... | collective-permute-start | bytes 98312 | tf_op jit(solution)/shard_map/ppermute | solution.py:489
  41.4 4.8 %collective-permute-start.9 = (bf16[64,256]{1,0:T(8,128)(2,1)}, bf16[64,256]{1,0:T(8,128)(2,1)S(1)}, u32[]{:S(2)}, u32[]{:S(2)}) collective-permute-start(bf16[64,256]{1,0:T(8,128)(2,1)} %get-tuple-element.94.refs_0_), channel_id=1, source_target_pairs={{0,1},{1,0},{2,3},{3,2},{4,5},{5,4},{6,7},{7,6},{8,9},{9,8},{10,11... | collective-permute-start | bytes 98312 | tf_op jit(solution)/shard_map/ppermute | solution.py:489
  43.5 2.8 %copy-start.3 = (bf16[64,256]{1,0:T(8,128)(2,1)}, bf16[64,256]{1,0:T(8,128)(2,1)S(1)}, u32[]{:S(2)}) copy-start(bf16[64,256]{1,0:T(8,128)(2,1)S(1)} %collective-permute-done.8.refs_1_) | copy-start | bytes 98308
  43.6 2.8 %collective-permute-start.10 = (bf16[64,256]{1,0:T(8,128)(2,1)S(1)}, bf16[64,256]{1,0:T(8,128)(2,1)S(1)}, u32[]{:S(2)}, u32[]{:S(2)}) collective-permute-start(bf16[64,256]{1,0:T(8,128)(2,1)S(1)} %collective-permute-done.8.refs_1_), channel_id=1, source_target_pairs={{0,1},{1,0},{2,3},{3,2},{4,5},{5,4},{6,7},{7,6},{8,9},{9,8},{10,11... | collective-permute-start | bytes 98312 | tf_op jit(solution)/shard_map/ppermute | solution.py:489
  45.5 12.9 %collective-permute-start.7 = (bf16[512,256]{1,0:T(8,128)(2,1)}, bf16[512,256]{1,0:T(8,128)(2,1)}, u32[]{:S(2)}, u32[]{:S(2)}) collective-permute-start(bf16[512,256]{1,0:T(8,128)(2,1)} %get-tuple-element.93), channel_id=1, source_target_pairs={{0,2},{1,3},{2,0},{3,1},{4,6},{5,7},{6,4},{7,5},{8,10},{9,11},{10,... | collective-permute-start | bytes 786440 | tf_op jit(solution)/shard_map/ppermute | solution.py:489
  45.9 13.0 %collective-permute-start.12 = (bf16[832,256]{1,0:T(8,128)(2,1)}, bf16[832,256]{1,0:T(8,128)(2,1)}, u32[]{:S(2)}, u32[]{:S(2)}) collective-permute-start(bf16[832,256]{1,0:T(8,128)(2,1)} %get-tuple-element.101), channel_id=1, source_target_pairs={{0,1},{1,0},{2,3},{3,2},{4,5},{5,4},{6,7},{7,6},{8,9},{9,8},{10,11... | collective-permute-start | bytes 1277960 | tf_op jit(solution)/shard_map/ppermute | solution.py:489
  46.2 0.6 copy-start.4
  46.8 0.6 copy-start.5
  51.7 3.1 %collective-permute-start.11 = (s32[1]{0:T(128)}, s32[1]{0:T(128)}, u32[]{:S(2)}, u32[]{:S(2)}) collective-permute-start(s32[1]{0:T(128)} %get-tuple-element.96), channel_id=1, source_target_pairs={{0,16},{16,0},{1,17},{17,1},{2,18},{18,2},{3,19},{19,3},{4,20},{20... | collective-permute-start | bytes 20 | tf_op jit(solution)/shard_map/ppermute | solution.py:486
  58.5 1.9 %collective-permute-start.13 = (bf16[512,256]{1,0:T(8,128)(2,1)}, bf16[512,256]{1,0:T(8,128)(2,1)}, u32[]{:S(2)}, u32[]{:S(2)}) collective-permute-start(bf16[512,256]{1,0:T(8,128)(2,1)} %collective-permute-done.7), channel_id=1, source_target_pairs={{0,1},{1,0},{2,3},{3,2},{4,5},{5,4},{6,7},{7,6},{8,9},{9,8},{10,11... | collective-permute-start | bytes 786440 | tf_op jit(solution)/shard_map/ppermute | solution.py:489
